TPU v7x, 32 devices: a whole 2x2x4 slice. The times are simulated.
32 devices in a mesh: shard: 4 (over z), ctx: 4 (over y, x), tp: 2 (over core).
Axes of the slice: x: 2, y: 2, z: 4, core: 2. Of those that a mesh axis runs over, the one named last changes fastest.
Arguments:
- tokens: bfloat16 [4, 2048, 1536], P('shard', 'ctx'), may hold values from -6 to 6
- cotangent: bfloat16 [4, 2048, 1536], P('shard', 'ctx'), may hold values from -6 to 6
- norm1_gain: bfloat16 [1536], replicated, may hold values from 0.5 to 1.5
- w_query: bfloat16 [1536, 1536], P('shard', 'tp'), may hold values from -0.15625 to 0.15625
- b_query: bfloat16 [1536], P('tp'), may hold values from -4 to 4
- w_key: bfloat16 [1536, 256], P('shard', 'tp'), may hold values from -0.15625 to 0.15625
- b_key: bfloat16 [256], P('tp'), may hold values from -4 to 4
- w_value: bfloat16 [1536, 256], P('shard', 'tp'), may hold values from -0.15625 to 0.15625
- b_value: bfloat16 [256], P('tp'), may hold values from -4 to 4
- w_out: bfloat16 [1536, 1536], P('shard', 'tp'), may hold values from -0.5 to 0.5
- norm2_gain: bfloat16 [1536], replicated, may hold values from 0.5 to 1.5
- w_gate: bfloat16 [1536, 8960], P('shard', 'tp'), may hold values from -0.15625 to 0.15625
- w_up: bfloat16 [1536, 8960], P('shard', 'tp'), may hold values from -0.15625 to 0.15625
- w_down: bfloat16 [1536, 8960], P('shard', 'tp'), may hold values from -0.0625 to 0.0625
- parents: int32 [4, 9], P('shard'), may hold values from 0 to 8, as said below
- segment_ids: int32 [4, 2048], P('shard'), may hold values from 0 to 8, as said below
- positions: int32 [4, 2048], P('shard'), may hold values from 0 to 1279, as said below
Outputs:
- output: bfloat16 [4, 2048, 1536], P('shard', 'ctx')
- grad_tokens: bfloat16 [4, 2048, 1536], P('shard', 'ctx')
- grad_norm1: float32 [1536], replicated
- grad_wq: float32 [1536, 1536], P('shard', 'tp')
- grad_bq: float32 [1536], P('tp')
- grad_wk: float32 [1536, 256], P('shard', 'tp')
- grad_bk: float32 [256], P('tp')
- grad_wv: float32 [1536, 256], P('shard', 'tp')
- grad_bv: float32 [256], P('tp')
- grad_wo: float32 [1536, 1536], P('shard', 'tp')
- grad_norm2: float32 [1536], replicated
- grad_wg: float32 [1536, 8960], P('shard', 'tp')
- grad_wu: float32 [1536, 8960], P('shard', 'tp')
- grad_wd: float32 [1536, 8960], P('shard', 'tp')
Inputs may be any that keep to these rules, and one draw needn't show every extreme that they name: `parents`: in each tree one segment, the trunk, is its own parent; four branch segments have the trunk as parent; four leaf segments each have a different branch as parent; segment numbers are shuffled. `segment_ids`: the trunk's 1024 tokens come first; the eight other segments follow with 128 tokens each, in any order. `positions`: trunk tokens count 0 up; a branch's tokens count from 1024, a leaf's from 1152, rising by one along the segment.
All inputs are finite; a program needn't handle non-finite values.
Results may differ from a plain program's by a relative error of at most 0.019.
Values may be sent and summed in bfloat16 or wider, within the bound.
No kernel may reach another device: no remote copies, remote signals or barrier semaphores. Data moves between devices by JAX's collectives and lax.ppermute only.
A program may use at most 320 MiB of HBM per device.

v0:
```python
import jax
import jax.numpy as jnp
from jax import lax
from jax.sharding import PartitionSpec as P

HD = 128


EPS = 1e-06
THETA = 1000000.0
NEG = -1e30


def ancestor_codes(parents):
    count = parents.shape[0]
    ids = jnp.arange(count, dtype=jnp.int32)
    chain = ids
    codes = jnp.left_shift(jnp.ones((count,), jnp.int32), ids)
    for step in range(count - 1):
        chain = jnp.sum(jnp.where(chain[:, None] == ids[None, :], parents[None, :], 0), axis=1)
        codes = jnp.bitwise_or(codes, jnp.left_shift(jnp.ones((count,), jnp.int32), chain))
    return codes


def rope_tables(pos):
    inverse = THETA ** (-jnp.arange(0, HD, 2, dtype=jnp.float32) / HD)
    angle = pos.astype(jnp.float32)[:, None] * inverse[None, :]
    return (
        jnp.concatenate([jnp.cos(angle)] * 2, axis=-1),
        jnp.concatenate([jnp.sin(angle)] * 2, axis=-1),
    )


def rotate_half(v):
    half = v.shape[-1] // 2
    return jnp.concatenate([-v[..., half:], v[..., :half]], axis=-1)


def rope(v, cosine, sine):
    return v * cosine[:, None, :] + rotate_half(v) * sine[:, None, :]


def rope_back(grad, cosine, sine):
    return grad * cosine[:, None, :] - rotate_half(grad * sine[:, None, :])


def contract_last(left, right):
    return lax.dot_general(
        left, right, (((1,), (1,)), ((), ())), preferred_element_type=jnp.float32
    )


def contract_first(left, right):
    return lax.dot_general(
        left, right, (((0,), (0,)), ((), ())), preferred_element_type=jnp.float32
    )


def tensor_sum(value):
    return lax.psum(value, "tp")


def norm_backward(normed_gradient, normalized_input, root_mean_square, norm_gain):
    scaled_rows = normed_gradient * norm_gain
    return root_mean_square * (
        scaled_rows
        - normalized_input * jnp.mean(scaled_rows * normalized_input, axis=-1, keepdims=True)
    )


def body(
    tokens,
    cotangent,
    norm1_gain,
    w_query,
    b_query,
    w_key,
    b_key,
    w_value,
    b_value,
    w_out,
    norm2_gain,
    w_gate,
    w_up,
    w_down,
    parents,
    segment_ids,
    positions,
):
    narrow_dtype = jnp.bfloat16
    rows = tokens.shape[1]
    head_loc = w_query.shape[1] // HD
    kv_loc = w_key.shape[1] // HD
    group = head_loc // kv_loc
    ffp = w_gate.shape[1]
    scale = HD ** (-0.5)
    first_row = lax.axis_index("ctx") * rows
    seg_all = segment_ids[0]
    pos_all = positions[0]
    seg_own = lax.dynamic_slice_in_dim(seg_all, first_row, rows)
    pos_own = lax.dynamic_slice_in_dim(pos_all, first_row, rows)
    codes = ancestor_codes(parents[0])
    seg_range = jnp.arange(codes.shape[0], dtype=jnp.int32)
    code_own = jnp.sum(jnp.where(seg_own[:, None] == seg_range[None, :], codes[None, :], 0), axis=1)
    allowed = (jnp.right_shift(code_own[:, None], seg_all[None, :]) & 1 == 1) & (
        pos_all[None, :] <= pos_own[:, None]
    )
    cosine, sine = rope_tables(pos_own)
    first_gain = norm1_gain.astype(jnp.float32)
    second_gain = norm2_gain.astype(jnp.float32)
    source_rows = tokens[0].astype(jnp.float32)
    first_root_mean = lax.rsqrt(jnp.mean(source_rows * source_rows, axis=-1, keepdims=True) + EPS)
    first_normalized = source_rows * first_root_mean
    first_normed = (first_normalized * first_gain).astype(narrow_dtype)
    wq_all, wk_all, wv_all, wo_all = (
        lax.all_gather(w_query, "shard", axis=0, tiled=True),
        lax.all_gather(w_key, "shard", axis=0, tiled=True),
        lax.all_gather(w_value, "shard", axis=0, tiled=True),
        lax.all_gather(w_out, "shard", axis=0, tiled=True),
    )
    query_lin = jnp.dot(first_normed, wq_all, preferred_element_type=jnp.float32) + b_query.astype(
        jnp.float32
    )
    key_lin = jnp.dot(first_normed, wk_all, preferred_element_type=jnp.float32) + b_key.astype(
        jnp.float32
    )
    value_b = (
        jnp.dot(first_normed, wv_all, preferred_element_type=jnp.float32)
        + b_value.astype(jnp.float32)
    ).astype(narrow_dtype)
    query_b = rope(query_lin.reshape(rows, head_loc, HD), cosine, sine).astype(narrow_dtype)
    key_b = (
        rope(key_lin.reshape(rows, kv_loc, HD), cosine, sine)
        .astype(narrow_dtype)
        .reshape(rows, kv_loc * HD)
    )
    keys_all, values_all = (
        lax.all_gather(key_b, "ctx", axis=0, tiled=True),
        lax.all_gather(value_b, "ctx", axis=0, tiled=True),
    )
    query_heads = jnp.transpose(query_b, (1, 0, 2))
    head_ids = jnp.arange(head_loc, dtype=jnp.int32)

    def head_scores(query_h, head):
        column = head // group * HD
        scores = jnp.where(allowed, contract_last(query_h, keys_all) * scale, NEG)
        return (scores, keys_all, values_all, column)

    def attend(items):
        query_h, head = items
        scores, key_h, value_h, column = head_scores(query_h, head)
        top = jnp.max(scores, axis=1, keepdims=True)
        expo = jnp.exp(scores - top)
        total = jnp.sum(expo, axis=1, keepdims=True)
        probs = (expo / total).astype(narrow_dtype)
        return (
            jnp.dot(probs, value_h, preferred_element_type=jnp.float32),
            (top + jnp.log(total))[:, 0],
        )

    mixed, logsum = lax.map(attend, (query_heads, head_ids))
    mixed_b = jnp.transpose(mixed.astype(narrow_dtype), (1, 0, 2)).reshape(rows, head_loc * HD)
    residual = source_rows + tensor_sum(contract_last(mixed_b, wo_all))
    second_root_mean = lax.rsqrt(jnp.mean(residual * residual, axis=-1, keepdims=True) + EPS)
    second_normalized = residual * second_root_mean
    second_normed = (second_normalized * second_gain).astype(narrow_dtype)
    pieces = (
        lax.all_gather(w_gate, "shard", axis=0, tiled=True),
        lax.all_gather(w_up, "shard", axis=0, tiled=True),
    )
    columns = second_normed
    gate = jnp.dot(columns, pieces[0], preferred_element_type=jnp.float32)
    up = jnp.dot(columns, pieces[1], preferred_element_type=jnp.float32)
    sigma = jax.nn.sigmoid(gate)
    act_b = (gate * sigma * up).astype(narrow_dtype)
    mlp = tensor_sum(contract_last(act_b, lax.all_gather(w_down, "shard", axis=0, tiled=True)))
    output = (residual + mlp).astype(narrow_dtype)
    output_gradient = cotangent[0]
    columns = output_gradient
    grad_act = jnp.dot(
        columns,
        lax.all_gather(w_down, "shard", axis=0, tiled=True),
        preferred_element_type=jnp.float32,
    )
    grad_up_b = (grad_act * gate * sigma).astype(narrow_dtype)
    grad_gate_b = (grad_act * up * sigma * (1.0 + gate * (1.0 - sigma))).astype(narrow_dtype)
    pieces = (
        lax.all_gather(w_gate, "shard", axis=0, tiled=True),
        lax.all_gather(w_up, "shard", axis=0, tiled=True),
    )
    term = contract_last(grad_gate_b, pieces[0]) + contract_last(grad_up_b, pieces[1])
    second_normed_gradient = tensor_sum(term)
    residual_gradient = output_gradient.astype(jnp.float32) + norm_backward(
        second_normed_gradient, second_normalized, second_root_mean, second_gain
    )
    grad_attn_b = residual_gradient.astype(narrow_dtype)
    grad_mixed = jnp.dot(grad_attn_b, wo_all, preferred_element_type=jnp.float32).astype(
        narrow_dtype
    )
    grad_heads = jnp.transpose(grad_mixed.reshape(rows, head_loc, HD), (1, 0, 2))
    kv_zero = jnp.zeros((keys_all.shape[0], kv_loc * HD), jnp.float32)

    def attend_back(carry, items):
        query_h, grad_h, lse_h, head = items
        scores, key_h, value_h, column = head_scores(query_h, head)
        probs = jnp.exp(scores - lse_h[:, None])
        grad_p = contract_last(grad_h, value_h)
        delta = jnp.sum(probs * grad_p, axis=1, keepdims=True)
        grad_s = (probs * (grad_p - delta) * scale).astype(narrow_dtype)
        grad_q = jnp.dot(grad_s, key_h, preferred_element_type=jnp.float32)
        grad_k = contract_first(grad_s, query_h)
        grad_v = contract_first(probs.astype(narrow_dtype), grad_h)
        key_acc, value_acc = carry
        key_acc = key_acc + grad_k
        value_acc = value_acc + grad_v
        return ((key_acc, value_acc), grad_q)

    (grad_keys, grad_values), grad_query = lax.scan(
        attend_back, (kv_zero, kv_zero), (query_heads, grad_heads, logsum, head_ids)
    )
    grad_key_own, grad_value_own = (
        lax.psum_scatter(grad_keys, "ctx", scatter_dimension=0, tiled=True),
        lax.psum_scatter(grad_values, "ctx", scatter_dimension=0, tiled=True),
    )
    grad_q_b = (
        rope_back(jnp.transpose(grad_query, (1, 0, 2)), cosine, sine)
        .astype(narrow_dtype)
        .reshape(rows, head_loc * HD)
    )
    grad_k_b = (
        rope_back(grad_key_own.reshape(rows, kv_loc, HD), cosine, sine)
        .astype(narrow_dtype)
        .reshape(rows, kv_loc * HD)
    )
    grad_v_b = grad_value_own.astype(narrow_dtype)
    first_normed_gradient = tensor_sum(
        contract_last(grad_q_b, wq_all)
        + contract_last(grad_k_b, wk_all)
        + contract_last(grad_v_b, wv_all)
    )
    source_gradient = (
        residual_gradient
        + norm_backward(first_normed_gradient, first_normalized, first_root_mean, first_gain)
    ).astype(narrow_dtype)
    small = lax.psum(
        (
            jnp.sum(first_normed_gradient * first_normalized, axis=0),
            jnp.sum(second_normed_gradient * second_normalized, axis=0),
            jnp.sum(grad_q_b.astype(jnp.float32), axis=0),
            jnp.sum(grad_k_b.astype(jnp.float32), axis=0),
            jnp.sum(grad_v_b.astype(jnp.float32), axis=0),
        ),
        ("shard", "ctx"),
    )
    qwp = w_query.shape[1]
    kwp = w_key.shape[1]
    total_cols = 2 * qwp + 2 * kwp + 3 * ffp
    stacked = lax.psum(
        lax.psum_scatter(
            jnp.concatenate(
                [
                    contract_first(first_normed, grad_q_b),
                    contract_first(first_normed, grad_k_b),
                    contract_first(first_normed, grad_v_b),
                    contract_first(grad_attn_b, mixed_b),
                    contract_first(second_normed, grad_gate_b),
                    contract_first(second_normed, grad_up_b),
                    contract_first(output_gradient, act_b),
                ],
                axis=1,
            ).astype(jnp.bfloat16),
            "shard",
            scatter_dimension=0,
            tiled=True,
        ),
        "ctx",
    ).astype(jnp.float32)
    edges = [
        0,
        qwp,
        qwp + kwp,
        qwp + 2 * kwp,
        2 * qwp + 2 * kwp,
        2 * qwp + 2 * kwp + ffp,
        2 * qwp + 2 * kwp + 2 * ffp,
        total_cols,
    ]
    pieces = [stacked[:, edges[i] : edges[i + 1]] for i in range(7)]
    return (
        output[None],
        source_gradient[None],
        small[0],
        pieces[0],
        small[2],
        pieces[1],
        small[3],
        pieces[2],
        small[4],
        pieces[3],
        small[1],
        pieces[4],
        pieces[5],
        pieces[6],
    )


def solution(mesh):
    return jax.shard_map(
        body,
        mesh=mesh,
        in_specs=(
            P("shard", "ctx", None),
            P("shard", "ctx", None),
            P(),
            P("shard", "tp"),
            P("tp"),
            P("shard", "tp"),
            P("tp"),
            P("shard", "tp"),
            P("tp"),
            P("shard", "tp"),
            P(),
            P("shard", "tp"),
            P("shard", "tp"),
            P("shard", "tp"),
            P("shard", None),
            P("shard", None),
            P("shard", None),
        ),
        out_specs=(
            P("shard", "ctx", None),
            P("shard", "ctx", None),
            P(),
            P("shard", "tp"),
            P("tp"),
            P("shard", "tp"),
            P("tp"),
            P("shard", "tp"),
            P("tp"),
            P("shard", "tp"),
            P(),
            P("shard", "tp"),
            P("shard", "tp"),
            P("shard", "tp"),
        ),
        check_vma=False,
    )
```

profile of v0, /device:TPU:0, one launch (start us, length us, event | category | flops | bytes accessed | tf_op | source)
XLA Modules:
  0.0 2172.1 jit_solution(14289037153219492070)
XLA Ops:
  21.1 21.4 all_gather.31
  43.3 18.3 all_gather.33
  62.3 10.6 all_gather.34
  74.3 9.5 all_gather.32
  92.3 24.1 %while.30 = (s32[]{:T(128)}, bf16[6,512,128]{1,2,0:T(8,128)(2,1)}, f32[6,512]{1,0:T(8,128)S(1)}, bf16[6,512,128]{2,1,0:T(8,128)(2,1)S(1)}, bf16[2048,128]{1,0:T(...) while((s32[]{:T(128)}, bf16[6,512,128]{1,2,0:T(8,128)(2,1)}, ...), condition=%wide.region_13.14_spmd.clone.clone, body=%wide.region_10.13_spmd.clone.sunk.clone | while | flops 550501888 | bytes 14065785 | solution.py:161
  116.4 9.7 all-gather.8.cloned.1.call-done
  126.1 5.0 fusion.82
  133.0 20.3 all-reduce.7.cloned.1.call-done
  157.9 235.7 %all-gather.12.cloned.1.call-done = bf16[1536,4480]{1,0:T(8,128)(2,1)} async-done(((bf16[384,4480]{1,0:T(8,128)(2,1)}), bf16[1536,4480]{1,0:T(8,128)(2,1)}) %all-gather.12.cloned.1.call-update) | async-done | bytes 13762576 | tf_op jit(solution)/shard_map/all_gather | solution.py:169
  393.6 13.7 fusion.84
  407.2 223.6 %all-gather.10.cloned.1.call-done = bf16[1536,4480]{1,0:T(8,128)(2,1)} async-done(((bf16[384,4480]{1,0:T(8,128)(2,1)}), bf16[1536,4480]{1,0:T(8,128)(2,1)}) %all-gather.10.cloned.1.call-update) | async-done | bytes 13762576 | tf_op jit(solution)/shard_map/all_gather | solution.py:168
  630.8 13.3 fusion.83
  644.0 224.0 %all-gather.14.cloned.1.call-done = bf16[1536,4480]{1,0:T(8,128)(2,1)} async-done(((bf16[384,4480]{1,0:T(8,128)(2,1)}), bf16[1536,4480]{1,0:T(8,128)(2,1)}) %all-gather.14.cloned.1.call-update) | async-done | bytes 13762576 | tf_op jit(solution)/shard_map/all_gather | solution.py:176
  868.0 21.9 %multiply_convert_fusion.1 = (bf16[512,4480]{1,0:T(8,128)(2,1)}, bf16[512,4480]{1,0:T(8,128)(2,1)}, bf16[512,4480]{1,0:T(8,128)(2,1)}) fusion(f32[512,4480]{1,0:T(8,128)} %fusion.83, f32[512,4480]{1,0:T(8,128)} %fusion.84, bf16[1536,4480]{1,0:T(8,128)(2,1)} %all-gather.14.cloned.1.call-done, bf16[1,512,1536]{2,1,0:T(8,128)(2,1)} %param.22), kind=kOutput, calls=%fused_computation.46 | convolution fusion | flops 7083130880 | bytes 47448064 | tf_op jit(solution)/shard_map/dot_general | solution.py:180
  889.9 11.8 fusion.86
  901.6 12.2 convolution_add_fusion.4
  913.9 21.5 all-reduce.9.cloned.1.call-done
  945.9 66.2 %while.31 = (s32[]{:T(128)}, f32[2048,128]{1,0:T(8,128)S(1)}, f32[2048,128]{1,0:T(8,128)S(1)}, f32[6,512,128]{1,2,0:T(8,128)}, bf16[6,512,128]{2,1,0:T(8,128)(2,...) while((s32[]{:T(128)}, f32[2048,128]{1,0:T(8,128)S(1)}, ...), condition=%wide.region_21.22_spmd.clone.clone, body=%wide.region_19.21_spmd.clone.sunk.clone | while | flops 1358953984 | bytes 38041764 | solution.py:218
  1013.8 4.7 convolution_convert_fusion.3
  1018.6 4.4 copy.78
  1030.6 4.3 copy.75
  1045.5 28.5 %reduce-scatter.6.cloned.1.call-done = f32[512,128]{1,0:T(8,128)} async-done(((f32[2048,128]{1,0:T(8,128)}), f32[512,128]{1,0:T(8,128)}) %reduce-scatter.6.cloned.1.call-update) | async-done | bytes 262160 | tf_op jit(solution)/shard_map/reduce_scatter | solution.py:223
  1081.4 12.6 fusion.29
  1094.0 10.3 fusion.28
  1104.3 10.2 fusion.31
  1114.9 13.3 fusion.85
  1133.0 747.1 %reduce-scatter.8.cloned.1.call-done = bf16[384,15232]{1,0:T(8,128)(2,1)} async-done(((bf16[1536,15232]{1,0:T(8,128)(2,1)}), bf16[384,15232]{1,0:T(8,128)(2,1)}) %reduce-scatter.8.cloned.1.call-update) | async-done | bytes 11698192 | tf_op jit(solution)/shard_map/reduce_scatter | solution.py:259
  1880.2 37.0 %all-reduce.13.cloned.1.call-done = (f32[512,1536]{1,0:T(8,128)}, f32[512,1536]{1,0:T(8,128)}) async-done(((f32[512,1536]{1,0:T(8,128)}, f32[512,1536]{1,0:T(8,128)}), (f32[512,1536]{1,0:T(8,128)}, f32[512,1536]{1,0:T(8,128)})) %all-reduce.13.cloned.1.call-update) | async-done | bytes 6291472 | tf_op jit(solution)/shard_map/psum | solution.py:60
  1920.4 78.3 %all-reduce = (f32[1536]{0:T(1024)}, f32[768]{0:T(1024)}, f32[128]{0:T(128)}, f32[128]{0:T(128)}, f32[1536]{0:T(1024)}) all-reduce(f32[1536]{0:T(1024)S(1)} %get-tuple-element.256, f32[768]{0:T(1024)S(1)} %bitcast.217, f32[128]{0:T(128)S(1)} %get-tuple-element.311, ...), channel_id=1, replica_groups=mesh['shard'=4,'ctx'=4,'tp'=2] {'shard','ctx'}, use_global_device_ids=true, to_apply=%region_27.28 | all-reduce | flops 4096 | bytes 32768 | tf_op jit(solution)/shard_map/psum | solution.py:245
  1998.7 7.7 fusion.49
  2006.4 144.0 %all-reduce.11.cloned.1.call-done = bf16[384,15232]{1,0:T(8,128)(2,1)} async-done(((bf16[384,15232]{1,0:T(8,128)(2,1)}), bf16[384,15232]{1,0:T(8,128)(2,1)}) %all-reduce.11.cloned.1.call-update) | async-done | bytes 11698192 | tf_op jit(solution)/shard_map/psum | solution.py:258
  2155.0 9.9 fusion.79
  (275 shorter events, 171.9 us)
Async XLA Ops:
  7.2 35.3 %copy-start.5 = (bf16[1,512,1536]{2,1,0:T(8,128)(2,1)S(1)}, bf16[1,512,1536]{2,1,0:T(8,128)(2,1)}, u32[]{:S(2)}) copy-start(bf16[1,512,1536]{2,1,0:T(8,128)(2,1)} %param.21) | copy-start | bytes 4718596
  7.2 13.8 copy-start.43
  7.2 13.9 copy-start.41
  7.2 13.9 copy-start.34
  7.2 77.0 %all-gather.6.cloned.1.call-start = ((), (), s32[]{:S(2)}) async-start(), calls=%async_computation.3 | async-start | bytes 2949120 | tf_op jit(solution)/shard_map/all_gather | solution.py:116
  8.0 118.2 %all-gather.8.cloned.1.call-start = ((), (), s32[]{:S(2)}) async-start(), calls=%async_computation.4 | async-start | bytes 2949120 | tf_op jit(solution)/shard_map/all_gather | solution.py:119
  8.7 144.6 %all-reduce.7.cloned.1.call-start = ((), (), s32[]{:S(2)}) async-start(), calls=%async_computation.5 | async-start | bytes 6291456 | tf_op jit(solution)/shard_map/psum | solution.py:60
  8.8 34.5 %copy-start.35 = (bf16[384,128]{1,0:T(8,128)(2,1)S(1)}, bf16[384,128]{1,0:T(8,128)(2,1)}, u32[]{:S(2)}) copy-start(bf16[384,128]{1,0:T(8,128)(2,1)} %param.28) | copy-start | bytes 294916
  21.0 63.2 %copy-start.39 = (f32[512]{0:T(512)}, f32[512]{0:T(512)S(1)}, u32[]{:S(2)}) copy-start(f32[512]{0:T(512)S(1)} %add_rsqrt_fusion.1) | copy-start | bytes 6148
  21.1 63.1 %copy-start.36 = (f32[1536]{0:T(1024)}, f32[1536]{0:T(1024)S(1)}, u32[]{:S(2)}) copy-start(f32[1536]{0:T(1024)S(1)} %convert_element_type.116) | copy-start | bytes 18436
  42.5 19.8 copy-start.22
  61.6 12.7 copy-start.24
  116.4 14.8 copy-start.7
  116.4 14.8 copy-start.9
  116.4 14.7 copy-start.14
  131.2 262.4 %all-gather.12.cloned.1.call-start = ((), (), s32[]{:S(2)}) async-start(), calls=%async_computation.7 | async-start | bytes 17203200 | tf_op jit(solution)/shard_map/all_gather | solution.py:169
  131.8 499.0 %all-gather.10.cloned.1.call-start = ((), (), s32[]{:S(2)}) async-start(), calls=%async_computation.6 | async-start | bytes 17203200 | tf_op jit(solution)/shard_map/all_gather | solution.py:168
  132.4 735.6 %all-gather.14.cloned.1.call-start = ((), (), s32[]{:S(2)}) async-start(), calls=%async_computation.8 | async-start | bytes 17203200 | tf_op jit(solution)/shard_map/all_gather | solution.py:176
  132.9 802.4 %all-reduce.9.cloned.1.call-start = ((), (), s32[]{:S(2)}) async-start(), calls=%async_computation.9 | async-start | bytes 6291456 | tf_op jit(solution)/shard_map/psum | solution.py:60
  156.2 782.6 %copy-start = (f32[512,1536]{1,0:T(8,128)}, f32[512,1536]{1,0:T(8,128)S(1)}, u32[]{:S(2)}) copy-start(f32[512,1536]{1,0:T(8,128)S(1)} %get-tuple-element.316) | copy-start | bytes 9437188
  913.8 128.7 %reduce-scatter.4.cloned.1.call-start = ((), (), s32[]{:S(2)}) async-start(), calls=%async_computation.10 | async-start | bytes 1310720 | tf_op jit(solution)/shard_map/reduce_scatter | solution.py:222
  1013.5 60.5 %reduce-scatter.6.cloned.1.call-start = ((), (), s32[]{:S(2)}) async-start(), calls=%async_computation.11 | async-start | bytes 1310720 | tf_op jit(solution)/shard_map/reduce_scatter | solution.py:223
  1024.4 855.6 %reduce-scatter.8.cloned.1.call-start = ((), (), s32[]{:S(2)}) async-start(), calls=%async_computation.12 | async-start | bytes 58490880 | tf_op jit(solution)/shard_map/reduce_scatter | solution.py:259
  1076.7 17.3 slice-start
  1081.4 12.6 slice-start.1
  1081.4 22.9 %slice-start.2 = ((s8[4587520]{0:T(1024)(128)(4,1)}), s8[4194304]{0:T(1024)(128)(4,1)S(1)}, s32[]{:S(2)}) async-start(s8[4587520]{0:T(1024)(128)(4,1)} %bitcast.233), calls=%async_computation.17 | async-start | bytes 8388608
  1114.5 13.6 copy-start.32
  1114.6 802.6 %all-reduce.13.cloned.1.call-start = ((), (), s32[]{:S(2)}) async-start(), calls=%async_computation.14 | async-start | bytes 12582912 | tf_op jit(solution)/shard_map/psum | solution.py:60
  1114.9 13.3 copy-start.46
  1132.9 1017.5 %all-reduce.11.cloned.1.call-start = ((), (), s32[]{:S(2)}) async-start(), calls=%async_computation.13 | async-start | bytes 23396352 | tf_op jit(solution)/shard_map/psum | solution.py:258
  1880.1 40.3 %copy-start.38 = (f32[1536]{0:T(1024)S(1)}, f32[1536]{0:T(1024)}, u32[]{:S(2)}) copy-start(f32[1536]{0:T(1024)} %get-tuple-element.254) | copy-start | bytes 18436
  1880.1 118.6 %copy-start.1 = (f32[512,1536]{1,0:T(8,128)S(1)}, f32[512,1536]{1,0:T(8,128)}, u32[]{:S(2)}) copy-start(f32[512,1536]{1,0:T(8,128)} %copy-done) | copy-start | bytes 9437188
  (33 other events, 126.8 us)
Sparse Core Ops, SparseCore 0:
  9.6 65.5 all-gather.5
  76.7 49.3 all-gather.7
  131.3 22.0 all-reduce.6
  154.8 238.6 all-gather.11
  395.0 235.6 all-gather.9
  632.3 235.6 all-gather.13
  913.9 21.3 all-reduce.8
  1013.6 28.8 reduce-scatter.3
  1046.3 27.6 reduce-scatter.5
  1114.7 765.3 reduce-scatter.7
  1883.2 33.9 all-reduce.12
  1921.0 229.3 all-reduce.10
where the time goes:
time: 2180 us; the launch traced here: 2170 us
  waiting for transfers between devices  1700 us (78%)
  matrix products  228 us (10%)
  blocking collectives  138 us (6%)
  other arithmetic  45.8 us (2%)
  local copies, waits for them, and re-layouts  44.6 us (2%)
    reduce_scatter x1, waiting for transfers between devices, body(): lax.psum_scatter(jnp.concatenate([contract_first(first_normed, grad_q_b),...  747 us
    all_gather x1, waiting for transfers between devices, body(): lax.all_gather(w_up, 'shard', axis=0, tiled=True)  236 us
    all_gather x1, waiting for transfers between devices, body(): lax.all_gather(w_down, 'shard', axis=0, tiled=True)  224 us
    all_gather x1, waiting for transfers between devices, body(): lax.all_gather(w_gate, 'shard', axis=0, tiled=True)  224 us
    psum x1, waiting for transfers between devices, body(): lax.psum(lax.psum_scatter(jnp.concatenate([contract_first(first_normed, g...  144 us
    dot_general x25, matrix products, contract_last(): lax.dot_general(left, right, (((1,), (1,)), ((), ())), preferred_element_...  83.9 us
    psum x3, waiting for transfers between devices, tensor_sum(): return lax.psum(value, 'tp')  78.8 us
    psum x1, blocking collectives, body(): lax.psum((jnp.sum(first_normed_gradient * first_normalized, axis=0), jnp....  78.3 us
  transfers between devices with their start and end apart: 12, of which 11 were waited for; matrix products, arithmetic and copies ran while one was open for 6% of the time, Pallas kernels for 0%

commit v1 on v0

v1 whole, which is shorter than its diff:
```python
import functools

import jax
import jax.numpy as jnp
from jax import lax
from jax.experimental import pallas as pl
from jax.experimental.pallas import tpu as pltpu
from jax.sharding import PartitionSpec as P

HD = 128


EPS = 1e-06
THETA = 1000000.0
NEG = -1e30


def ancestor_codes(parents):
    count = parents.shape[0]
    ids = jnp.arange(count, dtype=jnp.int32)
    chain = ids
    codes = jnp.left_shift(jnp.ones((count,), jnp.int32), ids)
    for step in range(count - 1):
        chain = jnp.sum(jnp.where(chain[:, None] == ids[None, :], parents[None, :], 0), axis=1)
        codes = jnp.bitwise_or(codes, jnp.left_shift(jnp.ones((count,), jnp.int32), chain))
    return codes


def rope_tables(pos):
    inverse = THETA ** (-jnp.arange(0, HD, 2, dtype=jnp.float32) / HD)
    angle = pos.astype(jnp.float32)[:, None] * inverse[None, :]
    return (
        jnp.concatenate([jnp.cos(angle)] * 2, axis=-1),
        jnp.concatenate([jnp.sin(angle)] * 2, axis=-1),
    )


def rotate_half(v):
    half = v.shape[-1] // 2
    return jnp.concatenate([-v[..., half:], v[..., :half]], axis=-1)


def rope(v, cosine, sine):
    return v * cosine[:, None, :] + rotate_half(v) * sine[:, None, :]


def rope_back(grad, cosine, sine):
    return grad * cosine[:, None, :] - rotate_half(grad * sine[:, None, :])


def contract_last(left, right):
    return lax.dot_general(
        left, right, (((1,), (1,)), ((), ())), preferred_element_type=jnp.float32
    )


def contract_first(left, right):
    return lax.dot_general(
        left, right, (((0,), (0,)), ((), ())), preferred_element_type=jnp.float32
    )


def norm_backward(normed_gradient, normalized_input, root_mean_square, norm_gain):
    scaled_rows = normed_gradient * norm_gain
    return root_mean_square * (
        scaled_rows
        - normalized_input * jnp.mean(scaled_rows * normalized_input, axis=-1, keepdims=True)
    )


def swap(value, axis, distance):
    size = lax.axis_size(axis)
    return lax.ppermute(value, axis, [(i, i ^ distance) for i in range(size)])


def context_gather(value):
    if lax.axis_size("ctx") != 4:
        return [[value]] + [[swap(value, "ctx", k)] for k in range(1, lax.axis_size("ctx"))]
    half = value.shape[0] // 2
    first = swap(value, "ctx", 1)
    second = swap(value, "ctx", 2)
    far_low = swap(first[:half], "ctx", 2)
    far_high = swap(second[half:], "ctx", 1)
    return [[value], [first], [second], [far_low, far_high]]


def add_narrow(left, right):
    return (left.astype(jnp.float32) + right.astype(jnp.float32)).astype(jnp.bfloat16)


def context_scatter(blocks):
    if lax.axis_size("ctx") != 4:
        total = blocks[0].astype(jnp.float32)
        for k in range(1, lax.axis_size("ctx")):
            total = total + swap(blocks[k].astype(jnp.bfloat16), "ctx", k).astype(jnp.float32)
        return total
    narrow = [block.astype(jnp.bfloat16) for block in blocks[1:]]
    half = blocks[0].shape[0] // 2
    far_low = swap(narrow[2][:half], "ctx", 1)
    far_high = swap(narrow[2][half:], "ctx", 2)
    second = jnp.concatenate(
        [add_narrow(blocks[2][:half], far_low), narrow[1][half:]], axis=0
    )
    first = jnp.concatenate(
        [narrow[0][:half], add_narrow(blocks[1][half:], far_high)], axis=0
    )
    first = swap(first, "ctx", 1)
    second = swap(second, "ctx", 2)
    return blocks[0].astype(jnp.float32) + first.astype(jnp.float32) + second.astype(jnp.float32)


def shard_scatter(terms):
    size = lax.axis_size("shard")
    if size > 4:
        return lax.psum_scatter(terms, "shard", scatter_dimension=0, tiled=False)
    me = lax.axis_index("shard")

    def take(index):
        return lax.dynamic_index_in_dim(
            terms, jnp.clip(index, 0, size - 1), axis=0, keepdims=False
        )

    rising = None
    falling = None
    for step in range(size - 1):
        upward = take(size - 1 - step + me)
        downward = take(me - (size - 1) + step)
        if step:
            upward = add_narrow(upward, rising)
            downward = add_narrow(downward, falling)
        rising = lax.ppermute(upward, "shard", [(i, i + 1) for i in range(step + 1)])
        falling = lax.ppermute(
            downward, "shard", [(i, i - 1) for i in range(size - 1 - step, size)]
        )
    own = take(me).astype(jnp.float32)
    return (own + rising.astype(jnp.float32) + falling.astype(jnp.float32)).astype(jnp.bfloat16)


def spread_kernel(plan, width, total, context_ref, *refs):
    count = len(plan)
    outs = refs[count:]
    context = context_ref[0]
    for ref, (distance, offset, columns) in zip(refs[:count], plan):
        start = jnp.bitwise_xor(context, distance) * width + offset
        size = ref.shape[0]
        for matrix, out in enumerate(outs):
            for piece in range(0, columns, 128):
                place = start + piece

                @pl.when(place < total)
                def _():
                    out[:, pl.ds(pl.multiple_of(place, 128), 128)] = ref[
                        :, pl.ds(matrix * columns + piece, 128)
                    ].astype(jnp.float32)


def spread(blocks, plan, width, total, context):
    rows = blocks[0].shape[0]
    tile = 48 if rows % 48 == 0 else rows
    return pl.pallas_call(
        functools.partial(spread_kernel, plan, width, total),
        grid=(rows // tile,),
        in_specs=[pl.BlockSpec(memory_space=pltpu.SMEM)]
        + [pl.BlockSpec((tile, block.shape[1]), lambda i: (i, 0)) for block in blocks],
        out_specs=[pl.BlockSpec((tile, total), lambda i: (i, 0))] * 3,
        out_shape=[jax.ShapeDtypeStruct((rows, total), jnp.float32)] * 3,
        compiler_params=pltpu.CompilerParams(vmem_limit_bytes=40 * 1024 * 1024),
    )(context.reshape(1), *blocks)


def body(
    tokens,
    cotangent,
    norm1_gain,
    w_query,
    b_query,
    w_key,
    b_key,
    w_value,
    b_value,
    w_out,
    norm2_gain,
    w_gate,
    w_up,
    w_down,
    parents,
    segment_ids,
    positions,
):
    narrow_dtype = jnp.bfloat16
    rows = tokens.shape[1]
    half = rows // 2
    depth = w_query.shape[0]
    model = tokens.shape[2]
    qwp = w_query.shape[1]
    kwp = w_key.shape[1]
    head_loc = qwp // HD
    kv_loc = kwp // HD
    group = head_loc // kv_loc
    ffp = w_gate.shape[1]
    scale = HD ** (-0.5)
    shards = lax.axis_size("shard")
    contexts = lax.axis_size("ctx")
    context = lax.axis_index("ctx")
    core = lax.axis_index("tp")
    first_row = context * rows
    distances = [jnp.bitwise_xor(context, k) for k in range(contexts)]

    def core_half(value):
        return lax.dynamic_slice_in_dim(value, core * half, half)

    def core_join(value):
        other = swap(value, "tp", 1)
        low = jnp.where(core == 0, value, other)
        high = jnp.where(core == 0, other, value)
        return jnp.concatenate([low, high], axis=0)

    def core_reduce(value, count):
        mine = lax.dynamic_slice_in_dim(value, core * count, count)
        other = lax.dynamic_slice_in_dim(value, (1 - core) * count, count)
        return mine.astype(jnp.float32) + swap(other.astype(narrow_dtype), "tp", 1).astype(
            jnp.float32
        )

    def tree_gather(value):
        mine = jnp.concatenate(sum(context_gather(value), []), axis=0)
        return jnp.concatenate([mine, swap(mine, "tp", 1)], axis=0)

    def tree_scatter(value):
        count = value.shape[0] // 2
        mine = value[:count].astype(jnp.float32) + swap(
            value[count:].astype(narrow_dtype), "tp", 1
        ).astype(jnp.float32)
        return context_scatter([mine[k * half : (k + 1) * half] for k in range(contexts)])

    part = depth // contexts
    attention_columns = [w_query, w_key, w_value, w_out]
    inner = qwp + 2 * kwp
    own_rows = jnp.concatenate(
        [lax.dynamic_slice_in_dim(w, context * part, part) for w in attention_columns], axis=1
    )

    def whole_weight(piece):
        columns = piece.shape[1]
        gathered = lax.all_gather(piece, "shard", axis=0, tiled=False)
        blocks = context_gather(gathered)
        whole = jnp.zeros((shards, contexts, part, columns), narrow_dtype)
        for k, block in enumerate(blocks):
            block = jnp.concatenate(block, axis=0)
            whole = lax.dynamic_update_slice(whole, block[:, None], (0, distances[k], 0, 0))
        return whole.reshape(model, columns)

    w_qkv = whole_weight(own_rows[:, :inner])
    wo_all = whole_weight(own_rows[:, inner:])

    width = -(-ffp // (contexts * 128)) * 128
    first_width = width // 256 * 128
    spans = [(0, first_width), (first_width, width - first_width)]
    padding = ((0, 0), (0, width * contexts - ffp))
    gate_pad, up_pad, down_pad = (jnp.pad(w, padding) for w in (w_gate, w_up, w_down))
    ff_weights = []
    for offset, size in spans:
        piece = jnp.concatenate(
            [
                lax.dynamic_slice_in_dim(w, context * width + offset, size, axis=1)
                for w in (gate_pad, up_pad, down_pad)
            ],
            axis=1,
        )
        ff_weights.append(lax.all_gather(piece, "shard", axis=0, tiled=True))

    seg_all = jnp.concatenate(
        [lax.dynamic_slice_in_dim(segment_ids[0], d * rows, rows) for d in distances]
    )
    pos_all = jnp.concatenate(
        [lax.dynamic_slice_in_dim(positions[0], d * rows, rows) for d in distances]
    )
    seg_own = seg_all[:rows]
    pos_own = pos_all[:rows]
    codes = ancestor_codes(parents[0])
    seg_range = jnp.arange(codes.shape[0], dtype=jnp.int32)
    code_own = jnp.sum(jnp.where(seg_own[:, None] == seg_range[None, :], codes[None, :], 0), axis=1)
    allowed = (jnp.right_shift(code_own[:, None], seg_all[None, :]) & 1 == 1) & (
        pos_all[None, :] <= pos_own[:, None]
    )
    cosine, sine = rope_tables(pos_own)
    first_gain = norm1_gain.astype(jnp.float32)
    second_gain = norm2_gain.astype(jnp.float32)
    source_rows = tokens[0].astype(jnp.float32)
    first_root_mean = lax.rsqrt(jnp.mean(source_rows * source_rows, axis=-1, keepdims=True) + EPS)
    first_normalized = source_rows * first_root_mean
    first_normed = (first_normalized * first_gain).astype(narrow_dtype)
    lin = jnp.dot(first_normed, w_qkv, preferred_element_type=jnp.float32)
    query_lin = lin[:, :qwp] + b_query.astype(jnp.float32)
    key_lin = lin[:, qwp : qwp + kwp] + b_key.astype(jnp.float32)
    value_b = (lin[:, qwp + kwp :] + b_value.astype(jnp.float32)).astype(narrow_dtype)
    query_b = rope(query_lin.reshape(rows, head_loc, HD), cosine, sine).astype(narrow_dtype)
    key_b = (
        rope(key_lin.reshape(rows, kv_loc, HD), cosine, sine)
        .astype(narrow_dtype)
        .reshape(rows, kv_loc * HD)
    )
    pairs = jnp.concatenate(
        sum(context_gather(jnp.concatenate([key_b, value_b], axis=1)), []), axis=0
    )
    keys_all, values_all = pairs[:, :kwp], pairs[:, kwp:]
    query_heads = jnp.transpose(query_b, (1, 0, 2))

    def attend(query_h):
        scores = jnp.where(allowed, contract_last(query_h, keys_all) * scale, NEG)
        top = jnp.max(scores, axis=1, keepdims=True)
        expo = jnp.exp(scores - top)
        total = jnp.sum(expo, axis=1, keepdims=True)
        probs = (expo / total).astype(narrow_dtype)
        return (
            jnp.dot(probs, values_all, preferred_element_type=jnp.float32),
            (top + jnp.log(total))[:, 0],
        )

    mixed, logsum = lax.map(attend, query_heads)
    mixed_b = jnp.transpose(mixed.astype(narrow_dtype), (1, 0, 2)).reshape(rows, head_loc * HD)

    output_gradient = cotangent[0]
    gradient_half = core_half(output_gradient).astype(jnp.float32)
    tree_gradient = tree_gather(core_half(output_gradient))

    source_half = core_half(source_rows)
    residual = source_half + core_reduce(contract_last(mixed_b, wo_all), half)
    second_root_mean = lax.rsqrt(jnp.mean(residual * residual, axis=-1, keepdims=True) + EPS)
    second_normalized = residual * second_root_mean
    second_normed = (second_normalized * second_gain).astype(narrow_dtype)
    tree_normed = tree_gather(second_normed)

    mlp = 0.0
    normed_gradient = 0.0
    ff_grads = []
    for (offset, size), weights in zip(spans, ff_weights):
        gate_up_w, down_w = weights[:, : 2 * size], weights[:, 2 * size :]
        gate_up = jnp.dot(tree_normed, gate_up_w, preferred_element_type=jnp.float32)
        gate, up = gate_up[:, :size], gate_up[:, size:]
        sigma = jax.nn.sigmoid(gate)
        act_b = (gate * sigma * up).astype(narrow_dtype)
        grad_act = jnp.dot(tree_gradient, down_w, preferred_element_type=jnp.float32)
        grad_up_b = (grad_act * gate * sigma).astype(narrow_dtype)
        grad_gate_b = (grad_act * up * sigma * (1.0 + gate * (1.0 - sigma))).astype(narrow_dtype)
        grads = jnp.concatenate(
            [
                contract_first(tree_normed, grad_gate_b).astype(narrow_dtype),
                contract_first(tree_normed, grad_up_b).astype(narrow_dtype),
                contract_first(tree_gradient, act_b).astype(narrow_dtype),
            ],
            axis=1,
        )
        ff_grads.append(shard_scatter(grads.reshape(shards, depth, 3 * size)))
        mlp = mlp + contract_last(act_b, down_w)
        normed_gradient = (
            normed_gradient
            + contract_last(grad_gate_b, gate_up_w[:, :size])
            + contract_last(grad_up_b, gate_up_w[:, size:])
        )
    second_normed_gradient = tree_scatter(normed_gradient)
    residual_gradient = gradient_half + norm_backward(
        second_normed_gradient, second_normalized, second_root_mean, second_gain
    )
    grad_attn_b = core_join(residual_gradient.astype(narrow_dtype))
    output = core_join((residual + tree_scatter(mlp)).astype(narrow_dtype))
    grad_mixed = jnp.dot(grad_attn_b, wo_all, preferred_element_type=jnp.float32).astype(
        narrow_dtype
    )
    grad_heads = jnp.transpose(grad_mixed.reshape(rows, head_loc, HD), (1, 0, 2))
    kv_zero = jnp.zeros((keys_all.shape[0], kv_loc * HD), jnp.float32)

    def attend_back(carry, items):
        query_h, grad_h, lse_h = items
        scores = jnp.where(allowed, contract_last(query_h, keys_all) * scale, NEG)
        probs = jnp.exp(scores - lse_h[:, None])
        grad_p = contract_last(grad_h, values_all)
        delta = jnp.sum(probs * grad_p, axis=1, keepdims=True)
        grad_s = (probs * (grad_p - delta) * scale).astype(narrow_dtype)
        grad_q = jnp.dot(grad_s, keys_all, preferred_element_type=jnp.float32)
        grad_k = contract_first(grad_s, query_h)
        grad_v = contract_first(probs.astype(narrow_dtype), grad_h)
        key_acc, value_acc = carry
        return ((key_acc + grad_k, value_acc + grad_v), grad_q)

    (grad_keys, grad_values), grad_query = lax.scan(
        attend_back, (kv_zero, kv_zero), (query_heads, grad_heads, logsum)
    )
    grad_pairs = jnp.concatenate([grad_keys, grad_values], axis=1)
    grad_pairs = context_scatter(
        [grad_pairs[k * rows : (k + 1) * rows] for k in range(contexts)]
    )
    grad_key_own, grad_value_own = grad_pairs[:, :kwp], grad_pairs[:, kwp:]
    grad_q_b = (
        rope_back(jnp.transpose(grad_query, (1, 0, 2)), cosine, sine)
        .astype(narrow_dtype)
        .reshape(rows, head_loc * HD)
    )
    grad_k_b = (
        rope_back(grad_key_own.reshape(rows, kv_loc, HD), cosine, sine)
        .astype(narrow_dtype)
        .reshape(rows, kv_loc * HD)
    )
    grad_v_b = grad_value_own.astype(narrow_dtype)
    grad_qkv = jnp.concatenate([grad_q_b, grad_k_b, grad_v_b], axis=1)
    first_normed_gradient = core_reduce(contract_last(grad_qkv, w_qkv), half)
    source_gradient = core_join(
        (
            residual_gradient
            + norm_backward(
                first_normed_gradient,
                core_half(first_normalized),
                core_half(first_root_mean),
                first_gain,
            )
        ).astype(narrow_dtype)
    )
    gain_sums = jnp.stack(
        [
            jnp.sum(first_normed_gradient * core_half(first_normalized), axis=0),
            jnp.sum(second_normed_gradient * second_normalized, axis=0),
        ]
    )
    bias_sums = jnp.sum(grad_qkv.astype(jnp.float32), axis=0)
    gain_sums = gain_sums + swap(gain_sums, "tp", 1)
    small = lax.psum(
        jnp.concatenate([gain_sums.reshape(-1), bias_sums]),
        ("shard", "ctx"),
    )

    attention_grads = jnp.concatenate(
        [contract_first(first_normed, grad_qkv), contract_first(grad_attn_b, mixed_b)], axis=1
    ).astype(narrow_dtype)
    columns = inner + qwp
    attention_grads = attention_grads.reshape(shards, contexts, part, columns)
    terms = [
        lax.dynamic_index_in_dim(attention_grads, d, axis=1, keepdims=False) for d in distances
    ]
    attention_sum = shard_scatter(context_scatter(terms).astype(narrow_dtype))
    whole = jnp.zeros((contexts, part, columns), narrow_dtype)
    for k, block in enumerate(context_gather(attention_sum)):
        block = jnp.concatenate(block, axis=0)
        whole = lax.dynamic_update_slice(whole, block[None], (distances[k], 0, 0))
    whole = whole.reshape(depth, columns).astype(jnp.float32)

    blocks = []
    plan = []
    for (offset, size), grads in zip(spans, ff_grads):
        for k, block in enumerate(context_gather(grads)):
            blocks.append(jnp.concatenate(block, axis=0))
            plan.append((k, offset, size))
    grad_wg, grad_wu, grad_wd = spread(blocks, tuple(plan), width, ffp, context)

    edges = [0, model, 2 * model, 2 * model + qwp, 2 * model + qwp + kwp, small.shape[0]]
    sums = [small[edges[i] : edges[i + 1]] for i in range(5)]
    return (
        output[None],
        source_gradient[None],
        sums[0],
        whole[:, :qwp],
        sums[2],
        whole[:, qwp : qwp + kwp],
        sums[3],
        whole[:, qwp + kwp : inner],
        sums[4],
        whole[:, inner:],
        sums[1],
        grad_wg,
        grad_wu,
        grad_wd,
    )


def solution(mesh):
    return jax.shard_map(
        body,
        mesh=mesh,
        in_specs=(
            P("shard", "ctx", None),
            P("shard", "ctx", None),
            P(),
            P("shard", "tp"),
            P("tp"),
            P("shard", "tp"),
            P("tp"),
            P("shard", "tp"),
            P("tp"),
            P("shard", "tp"),
            P(),
            P("shard", "tp"),
            P("shard", "tp"),
            P("shard", "tp"),
            P("shard", None),
            P("shard", None),
            P("shard", None),
        ),
        out_specs=(
            P("shard", "ctx", None),
            P("shard", "ctx", None),
            P(),
            P("shard", "tp"),
            P("tp"),
            P("shard", "tp"),
            P("tp"),
            P("shard", "tp"),
            P("tp"),
            P("shard", "tp"),
            P(),
            P("shard", "tp"),
            P("shard", "tp"),
            P("shard", "tp"),
        ),
        check_vma=False,
    )
```

time: 2180 us -> 956 us (0.44)
  waiting for transfers between devices: 1700 us -> 196 us
  starting transfers between devices: 0.94 us -> 102 us
  local copies, waits for them, and re-layouts: 44.6 us -> 139 us
  other arithmetic: 45.8 us -> 113 us
    reduce_scatter x3 -> x0, waiting for transfers between devices: 780 us -> none  [the longest x1 747 us: body(): lax.psum_scatter(jnp.concatenate([contract_first(first_normed, grad_q_b),...]
    all_gather x5 -> x2, waiting for transfers between devices: 693 us -> 33 us  [body(): ff_weights.append(lax.all_gather(piece, 'shard', axis=0, tiled=True))]
    psum x4 -> x0, waiting for transfers between devices: 223 us -> none  [the longest x1 144 us: body(): lax.psum(lax.psum_scatter(jnp.concatenate([contract_first(first_normed, g...]
    ppermute x0 -> x76, waiting for transfers between devices: none -> 163 us  [the longest x58 104 us: swap(): return lax.ppermute(value, axis, [(i, i ^ distance) for i in range(size)])]
    ppermute x0 -> x76, starting transfers between devices: none -> 102 us  [the longest x58 51.9 us: swap(): return lax.ppermute(value, axis, [(i, i ^ distance) for i in range(size)])]
    convert_element_type x3 -> x25, other arithmetic: 2.34 us -> 40.6 us  [the longest x14 26.1 us: add_narrow(): (left.astype(jnp.float32) + right.astype(jnp.float32)).astype(jnp.bfloat16)]
    concatenate x0 -> x10, local copies, waits for them, and re-layouts: none -> 25.3 us  [the longest x2 15.1 us: body(): jnp.concatenate([contract_first(tree_normed, grad_gate_b).astype(narrow_d...]
    all_gather x4 -> x2, blocking collectives: 59.8 us -> 37.4 us  [whole_weight(): gathered = lax.all_gather(piece, 'shard', axis=0, tiled=False)]
  transfers between devices with their start and end apart: 12 -> 78, of which waited for: 11 -> 29; matrix products, arithmetic and copies ran while one was open for 6% -> 50% of each run, Pallas kernels for 0% -> 1%
where the time goes in v1:
time: 956 us; the launch traced here: 946 us
  matrix products  242 us (25%)
  waiting for transfers between devices  196 us (21%)
  local copies, waits for them, and re-layouts  139 us (15%)
  blocking collectives  126 us (13%)
  other arithmetic  113 us (12%)
  starting transfers between devices  102 us (11%)
  between operations  16.4 us (2%)
  Pallas kernels  10.5 us (1%)
    ppermute x58, waiting for transfers between devices, swap(): return lax.ppermute(value, axis, [(i, i ^ distance) for i in range(size)])  104 us
    dot_general x26, matrix products, contract_last(): lax.dot_general(left, right, (((1,), (1,)), ((), ())), preferred_element_...  102 us
    psum x1, blocking collectives, body(): lax.psum(jnp.concatenate([gain_sums.reshape(-1), bias_sums]), ('shard', '...  88.6 us
    dot_general x20, matrix products, contract_first(): lax.dot_general(left, right, (((0,), (0,)), ((), ())), preferred_element_...  64.8 us
    ppermute x58, starting transfers between devices, swap(): return lax.ppermute(value, axis, [(i, i ^ distance) for i in range(size)])  51.9 us
    ppermute x9, waiting for transfers between devices, shard_scatter(): lax.ppermute(upward, 'shard', [(i, i + 1) for i in range(step + 1)])  42.7 us
    ppermute x9, starting transfers between devices, shard_scatter(): lax.ppermute(upward, 'shard', [(i, i + 1) for i in range(step + 1)])  37.8 us
    all_gather x2, blocking collectives, whole_weight(): gathered = lax.all_gather(piece, 'shard', axis=0, tiled=False)  37.4 us
  transfers between devices with their start and end apart: 78, of which 29 were waited for; matrix products, arithmetic and copies ran while one was open for 50% of the time, Pallas kernels for 1%

profile of v1, /device:TPU:0, one launch (start us, length us, event | category | flops | bytes accessed | tf_op | source)
XLA Modules:
  0.0 945.5 jit_solution(11593600743849656848)
XLA Ops:
  9.1 21.7 %all-gather = bf16[384,1024]{1,0:T(8,128)(2,1)} all-gather(bf16[96,1024]{1,0:T(8,128)(2,1)S(1)} %pad_maximum_fusion.20), channel_id=2, replica_groups=mesh['shard'=4,'ctx'=4,'tp'=2] {'shard'}, dimensions={0}, use_global_device_ids=true | all-gather | bytes 983040 | tf_op jit(solution)/shard_map/all_gather | solution.py:245
  34.7 15.7 %all-gather.1 = bf16[384,768]{1,0:T(8,128)(2,1)S(1)} all-gather(bf16[96,768]{1,0:T(8,128)(2,1)S(1)} %constant_dynamic-slice_fusion.1), channel_id=3, replica_groups=mesh['shard'=4,'ctx'=4,'tp'=2] {'shard'}, dimensions={0}, use_global_device_ids=true | all-gather | bytes 737280 | tf_op jit(solution)/shard_map/all_gather | solution.py:245
  119.7 32.0 %while.30 = (s32[]{:T(128)}, bf16[6,512,128]{1,2,0:T(8,128)(2,1)}, f32[6,512]{1,0:T(8,128)}, bf16[6,512,128]{2,1,0:T(8,128)(2,1)S(1)}, bf16[2048,128]{1,0:T(8,12...) while((s32[]{:T(128)}, bf16[6,512,128]{1,2,0:T(8,128)(2,1)}, ...), condition=%wide.region_13.14_spmd.clone.clone, body=%wide.region_10.13_spmd.clone.sunk.clone | while | flops 550501888 | bytes 14065785 | solution.py:320
  174.2 13.9 %collective-permute-done.13 = bf16[256,1536]{1,0:T(8,128)(2,1)S(1)} collective-permute-done((bf16[256,1536]{1,0:T(8,128)(2,1)S(1)}, bf16[256,1536]{1,0:T(8,128)(2,1)S(1)}, u32[]{:S(2)}, u32[]{:S(2)}) %collective-permute-start.13) | collective-permute-done | bytes 786464 | tf_op jit(solution)/shard_map/ppermute | solution.py:73
  212.9 12.9 %fusion.30 = f32[2048,1024]{1,0:T(8,128)} fusion(bf16[2048,1536]{1,0:T(8,128)(2,1)} %constant_dynamic-update-slice_fusion.10, bf16[1536,1536]{1,0:T(8,128)(2,1)} %all-gather.5.cloned.1.call-done), kind=kOutput, calls=%fused_computation.74 | convolution fusion | flops 6442450944 | bytes 17825792 | tf_op jit(solution)/shard_map/dot_general | solution.py:339
  225.8 8.6 multiply_convert_fusion.4
  247.2 6.6 copy.94
  260.8 8.6 fusion.60
  269.3 6.6 fusion.58
  275.9 6.4 fusion.72
  282.3 27.7 %collective-permute-done.56 = bf16[384,1536]{1,0:T(8,128)(2,1)S(1)} collective-permute-done((bf16[384,1536]{1,0:T(8,128)(2,1)S(1)}, bf16[384,1536]{1,0:T(8,128)(2,1)S(1)}, u32[]{:S(2)}, u32[]{:S(2)}) %collective-permute-start.56) | collective-permute-done | bytes 1179680 | tf_op jit(solution)/shard_map/ppermute | solution.py:131
  318.0 33.0 %all-gather.7.cloned.1.call-done = bf16[1536,1920]{1,0:T(8,128)(2,1)} async-done(((bf16[384,1920]{1,0:T(8,128)(2,1)}), bf16[1536,1920]{1,0:T(8,128)(2,1)}) %all-gather.7.cloned.1.call-update) | async-done | bytes 5898256 | tf_op jit(solution)/shard_map/all_gather | solution.py:270
  351.0 13.9 %fusion.28 = f32[2048,1280]{1,0:T(8,128)} fusion(bf16[2048,1536]{1,0:T(8,128)(2,1)} %constant_dynamic-update-slice_fusion.10, bf16[1536,1920]{1,0:T(8,128)(2,1)} %all-gather.7.cloned.1.call-done), kind=kOutput, calls=%fused_computation.63 | convolution fusion | flops 8053063680 | bytes 20709376 | tf_op jit(solution)/shard_map/dot_general | solution.py:339
  364.9 11.6 %multiply_convert_fusion.1 = (bf16[2048,640]{1,0:T(8,128)(2,1)S(1)}, bf16[2048,640]{1,0:T(8,128)(2,1)S(1)}, bf16[2048,640]{1,0:T(8,128)(2,1)S(1)}) fusion(f32[2048,1280]{1,0:T(8,128)} %fusion.28, bf16[2048,1536]{1,0:T(8,128)(2,1)} %constant_dynamic-update-slice_fusion.21, bf16[1536,1920]{1,0:T(8,128)(2,1)} %all-gather.7.cloned.1.call-done), kind=kOutput, calls=%fused_computation.54 | convolution fusion | flops 4047503360 | bytes 26607616 | tf_op jit(solution)/shard_map/dot_general | solution.py:343
  393.4 8.5 copy.95
  405.7 6.0 collective-permute-start.66
  411.7 9.4 fusion.48
  426.6 17.6 %add_add_fusion = f32[2048,1536]{1,0:T(8,128)} fusion(f32[2048,1536]{1,0:T(8,128)} %fusion.48, f32[2048,1536]{1,0:T(8,128)} %fusion.60, f32[2048,1536]{1,0:T(8,128)} %fusion.58, bf16[2048,640]{1,0:T(8,128)(2,1)S(1)} %get-tuple-element.305, bf16[1536,1920]{1,0:T(8,128)(2,1)} %all-gather.7.cloned.1.call-done), kind=kOutput, calls=%fused_computation.39 | convolution fusion | flops 4035969024 | bytes 54919168 | tf_op jit(solution)/shard_map/dot_general | solution.py:52
  462.6 8.8 convolution_add_fusion.2
  478.5 13.2 %collective-permute-done.61 = bf16[384,1536]{1,0:T(8,128)(2,1)} collective-permute-done((bf16[384,1536]{1,0:T(8,128)(2,1)S(1)}, bf16[384,1536]{1,0:T(8,128)(2,1)}, u32[]{:S(2)}, u32[]{:S(2)}) %collective-permute-start.61) | collective-permute-done | bytes 1179680 | tf_op jit(solution)/shard_map/ppermute | solution.py:132
  498.2 11.8 %collective-permute-done.67 = bf16[384,1920]{1,0:T(8,128)(2,1)} collective-permute-done((bf16[384,1920]{1,0:T(8,128)(2,1)}, bf16[384,1920]{1,0:T(8,128)(2,1)}, u32[]{:S(2)}, u32[]{:S(2)}) %collective-permute-start.67) | collective-permute-done | bytes 1474592 | tf_op jit(solution)/shard_map/ppermute | solution.py:131
  527.3 6.5 fusion.113
  560.7 7.0 collective-permute-done.33
  575.7 6.3 collective-permute-done.22
  605.0 94.4 %while.31 = (s32[]{:T(128)}, f32[2048,128]{1,0:T(8,128)S(1)}, f32[2048,128]{1,0:T(8,128)}, f32[6,512,128]{1,2,0:T(8,128)}, bf16[6,512,128]{2,1,0:T(8,128)(2,1)},...) while((s32[]{:T(128)}, f32[2048,128]{1,0:T(8,128)S(1)}, ...), condition=%wide.region_18.19_spmd.clone.clone, body=%wide.region_16.18_spmd.clone.sunk.clone | while | flops 1358953984 | bytes 79984896 | solution.py:386
  732.9 9.4 collective-permute-done.44
  743.2 6.3 collective-permute-done.42
  759.0 20.1 %collective-permute-done.45 = bf16[4,96,1792]{2,1,0:T(8,128)(2,1)S(1)} collective-permute-done((bf16[4,96,1792]{2,1,0:T(8,128)(2,1)S(1)}, bf16[4,96,1792]{2,1,0:T(8,128)(2,1)S(1)}, u32[]{:S(2)}, u32[]{:S(2)}) %collective-permute-start.45) | collective-permute-done | bytes 1376288 | tf_op jit(solution)/shard_map/ppermute | solution.py:73
  784.5 7.5 collective-permute-start.46
  803.4 88.6 %psum.7 = f32[4096]{0:T(1024)S(1)} all-reduce(f32[4096]{0:T(1024)S(1)} %pad_maximum_fusion.21), channel_id=1, replica_groups=mesh['shard'=4,'ctx'=4,'tp'=2] {'shard','ctx'}, use_global_device_ids=true, to_apply=%region_23.24 | all-reduce | flops 4096 | bytes 32768 | tf_op jit(solution)/shard_map/psum | solution.py:426
  910.8 5.5 collective-permute-done.75
  917.7 10.5 %shard_map.272 = (f32[384,4480]{1,0:T(8,128)}, f32[384,4480]{1,0:T(8,128)}, f32[384,4480]{1,0:T(8,128)}) custom-call(s32[1]{0:T(128)} %bitcast.75.context_ref, bf16[384,1536]{1,0:T(8,128)(2,1)S(1)} %fusion.46.refs_0_, bf16[384,1536]{1,0:T(8,128)(2,1)S(1)} %copy-done.4, bf16[384,1536]{1,0:T(8,128)(2,1)S(1)} %copy-done.6, bf16[384,1536]{1,0:T(8,128)(2,1)S(1)} %copy-done.2, ...), custom_call_target="tpu_custom_call" | custom-call | tf_op jit(solution)/shard_map/pallas_call | solution.py:160
  (648 shorter events, 498.6 us)
Async XLA Ops:
  7.2 205.7 %all-gather.5.cloned.1.call-start = ((), (), s32[]{:S(2)}) async-start(), calls=%async_computation | async-start | bytes 5898240 | tf_op jit(solution)/shard_map/all_gather | solution.py:270
  30.8 48.5 %collective-permute-start = (bf16[4,96,1024]{2,1,0:T(8,128)(2,1)}, bf16[4,96,1024]{2,1,0:T(8,128)(2,1)}, u32[]{:S(2)}, u32[]{:S(2)}) collective-permute-start(bf16[4,96,1024]{2,1,0:T(8,128)(2,1)} %bitcast.4), channel_id=1, source_target_pairs={{0,2},{2,0},{4,6},{6,4},{1,3},{3,1},{5,7},{7,5},{8,10},{10,8},{12,... | collective-permute-start | bytes 2359304 | tf_op jit(solution)/shard_map/ppermute | solution.py:73
  32.3 44.5 %collective-permute-start.1 = (bf16[4,96,1024]{2,1,0:T(8,128)(2,1)}, bf16[4,96,1024]{2,1,0:T(8,128)(2,1)}, u32[]{:S(2)}, u32[]{:S(2)}) collective-permute-start(bf16[4,96,1024]{2,1,0:T(8,128)(2,1)} %bitcast.4), channel_id=1, source_target_pairs={{0,4},{2,6},{4,0},{6,2},{1,5},{3,7},{5,1},{7,3},{8,12},{10,14},{12... | collective-permute-start | bytes 2359304 | tf_op jit(solution)/shard_map/ppermute | solution.py:73
  52.7 105.1 %collective-permute-start.24 = (bf16[256,1536]{1,0:T(8,128)(2,1)S(1)}, bf16[256,1536]{1,0:T(8,128)(2,1)}, u32[]{:S(2)}, u32[]{:S(2)}) collective-permute-start(bf16[256,1536]{1,0:T(8,128)(2,1)S(1)} %get-tuple-element.294), channel_id=1, source_target_pairs={{0,2},{2,0},{4,6},{6,4},{1,3},{3,1},{5,7},{7,5},{8,10},{10,8},{12,... | collective-permute-start | bytes 2359304 | tf_op jit(solution)/shard_map/ppermute | solution.py:73
  57.4 293.6 %all-gather.7.cloned.1.call-start = ((), (), s32[]{:S(2)}) async-start(), calls=%async_computation.1 | async-start | bytes 7372800 | tf_op jit(solution)/shard_map/all_gather | solution.py:270
  87.6 72.5 %collective-permute-start.25 = (bf16[256,1536]{1,0:T(8,128)(2,1)S(1)}, bf16[256,1536]{1,0:T(8,128)(2,1)}, u32[]{:S(2)}, u32[]{:S(2)}) collective-permute-start(bf16[256,1536]{1,0:T(8,128)(2,1)S(1)} %get-tuple-element.294), channel_id=1, source_target_pairs={{0,4},{2,6},{4,0},{6,2},{1,5},{3,7},{5,1},{7,3},{8,12},{10,14},{12... | collective-permute-start | bytes 2359304 | tf_op jit(solution)/shard_map/ppermute | solution.py:73
  174.1 31.1 %collective-permute-start.28 = (bf16[1024,1536]{1,0:T(8,128)(2,1)}, bf16[1024,1536]{1,0:T(8,128)(2,1)}, u32[]{:S(2)}, u32[]{:S(2)}) collective-permute-start(bf16[1024,1536]{1,0:T(8,128)(2,1)} %get-tuple-element.375), channel_id=1, source_target_pairs={{0,1},{1,0},{2,3},{3,2},{4,5},{5,4},{6,7},{7,6},{8,9},{9,8},{10,11... | collective-permute-start | bytes 9437192 | tf_op jit(solution)/shard_map/ppermute | solution.py:73
  256.7 53.3 %collective-permute-start.56 = (bf16[384,1536]{1,0:T(8,128)(2,1)S(1)}, bf16[384,1536]{1,0:T(8,128)(2,1)S(1)}, u32[]{:S(2)}, u32[]{:S(2)}) collective-permute-start(bf16[384,1536]{1,0:T(8,128)(2,1)S(1)} %get-tuple-element.324), channel_id=1, source_target_pairs={{0,8},{1,9},{2,10},{3,11},{4,12},{5,13},{6,14},{7,15}} | collective-permute-start | bytes 3538952 | tf_op jit(solution)/shard_map/ppermute | solution.py:131
  258.9 162.3 %collective-permute-start.59 = (bf16[384,1536]{1,0:T(8,128)(2,1)}, bf16[384,1536]{1,0:T(8,128)(2,1)}, u32[]{:S(2)}, u32[]{:S(2)}) collective-permute-start(bf16[384,1536]{1,0:T(8,128)(2,1)} %get-tuple-element.325), channel_id=1, source_target_pairs={{24,16},{25,17},{26,18},{27,19},{28,20},{29,21},{30,22},{31,23}} | collective-permute-start | bytes 3538952 | tf_op jit(solution)/shard_map/ppermute | solution.py:132
  312.6 108.5 %collective-permute-start.57 = (bf16[384,1536]{1,0:T(8,128)(2,1)}, bf16[384,1536]{1,0:T(8,128)(2,1)}, u32[]{:S(2)}, u32[]{:S(2)}) collective-permute-start(bf16[384,1536]{1,0:T(8,128)(2,1)} %fusion.43), channel_id=1, source_target_pairs={{0,8},{8,16},{1,9},{9,17},{2,10},{10,18},{3,11},{11,19},{4,12},{12... | collective-permute-start | bytes 3538952 | tf_op jit(solution)/shard_map/ppermute | solution.py:131
  405.7 46.6 %collective-permute-start.66 = (bf16[384,1920]{1,0:T(8,128)(2,1)}, bf16[384,1920]{1,0:T(8,128)(2,1)}, u32[]{:S(2)}, u32[]{:S(2)}) collective-permute-start(bf16[384,1920]{1,0:T(8,128)(2,1)} %get-tuple-element.317), channel_id=1, source_target_pairs={{0,8},{1,9},{2,10},{3,11},{4,12},{5,13},{6,14},{7,15}} | collective-permute-start | bytes 4423688 | tf_op jit(solution)/shard_map/ppermute | solution.py:131
  424.8 34.6 %collective-permute-start.60 = (bf16[384,1536]{1,0:T(8,128)(2,1)}, bf16[384,1536]{1,0:T(8,128)(2,1)}, u32[]{:S(2)}, u32[]{:S(2)}) collective-permute-start(bf16[384,1536]{1,0:T(8,128)(2,1)} %get-tuple-element.323), channel_id=1, source_target_pairs={{16,8},{24,16},{17,9},{25,17},{18,10},{26,18},{19,11},{27,19},{20,... | collective-permute-start | bytes 3538952 | tf_op jit(solution)/shard_map/ppermute | solution.py:132
  449.1 67.9 %collective-permute-start.29 = (bf16[1024,1536]{1,0:T(8,128)(2,1)}, bf16[1024,1536]{1,0:T(8,128)(2,1)}, u32[]{:S(2)}, u32[]{:S(2)}) collective-permute-start(bf16[1024,1536]{1,0:T(8,128)(2,1)} %slice.579), channel_id=1, source_target_pairs={{0,1},{1,0},{2,3},{3,2},{4,5},{5,4},{6,7},{7,6},{8,9},{9,8},{10,11... | collective-permute-start | bytes 9437192 | tf_op jit(solution)/shard_map/ppermute | solution.py:73
  449.1 47.2 %collective-permute-start.69 = (bf16[384,1920]{1,0:T(8,128)(2,1)}, bf16[384,1920]{1,0:T(8,128)(2,1)}, u32[]{:S(2)}, u32[]{:S(2)}) collective-permute-start(bf16[384,1920]{1,0:T(8,128)(2,1)} %get-tuple-element.318), channel_id=1, source_target_pairs={{24,16},{25,17},{26,18},{27,19},{28,20},{29,21},{30,22},{31,23}} | collective-permute-start | bytes 4423688 | tf_op jit(solution)/shard_map/ppermute | solution.py:132
  455.5 54.5 %collective-permute-start.67 = (bf16[384,1920]{1,0:T(8,128)(2,1)}, bf16[384,1920]{1,0:T(8,128)(2,1)}, u32[]{:S(2)}, u32[]{:S(2)}) collective-permute-start(bf16[384,1920]{1,0:T(8,128)(2,1)} %fusion.35), channel_id=1, source_target_pairs={{0,8},{8,16},{1,9},{9,17},{2,10},{10,18},{3,11},{11,19},{4,12},{12... | collective-permute-start | bytes 4423688 | tf_op jit(solution)/shard_map/ppermute | solution.py:131
  461.3 30.4 %collective-permute-start.61 = (bf16[384,1536]{1,0:T(8,128)(2,1)S(1)}, bf16[384,1536]{1,0:T(8,128)(2,1)}, u32[]{:S(2)}, u32[]{:S(2)}) collective-permute-start(bf16[384,1536]{1,0:T(8,128)(2,1)S(1)} %fusion.42), channel_id=1, source_target_pairs={{8,0},{16,8},{24,16},{9,1},{17,9},{25,17},{10,2},{18,10},{26,18},{... | collective-permute-start | bytes 3538952 | tf_op jit(solution)/shard_map/ppermute | solution.py:132
  478.5 46.8 %collective-permute-start.18 = (bf16[1024,1536]{1,0:T(8,128)(2,1)}, bf16[1024,1536]{1,0:T(8,128)(2,1)}, u32[]{:S(2)}, u32[]{:S(2)}) collective-permute-start(bf16[1024,1536]{1,0:T(8,128)(2,1)} %slice.580), channel_id=1, source_target_pairs={{0,1},{1,0},{2,3},{3,2},{4,5},{5,4},{6,7},{7,6},{8,9},{9,8},{10,11... | collective-permute-start | bytes 9437192 | tf_op jit(solution)/shard_map/ppermute | solution.py:73
  493.8 57.1 %collective-permute-start.62 = (bf16[384,1536]{1,0:T(8,128)(2,1)S(1)}, bf16[384,1536]{1,0:T(8,128)(2,1)S(1)}, u32[]{:S(2)}, u32[]{:S(2)}) collective-permute-start(bf16[384,1536]{1,0:T(8,128)(2,1)S(1)} %fusion.46.refs_0_), channel_id=1, source_target_pairs={{0,2},{2,0},{4,6},{6,4},{1,3},{3,1},{5,7},{7,5},{8,10},{10,8},{12,... | collective-permute-start | bytes 3538952 | tf_op jit(solution)/shard_map/ppermute | solution.py:73
  496.3 55.0 %collective-permute-start.63 = (bf16[384,1536]{1,0:T(8,128)(2,1)S(1)}, bf16[384,1536]{1,0:T(8,128)(2,1)S(1)}, u32[]{:S(2)}, u32[]{:S(2)}) collective-permute-start(bf16[384,1536]{1,0:T(8,128)(2,1)S(1)} %fusion.46.refs_0_), channel_id=1, source_target_pairs={{0,4},{2,6},{4,0},{6,2},{1,5},{3,7},{5,1},{7,3},{8,12},{10,14},{12... | collective-permute-start | bytes 3538952 | tf_op jit(solution)/shard_map/ppermute | solution.py:73
  515.1 75.0 %collective-permute-start.70 = (bf16[384,1920]{1,0:T(8,128)(2,1)}, bf16[384,1920]{1,0:T(8,128)(2,1)}, u32[]{:S(2)}, u32[]{:S(2)}) collective-permute-start(bf16[384,1920]{1,0:T(8,128)(2,1)} %get-tuple-element.316), channel_id=1, source_target_pairs={{16,8},{24,16},{17,9},{25,17},{18,10},{26,18},{19,11},{27,19},{20,... | collective-permute-start | bytes 4423688 | tf_op jit(solution)/shard_map/ppermute | solution.py:132
  550.9 31.0 %collective-permute-start.22 = (bf16[256,1536]{1,0:T(8,128)(2,1)}, bf16[256,1536]{1,0:T(8,128)(2,1)}, u32[]{:S(2)}, u32[]{:S(2)}) collective-permute-start(bf16[256,1536]{1,0:T(8,128)(2,1)} %pad_maximum_fusion.12), channel_id=1, source_target_pairs={{0,4},{2,6},{4,0},{6,2},{1,5},{3,7},{5,1},{7,3},{8,12},{10,14},{12... | collective-permute-start | bytes 2359304 | tf_op jit(solution)/shard_map/ppermute | solution.py:73
  552.3 32.4 %collective-permute-start.20 = (bf16[256,1536]{1,0:T(8,128)(2,1)}, bf16[256,1536]{1,0:T(8,128)(2,1)}, u32[]{:S(2)}, u32[]{:S(2)}) collective-permute-start(bf16[256,1536]{1,0:T(8,128)(2,1)} %pad_maximum_fusion.11), channel_id=1, source_target_pairs={{0,2},{2,0},{4,6},{6,4},{1,3},{3,1},{5,7},{7,5},{8,10},{10,8},{12,... | collective-permute-start | bytes 2359304 | tf_op jit(solution)/shard_map/ppermute | solution.py:73
  567.7 185.6 %collective-permute-start.68 = (bf16[384,1920]{1,0:T(8,128)(2,1)}, bf16[384,1920]{1,0:T(8,128)(2,1)}, u32[]{:S(2)}, u32[]{:S(2)}) collective-permute-start(bf16[384,1920]{1,0:T(8,128)(2,1)} %get-tuple-element.315), channel_id=1, source_target_pairs={{0,8},{8,16},{16,24},{1,9},{9,17},{17,25},{2,10},{10,18},{18,26},{... | collective-permute-start | bytes 4423688 | tf_op jit(solution)/shard_map/ppermute | solution.py:131
  590.1 115.7 %collective-permute-start.23 = (bf16[256,1536]{1,0:T(8,128)(2,1)}, bf16[256,1536]{1,0:T(8,128)(2,1)}, u32[]{:S(2)}, u32[]{:S(2)}) collective-permute-start(bf16[256,1536]{1,0:T(8,128)(2,1)} %get-tuple-element.350), channel_id=1, source_target_pairs={{0,1},{1,0},{2,3},{3,2},{4,5},{5,4},{6,7},{7,6},{8,9},{9,8},{10,11... | collective-permute-start | bytes 2359304 | tf_op jit(solution)/shard_map/ppermute | solution.py:73
  594.7 158.6 %collective-permute-start.71 = (bf16[384,1920]{1,0:T(8,128)(2,1)}, bf16[384,1920]{1,0:T(8,128)(2,1)}, u32[]{:S(2)}, u32[]{:S(2)}) collective-permute-start(bf16[384,1920]{1,0:T(8,128)(2,1)} %fusion.34), channel_id=1, source_target_pairs={{8,0},{16,8},{24,16},{9,1},{17,9},{25,17},{10,2},{18,10},{26,18},{... | collective-permute-start | bytes 4423688 | tf_op jit(solution)/shard_map/ppermute | solution.py:132
  742.7 36.3 %collective-permute-start.45 = (bf16[4,96,1792]{2,1,0:T(8,128)(2,1)S(1)}, bf16[4,96,1792]{2,1,0:T(8,128)(2,1)S(1)}, u32[]{:S(2)}, u32[]{:S(2)}) collective-permute-start(bf16[4,96,1792]{2,1,0:T(8,128)(2,1)S(1)} %pad_maximum_fusion.6), channel_id=1, source_target_pairs={{0,4},{2,6},{4,0},{6,2},{1,5},{3,7},{5,1},{7,3},{8,12},{10,14},{12... | collective-permute-start | bytes 4128776 | tf_op jit(solution)/shard_map/ppermute | solution.py:73
  749.9 33.2 %collective-permute-start.43 = (bf16[4,96,1792]{2,1,0:T(8,128)(2,1)S(1)}, bf16[4,96,1792]{2,1,0:T(8,128)(2,1)S(1)}, u32[]{:S(2)}, u32[]{:S(2)}) collective-permute-start(bf16[4,96,1792]{2,1,0:T(8,128)(2,1)S(1)} %pad_maximum_fusion.5), channel_id=1, source_target_pairs={{0,2},{2,0},{4,6},{6,4},{1,3},{3,1},{5,7},{7,5},{8,10},{10,8},{12,... | collective-permute-start | bytes 4128776 | tf_op jit(solution)/shard_map/ppermute | solution.py:73
  756.2 146.7 %collective-permute-start.72 = (bf16[384,1920]{1,0:T(8,128)(2,1)S(1)}, bf16[384,1920]{1,0:T(8,128)(2,1)}, u32[]{:S(2)}, u32[]{:S(2)}) collective-permute-start(bf16[384,1920]{1,0:T(8,128)(2,1)S(1)} %fusion.38.refs_4_), channel_id=1, source_target_pairs={{0,2},{2,0},{4,6},{6,4},{1,3},{3,1},{5,7},{7,5},{8,10},{10,8},{12,... | collective-permute-start | bytes 4423688 | tf_op jit(solution)/shard_map/ppermute | solution.py:73
  757.3 144.4 %collective-permute-start.73 = (bf16[384,1920]{1,0:T(8,128)(2,1)S(1)}, bf16[384,1920]{1,0:T(8,128)(2,1)}, u32[]{:S(2)}, u32[]{:S(2)}) collective-permute-start(bf16[384,1920]{1,0:T(8,128)(2,1)S(1)} %fusion.38.refs_4_), channel_id=1, source_target_pairs={{0,4},{2,6},{4,0},{6,2},{1,5},{3,7},{5,1},{7,3},{8,12},{10,14},{12... | collective-permute-start | bytes 4423688 | tf_op jit(solution)/shard_map/ppermute | solution.py:73
  793.4 106.8 %collective-permute-start.40 = (bf16[256,1536]{1,0:T(8,128)(2,1)}, bf16[256,1536]{1,0:T(8,128)(2,1)}, u32[]{:S(2)}, u32[]{:S(2)}) collective-permute-start(bf16[256,1536]{1,0:T(8,128)(2,1)} %add_convert_fusion), channel_id=1, source_target_pairs={{0,1},{1,0},{2,3},{3,2},{4,5},{5,4},{6,7},{7,6},{8,9},{9,8},{10,11... | collective-permute-start | bytes 2359304 | tf_op jit(solution)/shard_map/ppermute | solution.py:73
  796.7 95.2 %collective-permute-start.49 = (bf16[96,1792]{1,0:T(8,128)(2,1)}, bf16[96,1792]{1,0:T(8,128)(2,1)S(1)}, u32[]{:S(2)}, u32[]{:S(2)}) collective-permute-start(bf16[96,1792]{1,0:T(8,128)(2,1)} %get-tuple-element.358), channel_id=1, source_target_pairs={{24,16},{25,17},{26,18},{27,19},{28,20},{29,21},{30,22},{31,23}} | collective-permute-start | bytes 1032200 | tf_op jit(solution)/shard_map/ppermute | solution.py:132
  798.2 94.5 %collective-permute-start.47 = (bf16[96,1792]{1,0:T(8,128)(2,1)}, bf16[96,1792]{1,0:T(8,128)(2,1)}, u32[]{:S(2)}, u32[]{:S(2)}) collective-permute-start(bf16[96,1792]{1,0:T(8,128)(2,1)} %fusion.91), channel_id=1, source_target_pairs={{0,8},{8,16},{1,9},{9,17},{2,10},{10,18},{3,11},{11,19},{4,12},{12... | collective-permute-start | bytes 1032200 | tf_op jit(solution)/shard_map/ppermute | solution.py:131
  (159 other events, 1581.1 us)
Sparse Core Ops, SparseCore 0:
  57.5 87.6 all-gather.4
  205.4 145.5 all-gather.6

commit v2 on v1

v2 whole, which is shorter than its diff:
```python
import functools

import jax
import jax.numpy as jnp
from jax import lax
from jax.experimental import pallas as pl
from jax.experimental.pallas import tpu as pltpu
from jax.sharding import PartitionSpec as P

HD = 128


EPS = 1e-06
THETA = 1000000.0
NEG = -1e30


def ancestor_codes(parents):
    count = parents.shape[0]
    ids = jnp.arange(count, dtype=jnp.int32)
    chain = ids
    codes = jnp.left_shift(jnp.ones((count,), jnp.int32), ids)
    for step in range(count - 1):
        chain = jnp.sum(jnp.where(chain[:, None] == ids[None, :], parents[None, :], 0), axis=1)
        codes = jnp.bitwise_or(codes, jnp.left_shift(jnp.ones((count,), jnp.int32), chain))
    return codes


def rope_tables(pos):
    inverse = THETA ** (-jnp.arange(0, HD, 2, dtype=jnp.float32) / HD)
    angle = pos.astype(jnp.float32)[:, None] * inverse[None, :]
    return (
        jnp.concatenate([jnp.cos(angle)] * 2, axis=-1),
        jnp.concatenate([jnp.sin(angle)] * 2, axis=-1),
    )


def rotate_half(v):
    half = v.shape[-1] // 2
    return jnp.concatenate([-v[..., half:], v[..., :half]], axis=-1)


def rope(v, cosine, sine):
    return v * cosine[:, None, :] + rotate_half(v) * sine[:, None, :]


def rope_back(grad, cosine, sine):
    return grad * cosine[:, None, :] - rotate_half(grad * sine[:, None, :])


def contract_last(left, right):
    return lax.dot_general(
        left, right, (((1,), (1,)), ((), ())), preferred_element_type=jnp.float32
    )


def contract_first(left, right):
    return lax.dot_general(
        left, right, (((0,), (0,)), ((), ())), preferred_element_type=jnp.float32
    )


def norm_backward(normed_gradient, normalized_input, root_mean_square, norm_gain):
    scaled_rows = normed_gradient * norm_gain
    return root_mean_square * (
        scaled_rows
        - normalized_input * jnp.mean(scaled_rows * normalized_input, axis=-1, keepdims=True)
    )


def swap(value, axis, distance):
    size = lax.axis_size(axis)
    return lax.ppermute(value, axis, [(i, i ^ distance) for i in range(size)])


def after(value, *others):
    return lax.optimization_barrier((value, *others))[0]


def context_gather_start(value):
    return swap(value, "ctx", 1), swap(value, "ctx", 2)


def context_gather_end(value, first, second):
    half = value.shape[0] // 2
    far_low = swap(first[:half], "ctx", 2)
    far_high = swap(second[half:], "ctx", 1)
    return [[value], [first], [second], [far_low, far_high]]


def context_gather(value):
    return context_gather_end(value, *context_gather_start(value))


def context_send(blocks):
    return [blocks[0]] + [swap(blocks[k], "ctx", k) for k in range(1, len(blocks))]


def context_sum(blocks):
    received = context_send([block.astype(jnp.bfloat16) for block in blocks])
    return sum(block.astype(jnp.float32) for block in (blocks[0], *received[1:]))


def spread_kernel(plan, width, total, context_ref, *refs):
    count = len(plan)
    outs = refs[count:]
    context = context_ref[0]
    for ref, (distance, offset, columns, matrices) in zip(refs[:count], plan):
        start = jnp.bitwise_xor(context, distance) * width + offset
        for slot, matrix in enumerate(matrices):
            out = outs[matrix]
            for piece in range(0, columns, 128):
                place = start + piece

                @pl.when(place < total)
                def _():
                    out[:, pl.ds(pl.multiple_of(place, 128), 128)] = ref[
                        :, pl.ds(slot * columns + piece, 128)
                    ].astype(jnp.float32)


def spread(blocks, plan, width, total, context):
    rows = blocks[0].shape[0]
    tile = 48 if rows % 48 == 0 else rows
    return pl.pallas_call(
        functools.partial(spread_kernel, plan, width, total),
        grid=(rows // tile,),
        in_specs=[pl.BlockSpec(memory_space=pltpu.SMEM)]
        + [pl.BlockSpec((tile, block.shape[1]), lambda i: (i, 0)) for block in blocks],
        out_specs=[pl.BlockSpec((tile, total), lambda i: (i, 0))] * 3,
        out_shape=[jax.ShapeDtypeStruct((rows, total), jnp.float32)] * 3,
        compiler_params=pltpu.CompilerParams(vmem_limit_bytes=40 * 1024 * 1024),
    )(context.reshape(1), *blocks)


def place_kernel(count, context_ref, *refs):
    query_ref, key_ref, value_ref, out_ref = refs[2 * count :]
    context = context_ref[0]
    quarter = refs[0].shape[1]
    part = refs[count].shape[0]
    whole = query_ref.shape[1] // quarter
    keys = key_ref.shape[1]
    for k in range(count):
        place = jnp.bitwise_xor(context, k)
        block = refs[k][...].astype(jnp.float32)

        @pl.when(place < whole)
        def _():
            query_ref[:, pl.ds(pl.multiple_of(place * quarter, 128), quarter)] = block

        @pl.when(place == whole)
        def _():
            key_ref[...] = block[:, :keys]
            value_ref[...] = block[:, keys:]

        row = pl.multiple_of(place * part, 8)
        out_ref[pl.ds(row, part), :] = refs[count + k][...].astype(jnp.float32)


def place_attention(columns, rows, query_width, key_width, context):
    count = len(columns)
    depth = columns[0].shape[0]
    widths = (query_width, key_width, key_width, query_width)
    vmem = pl.BlockSpec(memory_space=pltpu.VMEM)
    return pl.pallas_call(
        functools.partial(place_kernel, count),
        in_specs=[pl.BlockSpec(memory_space=pltpu.SMEM)] + [vmem] * (2 * count),
        out_specs=[vmem] * 4,
        out_shape=[jax.ShapeDtypeStruct((depth, width), jnp.float32) for width in widths],
        compiler_params=pltpu.CompilerParams(vmem_limit_bytes=VMEM_LIMIT),
    )(context.reshape(1), *columns, *rows)


NT = (((1,), (1,)), ((), ()))
NN = (((1,), (0,)), ((), ()))
TN = (((0,), (0,)), ((), ()))
VMEM_LIMIT = 56 * 1024 * 1024


def multiply(left, right, dims):
    return lax.dot_general(left, right, dims, preferred_element_type=jnp.float32)


def ff_kernel(size, first, normed_ref, gradient_ref, weight_ref, *refs):
    inputs, (acts_ref, *outs) = ((), refs) if first else (refs[:4], refs[4:])
    normed = normed_ref[...]
    gate_up = multiply(normed, weight_ref[:, : 2 * size], NN)
    gate, up = gate_up[:, :size], gate_up[:, size:]
    grad_act = multiply(gradient_ref[...], weight_ref[:, 2 * size :], NN)
    sigma = 1.0 / (1.0 + jnp.exp(-gate))
    silu = gate * sigma
    act = (silu * up).astype(jnp.bfloat16)
    grad_up = (grad_act * silu).astype(jnp.bfloat16)
    grad_gate = (grad_act * up * (sigma * (1.0 + gate * (1.0 - sigma)))).astype(jnp.bfloat16)
    acts_ref[:, :size] = grad_gate
    acts_ref[:, size : 2 * size] = grad_up
    acts_ref[:, 2 * size :] = act
    back = multiply(grad_gate, weight_ref[:, :size], NT) + multiply(
        grad_up, weight_ref[:, size : 2 * size], NT
    )
    mlp = multiply(act, weight_ref[:, 2 * size :], NT)
    late = pl.program_id(0) >= pl.num_programs(0) // 2
    for side in range(2):

        @pl.when(late == (side == 1))
        def _():
            for which, value in enumerate((mlp, back)):
                if not first:
                    value = value + inputs[2 * which + side][...].astype(jnp.float32)
                outs[2 * which + side][...] = value.astype(jnp.bfloat16)


def feed_forward(normed, gradient, weights, previous=(), tile=256):
    rows, model = normed.shape
    columns = weights.shape[1]
    steps = rows // tile // 2
    row = pl.BlockSpec((tile, model), lambda i: (i, 0))
    sides = [
        pl.BlockSpec((tile, model), lambda i: (jnp.minimum(i, steps - 1), 0)),
        pl.BlockSpec((tile, model), lambda i: (jnp.maximum(i - steps, 0), 0)),
    ] * 2
    return pl.pallas_call(
        functools.partial(ff_kernel, columns // 3, not previous),
        grid=(rows // tile,),
        in_specs=[row, row, pl.BlockSpec((model, columns), lambda i: (0, 0))]
        + sides[: len(previous)],
        out_specs=[pl.BlockSpec((tile, columns), lambda i: (i, 0))] + sides,
        out_shape=[jax.ShapeDtypeStruct((rows, columns), jnp.bfloat16)]
        + [jax.ShapeDtypeStruct((rows // 2, model), jnp.bfloat16)] * 4,
        compiler_params=pltpu.CompilerParams(vmem_limit_bytes=VMEM_LIMIT),
        cost_estimate=pl.CostEstimate(
            flops=4 * rows * model * columns,
            bytes_accessed=2 * (rows * columns + 4 * rows * model + model * columns),
            transcendentals=rows * columns // 3,
        ),
    )(normed, gradient, weights, *previous)


def ff_grads_kernel(size, normed_ref, gradient_ref, acts_ref, *outs):
    gate_up = multiply(normed_ref[...], acts_ref[:, : 2 * size], TN).astype(jnp.bfloat16)
    down = multiply(gradient_ref[...], acts_ref[:, 2 * size :], TN).astype(jnp.bfloat16)
    if len(outs) == 2:
        outs[0][...] = gate_up
        outs[1][...] = down
    else:
        outs[0][:, : 2 * size] = gate_up
        outs[0][:, 2 * size :] = down


def ff_grads(normed, gradient, acts, split, tile=384):
    rows, model = normed.shape
    columns = acts.shape[1]
    widths = (columns // 3 * 2, columns // 3) if split else (columns,)
    column = pl.BlockSpec((rows, tile), lambda i: (0, i))
    return pl.pallas_call(
        functools.partial(ff_grads_kernel, columns // 3),
        grid=(model // tile,),
        in_specs=[column, column, pl.BlockSpec((rows, columns), lambda i: (0, 0))],
        out_specs=[pl.BlockSpec((tile, width), lambda i: (i, 0)) for width in widths],
        out_shape=[jax.ShapeDtypeStruct((model, width), jnp.bfloat16) for width in widths],
        compiler_params=pltpu.CompilerParams(vmem_limit_bytes=VMEM_LIMIT),
        cost_estimate=pl.CostEstimate(
            flops=2 * rows * model * columns,
            bytes_accessed=2 * (rows * columns + 2 * rows * model + model * columns),
            transcendentals=0,
        ),
    )(normed, gradient, acts)


def rotate_lanes(value):
    half = HD // 2
    rolled = pltpu.roll(value, half, 1)
    lane = lax.broadcasted_iota(jnp.int32, value.shape, 1)
    return jnp.where(lane < half, -rolled, rolled)


def set_mask(mask_ref, code_ref, pos_ref, seg_all_ref, pos_all_ref):
    allowed = (jnp.right_shift(code_ref[...], seg_all_ref[...]) & 1 == 1) & (
        pos_all_ref[...] <= pos_ref[...]
    )
    mask_ref[...] = jnp.where(allowed, 0.0, NEG)


def attend_kernel(
    query_ref,
    key_ref,
    value_ref,
    code_ref,
    pos_ref,
    seg_all_ref,
    pos_all_ref,
    mixed_ref,
    logsum_ref,
    mask_ref,
    value_t_ref,
):
    head = pl.program_id(1)

    @pl.when(head == 0)
    def _():
        set_mask(mask_ref, code_ref, pos_ref, seg_all_ref, pos_all_ref)
        value_t_ref[...] = value_ref[...].T

    scores = multiply(key_ref[...], query_ref[0], NT) * (HD ** (-0.5)) + mask_ref[...]
    top = jnp.max(scores, axis=0, keepdims=True)
    expo = jnp.exp(scores - top)
    total = jnp.sum(expo, axis=0, keepdims=True)
    mixed = multiply(value_t_ref[...], expo.astype(jnp.bfloat16), NN) * (1.0 / total)
    mixed_ref[...] = mixed.T.astype(jnp.bfloat16)
    logsum_ref[pl.ds(head, 1), :] = top + jnp.log(total)


def attention_specs(tile, total):
    query = pl.BlockSpec((1, tile, HD), lambda i, h: (h // 2, i, h % 2))
    block = pl.BlockSpec((tile, HD), lambda i, h: (i, h))
    key = pl.BlockSpec((total, HD), lambda i, h: (0, 0))
    value = pl.BlockSpec((total, HD), lambda i, h: (0, 1))
    line = pl.BlockSpec((1, tile), lambda i, h: (0, i))
    whole = pl.BlockSpec((total, 1), lambda i, h: (0, 0))
    logsum = pl.BlockSpec((8, tile), lambda i, h: (0, i))
    return query, block, key, value, line, whole, logsum


def attend(queries, pairs, code, pos, seg_all, pos_all, heads):
    rows = queries.shape[1]
    total = pairs.shape[0]
    tile = min(rows, 512)
    query, block, key, value, line, whole, logsum = attention_specs(tile, total)
    return pl.pallas_call(
        attend_kernel,
        grid=(rows // tile, heads),
        in_specs=[query, key, value, line, line, whole, whole],
        out_specs=[block, logsum],
        out_shape=[
            jax.ShapeDtypeStruct((rows, heads * HD), jnp.bfloat16),
            jax.ShapeDtypeStruct((8, rows), jnp.float32),
        ],
        scratch_shapes=[
            pltpu.VMEM((total, tile), jnp.float32),
            pltpu.VMEM((HD, total), jnp.bfloat16),
        ],
        compiler_params=pltpu.CompilerParams(vmem_limit_bytes=VMEM_LIMIT),
        cost_estimate=pl.CostEstimate(
            flops=8 * rows * total * HD * heads,
            bytes_accessed=rows * heads * HD * 6,
            transcendentals=rows * total * heads,
        ),
    )(queries, pairs, pairs, code, pos, seg_all, pos_all)


def attend_back_kernel(
    query_ref,
    grad_ref,
    cosine_ref,
    sine_ref,
    key_ref,
    value_ref,
    code_ref,
    pos_ref,
    seg_all_ref,
    pos_all_ref,
    logsum_ref,
    grad_query_ref,
    grad_pairs_ref,
    mask_ref,
    key_t_ref,
):
    head = pl.program_id(1)

    @pl.when(head == 0)
    def _():
        set_mask(mask_ref, code_ref, pos_ref, seg_all_ref, pos_all_ref)
        key_t_ref[...] = key_ref[...].T

    @pl.when((head == 0) & (pl.program_id(0) == 0))
    def _():
        grad_pairs_ref[...] = jnp.zeros_like(grad_pairs_ref)

    scale = HD ** (-0.5)
    query = query_ref[0]
    grad = grad_ref[...]
    scores = multiply(key_ref[...], query, NT) * scale + mask_ref[...]
    probs = jnp.exp(scores - logsum_ref[pl.ds(head, 1), :])
    grad_p = multiply(value_ref[...], grad, NT)
    delta = jnp.sum(probs * grad_p, axis=0, keepdims=True)
    grad_s = (probs * (grad_p - delta) * scale).astype(jnp.bfloat16)
    grad_query = multiply(key_t_ref[...], grad_s, NN).T
    grad_pairs_ref[:, :HD] += multiply(grad_s, query, NN)
    grad_pairs_ref[:, HD:] += multiply(probs.astype(jnp.bfloat16), grad, NN)
    grad_query_ref[0] = (
        grad_query * cosine_ref[...] - rotate_lanes(grad_query * sine_ref[...])
    ).astype(jnp.bfloat16)


def attend_back(queries, grad, cosine, sine, pairs, code, pos, seg_all, pos_all, logsum, heads):
    rows = queries.shape[1]
    total = pairs.shape[0]
    tile = min(rows, 512)
    query, block, key, value, line, whole, sums = attention_specs(tile, total)
    table = pl.BlockSpec((tile, HD), lambda i, h: (i, 0))
    return pl.pallas_call(
        attend_back_kernel,
        grid=(rows // tile, heads),
        in_specs=[query, block, table, table, key, value, line, line, whole, whole, sums],
        out_specs=[query, pl.BlockSpec((total, 2 * HD), lambda i, h: (0, 0))],
        out_shape=[
            jax.ShapeDtypeStruct((heads // 2, rows, 2 * HD), jnp.bfloat16),
            jax.ShapeDtypeStruct((total, 2 * HD), jnp.float32),
        ],
        scratch_shapes=[
            pltpu.VMEM((total, tile), jnp.float32),
            pltpu.VMEM((HD, total), jnp.bfloat16),
        ],
        compiler_params=pltpu.CompilerParams(vmem_limit_bytes=VMEM_LIMIT),
        cost_estimate=pl.CostEstimate(
            flops=20 * rows * total * HD * heads,
            bytes_accessed=rows * heads * HD * 6,
            transcendentals=rows * total * heads,
        ),
    )(queries, grad, cosine, sine, pairs, pairs, code, pos, seg_all, pos_all, logsum)


def shard_gather_small(piece):
    size = lax.axis_size("shard")
    me = lax.axis_index("shard")
    if size > 4:
        return lax.all_gather(piece, "shard", axis=0, tiled=False)
    parts = [piece] + [
        lax.ppermute(piece, "shard", [(i, (i + k) % size) for i in range(size)])
        for k in range(1, size)
    ]
    whole = jnp.zeros((size,) + piece.shape, piece.dtype)
    for k, part in enumerate(parts):
        whole = lax.dynamic_update_slice(whole, part[None], (lax.rem(me - k + size, size), 0, 0))
    return whole


def body(
    tokens,
    cotangent,
    norm1_gain,
    w_query,
    b_query,
    w_key,
    b_key,
    w_value,
    b_value,
    w_out,
    norm2_gain,
    w_gate,
    w_up,
    w_down,
    parents,
    segment_ids,
    positions,
):
    narrow_dtype = jnp.bfloat16
    rows = tokens.shape[1]
    half = rows // 2
    depth = w_query.shape[0]
    model = tokens.shape[2]
    qwp = w_query.shape[1]
    kwp = w_key.shape[1]
    head_loc = qwp // HD
    ffp = w_gate.shape[1]
    shards = lax.axis_size("shard")
    contexts = lax.axis_size("ctx")
    context = lax.axis_index("ctx")
    core = lax.axis_index("tp")
    inner = qwp + 2 * kwp
    quarter = inner // contexts
    distances = [jnp.bitwise_xor(context, k) for k in range(contexts)]
    bar = lax.optimization_barrier

    def core_half(value):
        return lax.dynamic_slice_in_dim(value, core * half, half)

    def core_order(mine, other):
        low = jnp.where(core == 0, mine, other)
        high = jnp.where(core == 0, other, mine)
        return jnp.concatenate([low, high], axis=0)

    def core_join(value):
        return core_order(value, swap(value, "tp", 1))

    def core_reduce(value):
        mine = lax.dynamic_slice_in_dim(value, core * half, half)
        other = lax.dynamic_slice_in_dim(value, (1 - core) * half, half)
        return mine.astype(jnp.float32) + swap(other.astype(narrow_dtype), "tp", 1).astype(
            jnp.float32
        )

    def tree_gather(value):
        mine = jnp.concatenate(sum(context_gather(value), []), axis=0)
        return jnp.concatenate([mine, swap(mine, "tp", 1)], axis=0)

    def tree_terms(mine, other):
        mine = mine.astype(jnp.float32) + other.astype(jnp.float32)
        return [mine[k * half : (k + 1) * half] for k in range(contexts)]

    def tree_block(value, k):
        count = value.shape[0] // 2
        return core_order(
            value[k * half : (k + 1) * half], value[count + k * half : count + (k + 1) * half]
        )

    def tree_line(line):
        return jnp.concatenate(
            [
                lax.dynamic_slice_in_dim(line, d * rows + side * half, half)
                for side in (core, 1 - core)
                for d in distances
            ]
        )

    first_gain = norm1_gain.astype(jnp.float32)
    second_gain = norm2_gain.astype(jnp.float32)
    source_half = core_half(tokens[0]).astype(jnp.float32)
    first_root_mean = lax.rsqrt(jnp.mean(source_half * source_half, axis=-1, keepdims=True) + EPS)
    first_normalized = source_half * first_root_mean
    first_normed = tree_gather((first_normalized * first_gain).astype(narrow_dtype))

    joined = jnp.concatenate([w_query, w_key, w_value], axis=1)
    quarter_own = lax.dynamic_slice_in_dim(joined, context * quarter, quarter, axis=1)
    columns_all = shard_gather_small(
        jnp.concatenate([quarter_own, joined[:, qwp:]], axis=1)
    ).reshape(model, quarter + 2 * kwp)

    pos_all = tree_line(positions[0])
    cosine_all, sine_all = rope_tables(pos_all)
    first_normed, w_out, parent_line, segment_line, w_gate_late, w_up_late, w_down_late = bar(
        (first_normed, w_out, parents[0], segment_ids[0], w_gate, w_up, w_down)
    )
    seg_all = tree_line(segment_line)
    first_row = context * rows
    seg_own = lax.dynamic_slice_in_dim(segment_line, first_row, rows)
    pos_own = lax.dynamic_slice_in_dim(positions[0], first_row, rows)
    labels = jnp.arange(parents.shape[1], dtype=jnp.int32)

    def parent_of(segment):
        return jnp.sum(jnp.where(segment[:, None] == labels[None], parent_line[None], 0), axis=1)

    above = parent_of(labels)
    code_line = 1 << labels | 1 << above | 1 << parent_of(above)
    code_own = jnp.sum(jnp.where(seg_own[:, None] == labels[None], code_line[None], 0), axis=1)
    mask_lines = (code_own[None], pos_own[None], seg_all[:, None], pos_all[:, None])
    cosine, sine = rope_tables(pos_own)

    lin = jnp.dot(first_normed, columns_all, preferred_element_type=jnp.float32)
    biases = jnp.concatenate([b_query, b_key, b_value]).astype(jnp.float32)

    def turned(value, bias):
        value = (value + bias).reshape(value.shape[0], -1, HD)
        return rope(value, cosine_all, sine_all).reshape(value.shape[0], -1)

    queries_all = turned(
        lin[:, :quarter], lax.dynamic_slice_in_dim(biases, context * quarter, quarter)
    ).astype(narrow_dtype)
    pairs = jnp.concatenate(
        [
            turned(lin[:, quarter : quarter + kwp], biases[qwp : qwp + kwp]),
            lin[:, quarter + kwp :] + biases[qwp + kwp :],
        ],
        axis=1,
    ).astype(narrow_dtype)
    queries = jnp.zeros((contexts, rows, quarter), narrow_dtype)
    exchanged = context_send([tree_block(queries_all, k) for k in range(contexts)])
    for k, block in enumerate(exchanged):
        queries = lax.dynamic_update_slice(queries, block[None], (distances[k], 0, 0))

    part = depth // contexts
    wo_piece = lax.dynamic_slice_in_dim(w_out, context * part, part)
    wo_all = jnp.zeros((shards, contexts, part, qwp), narrow_dtype)
    for k, block in enumerate(context_gather(shard_gather_small(wo_piece))):
        block = jnp.concatenate(block, axis=0)
        wo_all = lax.dynamic_update_slice(wo_all, block[:, None], (0, distances[k], 0, 0))
    wo_all = wo_all.reshape(model, qwp)

    width = -(-ffp // (contexts * 128)) * 128
    first_width = width // 192 * 128
    spans = [(0, first_width), (first_width, width - first_width)]
    padding = ((0, 0), (0, width * contexts - ffp))
    ff_weights = []
    for (offset, size), group in zip(
        spans, ((w_gate, w_up, w_down), (w_gate_late, w_up_late, w_down_late))
    ):
        piece = jnp.concatenate(
            [
                lax.dynamic_slice_in_dim(
                    jnp.pad(w, padding), context * width + offset, size, axis=1
                )
                for w in group
            ],
            axis=1,
        )
        ff_weights.append(lax.all_gather(piece, "shard", axis=0, tiled=True))

    queries, cotangent_late = bar((queries, cotangent))
    gradient_half = core_half(cotangent_late[0])
    tree_gradient = tree_gather(gradient_half)
    mixed_b, logsum = attend(queries, pairs, *mask_lines, head_loc)


    residual = source_half + core_reduce(contract_last(mixed_b, wo_all))
    second_root_mean = lax.rsqrt(jnp.mean(residual * residual, axis=-1, keepdims=True) + EPS)
    second_normalized = residual * second_root_mean
    second_normed = (second_normalized * second_gain).astype(narrow_dtype)
    tree_normed = tree_gather(second_normed)
    tree_normed, quarter_late = bar((tree_normed, columns_all[:, :quarter]))
    quarter_blocks = context_send([quarter_late] * contexts)

    acts, *sums = feed_forward(tree_normed, tree_gradient, ff_weights[0])
    (grads,) = ff_grads(tree_normed, tree_gradient, acts, False)
    grads, late_weights = bar((grads, ff_weights[1]))
    late_acts, *sums = feed_forward(
        tree_normed, tree_gradient, late_weights, tuple(sums)
    )
    (late_grads,) = ff_grads(tree_normed, tree_gradient, late_acts, False)

    def over_shard(value):
        return lax.psum_scatter(
            value.reshape(shards, depth, value.shape[1]), "shard", scatter_dimension=0, tiled=False
        )

    ff_sums = [over_shard(grads)]

    mlp_mine, mlp_other, back_mine, back_other = sums
    back_mine, back_other, late_grads = bar((back_mine, swap(back_other, "tp", 1), late_grads))
    second_normed_gradient = context_sum(tree_terms(back_mine, back_other))
    second_normed_gradient, mlp_mine, mlp_other = bar(
        (second_normed_gradient, mlp_mine, mlp_other)
    )
    mlp = context_sum(tree_terms(mlp_mine, swap(mlp_other, "tp", 1)))
    residual_gradient = gradient_half.astype(jnp.float32) + norm_backward(
        second_normed_gradient, second_normalized, second_root_mean, second_gain
    )
    grad_attn_b = core_join(residual_gradient.astype(narrow_dtype))
    grad_mixed = jnp.dot(grad_attn_b, wo_all, preferred_element_type=jnp.float32).astype(
        narrow_dtype
    )

    groups = qwp // quarter
    grad_wo = contract_first(grad_attn_b, mixed_b).astype(narrow_dtype)
    grad_wo = grad_wo.reshape(shards, contexts, part, qwp)
    grad_wo = [lax.dynamic_index_in_dim(grad_wo, d, axis=1, keepdims=False) for d in distances]
    grad_wo = context_sum(grad_wo).astype(narrow_dtype)
    grad_query, grad_pairs = attend_back(
        queries, grad_mixed, cosine, sine, pairs, *mask_lines, logsum, head_loc
    )
    grad_query, grad_pairs, ff_sums[0], late_grads = bar(
        (grad_query, grad_pairs, ff_sums[0], late_grads)
    )
    ff_sums.append(over_shard(late_grads))
    early_near = context_gather_start(ff_sums[0])
    grad_pairs = context_sum([tree_block(grad_pairs, k) for k in range(contexts)])
    grad_keys = rope_back(grad_pairs[:, :kwp].reshape(rows, -1, HD), cosine, sine)
    grad_pairs = jnp.concatenate(
        [grad_keys.reshape(rows, kwp), grad_pairs[:, kwp:]], axis=1
    ).astype(narrow_dtype)
    grad_quarters = jnp.concatenate([grad_query, grad_pairs[None]], axis=0)
    relative_grads = [
        lax.dynamic_index_in_dim(grad_quarters, d, axis=0, keepdims=False) for d in distances
    ]
    exchanged = context_send(relative_grads)
    exchanged, early_near, grad_wo, ff_sums[1] = bar(
        (exchanged, early_near, grad_wo, ff_sums[1])
    )
    early_blocks = context_gather_end(ff_sums[0], *early_near)
    late_near = context_gather_start(ff_sums[1])
    normed_gradient = sum(
        contract_last(grads, block) for grads, block in zip(relative_grads, quarter_blocks)
    )
    first_normed_gradient = core_reduce(normed_gradient)
    source_gradient = (
        residual_gradient
        + norm_backward(first_normed_gradient, first_normalized, first_root_mean, first_gain)
    ).astype(narrow_dtype)
    source_gradient = core_join(source_gradient)
    small = jnp.concatenate(
        [
            jnp.sum(first_normed_gradient * first_normalized, axis=0),
            jnp.sum(second_normed_gradient * second_normalized, axis=0),
        ]
    )
    small = small + swap(small, "tp", 1)
    small = jnp.concatenate([small, jnp.sum(grad_quarters.astype(jnp.float32), axis=1).reshape(-1)])

    exchanged = jnp.concatenate(
        [
            lax.dynamic_slice_in_dim(block, side * half, half)
            for side in (core, 1 - core)
            for block in exchanged
        ],
        axis=0,
    )
    grad_columns = contract_first(first_normed, exchanged).astype(narrow_dtype)

    def packed(value):
        value = value.reshape(-1, quarter)
        high = value.astype(narrow_dtype)
        return high, (value - high.astype(jnp.float32)).astype(narrow_dtype)

    def unpacked(value):
        count = value.shape[-2] // 2
        value = value.astype(jnp.float32)
        return value[..., :count, :] + value[..., count:, :]

    me = lax.axis_index("shard")
    terms = jnp.concatenate(
        [grad_columns.reshape(shards, depth, quarter)]
        + [grad_wo[:, :, g * quarter : (g + 1) * quarter] for g in range(groups)]
        + [jnp.broadcast_to(half_value, (shards,) + half_value.shape) for half_value in packed(small)],
        axis=1,
    )
    if shards > 4:
        received = [lax.all_to_all(terms, "shard", 0, 0)[k] for k in range(shards)]
    else:
        received = [lax.dynamic_index_in_dim(terms, me, axis=0, keepdims=False)]
        for k in range(1, shards):
            received.append(
                lax.ppermute(
                    lax.dynamic_index_in_dim(terms, lax.rem(me + k, shards), keepdims=False),
                    "shard",
                    [(i, (i + k) % shards) for i in range(shards)],
                )
            )
    received, early_blocks, late_near, mlp = bar((received, early_blocks, late_near, mlp))
    output = core_join((residual + mlp).astype(narrow_dtype))
    late_blocks = context_gather_end(ff_sums[1], *late_near)
    count = depth + groups * part
    weight_sums = sum(value[:count].astype(jnp.float32) for value in received).astype(narrow_dtype)
    small = sum(unpacked(value[count:]) for value in received)
    blocks = context_send([jnp.concatenate([weight_sums, *packed(small)], axis=0)] * contexts)
    small = sum(unpacked(block[count:]) for block in blocks).reshape(-1)
    column_blocks = [block[:depth] for block in blocks]
    row_blocks = [
        jnp.concatenate(
            [block[depth + g * part : depth + (g + 1) * part] for g in range(groups)], axis=1
        )
        for block in blocks
    ]
    grad_wq, grad_wk, grad_wv, grad_wo = place_attention(
        column_blocks, row_blocks, qwp, kwp, context
    )

    early_blocks, late_blocks, output, source_gradient, small, grad_wq = bar(
        (early_blocks, late_blocks, output, source_gradient, small, grad_wq)
    )
    plan = [
        (k, offset, size, (0, 1, 2)) for offset, size in spans for k in range(contexts)
    ]
    grad_wg, grad_wu, grad_wd = spread(
        [jnp.concatenate(block, axis=0) for block in early_blocks + late_blocks], tuple(plan), width, ffp, context
    )

    edges = [0, model, 2 * model, 2 * model + qwp, 2 * model + qwp + kwp, small.shape[0]]
    sums = [small[edges[i] : edges[i + 1]] for i in range(5)]
    return (
        output[None],
        source_gradient[None],
        sums[0],
        grad_wq,
        sums[2],
        grad_wk,
        sums[3],
        grad_wv,
        sums[4],
        grad_wo,
        sums[1],
        grad_wg,
        grad_wu,
        grad_wd,
    )


def solution(mesh):
    return jax.shard_map(
        body,
        mesh=mesh,
        in_specs=(
            P("shard", "ctx", None),
            P("shard", "ctx", None),
            P(),
            P("shard", "tp"),
            P("tp"),
            P("shard", "tp"),
            P("tp"),
            P("shard", "tp"),
            P("tp"),
            P("shard", "tp"),
            P(),
            P("shard", "tp"),
            P("shard", "tp"),
            P("shard", "tp"),
            P("shard", None),
            P("shard", None),
            P("shard", None),
        ),
        out_specs=(
            P("shard", "ctx", None),
            P("shard", "ctx", None),
            P(),
            P("shard", "tp"),
            P("tp"),
            P("shard", "tp"),
            P("tp"),
            P("shard", "tp"),
            P("tp"),
            P("shard", "tp"),
            P(),
            P("shard", "tp"),
            P("shard", "tp"),
            P("shard", "tp"),
        ),
        check_vma=False,
    )
```

time: 956 us -> 640 us (0.67)
  matrix products: 242 us -> 22.5 us
  Pallas kernels: 10.5 us -> 160 us
  blocking collectives: 126 us -> 0 us
  local copies, waits for them, and re-layouts: 139 us -> 81.9 us
  other arithmetic: 113 us -> 62.9 us
  starting transfers between devices: 102 us -> 75.5 us
  waiting for transfers between devices: 196 us -> 216 us
    pallas_call x0 -> x7, Pallas kernels: none -> 150 us  [the longest x2 69.3 us: feed_forward(): pl.pallas_call(functools.partial(ff_kernel, columns // 3, not previous),...]
    ppermute x58 -> x59, waiting for transfers between devices: 104 us -> 209 us  [swap(): return lax.ppermute(value, axis, [(i, i ^ distance) for i in range(size)])]
    dot_general x26 -> x5, matrix products: 102 us -> 8.65 us  [contract_last(): lax.dot_general(left, right, (((1,), (1,)), ((), ())), preferred_element_...]
    psum x1 -> x0, blocking collectives: 88.6 us -> none  [body(): lax.psum(jnp.concatenate([gain_sums.reshape(-1), bias_sums]), ('shard', '...]
    dot_general x17 -> x1, matrix products: 70.8 us -> 5.47 us  [body(): lin = jnp.dot(first_normed, columns_all, preferred_element_type=jnp.float32)]
    dot_general x20 -> x2, matrix products: 64.8 us -> 6.11 us  [contract_first(): lax.dot_general(left, right, (((0,), (0,)), ((), ())), preferred_element_...]
    ppermute x18 -> x9, waiting for transfers between devices: 59.8 us -> 6.65 us  [the longest x3 6.64 us: body(): lax.ppermute(lax.dynamic_index_in_dim(terms, lax.rem(me + k, shards), kee...]
    convert_element_type x32 -> x15, other arithmetic: 48.7 us -> 5.65 us  [the longest x1 2.09 us: body(): source_gradient = (residual_gradient + norm_backward(first_normed_gradien...]
  transfers between devices with their start and end apart: 78 -> 72, of which waited for: 29 -> 27; matrix products, arithmetic and copies ran while one was open for 50% -> 23% of each run, Pallas kernels for 1% -> 24%
where the time goes in v2:
time: 640 us; the launch traced here: 635 us
  waiting for transfers between devices  216 us (34%)
  Pallas kernels  160 us (25%)
  local copies, waits for them, and re-layouts  81.9 us (13%)
  starting transfers between devices  75.5 us (12%)
  other arithmetic  62.9 us (10%)
  matrix products  22.5 us (4%)
  between operations  15.8 us (2%)
    ppermute x59, waiting for transfers between devices, swap(): return lax.ppermute(value, axis, [(i, i ^ distance) for i in range(size)])  209 us
    pallas_call x2, Pallas kernels, feed_forward(): pl.pallas_call(functools.partial(ff_kernel, columns // 3, not previous),...  69.3 us
    ppermute x59, starting transfers between devices, swap(): return lax.ppermute(value, axis, [(i, i ^ distance) for i in range(size)])  58.7 us
    pallas_call x2, Pallas kernels, ff_grads(): pl.pallas_call(functools.partial(ff_grads_kernel, columns // 3), grid=(mo...  34.8 us
    unnamed x185, local copies, waits for them, and re-layouts  33.7 us
    pallas_call x1, Pallas kernels, attend_back(): pl.pallas_call(attend_back_kernel, grid=(rows // tile, heads), in_specs=[...  27.1 us
    pallas_call x1, Pallas kernels, attend(): pl.pallas_call(attend_kernel, grid=(rows // tile, heads), in_specs=[query...  16 us
    ppermute x6, starting transfers between devices, shard_gather_small(): lax.ppermute(piece, 'shard', [(i, (i + k) % size) for i in range(size)])  13.1 us
  transfers between devices with their start and end apart: 72, of which 27 were waited for; matrix products, arithmetic and copies ran while one was open for 23% of the time, Pallas kernels for 24%

profile of v2, /device:TPU:0, one launch (start us, length us, event | category | flops | bytes accessed | tf_op | source)
XLA Modules:
  0.0 634.8 jit_solution(13976092467855046198)
XLA Ops:
  53.1 5.3 multiply_cosine_fusion
  64.0 4.5 constant_dynamic-update-slice_fusion.5
  77.8 5.5 fusion.59
  111.1 6.7 %collective-permute-done.9 = bf16[512,256]{1,0:T(8,128)(2,1)S(1)} collective-permute-done((bf16[512,256]{1,0:T(8,128)(2,1)}, bf16[512,256]{1,0:T(8,128)(2,1)S(1)}, u32[]{:S(2)}, u32[]{:S(2)}) %collective-permute-start.9) | collective-permute-done | bytes 262176 | tf_op jit(solution)/shard_map/ppermute | solution.py:73
  121.5 16.0 %shard_map.272 = (bf16[512,768]{1,0:T(8,128)(2,1)}, f32[8,512]{1,0:T(8,128)}) custom-call(bf16[4,512,256]{2,1,0:T(8,128)(2,1)} %copy-done.33, bf16[2048,256]{1,0:T(8,128)(2,1)} %pad_maximum_fusion.7.key_ref.value_ref, bf16[2048,256]{1,0:T(8,128)(2,1)} %pad_maximum_fusion.7.key_ref.value_ref, s32[1,512]{1,0:T(1,128)} %bitcast.195, ...), custom_call_target="tpu_custom_call" | custom-call | flops 6442450944 | bytes 2359296 | tf_op jit(solution)/shard_map/pallas_call | solution.py:329
  139.4 8.1 %collective-permute-done.17 = bf16[2,96,768]{2,1,0:T(8,128)(2,1)S(1)} collective-permute-done((bf16[2,96,768]{2,1,0:T(8,128)(2,1)S(1)}, bf16[2,96,768]{2,1,0:T(8,128)(2,1)S(1)}, u32[]{:S(2)}, u32[]{:S(2)}) %collective-permute-start.17) | collective-permute-done | bytes 294944 | tf_op jit(solution)/shard_map/ppermute | solution.py:73
  147.4 4.4 collective-permute-done.16
  161.7 5.6 collective-permute-done.26
  169.0 14.4 %collective-permute-done.20 = bf16[256,1536]{1,0:T(8,128)(2,1)S(1)} collective-permute-done((bf16[256,1536]{1,0:T(8,128)(2,1)S(1)}, bf16[256,1536]{1,0:T(8,128)(2,1)S(1)}, u32[]{:S(2)}, u32[]{:S(2)}) %collective-permute-start.20) | collective-permute-done | bytes 786464 | tf_op jit(solution)/shard_map/ppermute | solution.py:73
  187.7 6.7 %collective-permute-done.21 = bf16[128,1536]{1,0:T(8,128)(2,1)S(1)} collective-permute-done((bf16[128,1536]{1,0:T(8,128)(2,1)S(1)}, bf16[128,1536]{1,0:T(8,128)(2,1)S(1)}, u32[]{:S(2)}, u32[]{:S(2)}) %collective-permute-start.21) | collective-permute-done | bytes 393248 | tf_op jit(solution)/shard_map/ppermute | solution.py:73
  208.7 3.9 constant_dynamic-update-slice_fusion.18.normed_ref
  212.7 41.1 %shard_map.273 = (bf16[2048,2304]{1,0:T(8,128)(2,1)}, bf16[1024,1536]{1,0:T(8,128)(2,1)}, bf16[1024,1536]{1,0:T(8,128)(2,1)}, bf16[1024,1536]{1,0:T(8,128)(2,1)}, bf16[1024,1536]{1,0:T(8,128)(2,1)}) custom-call(bf16[2048,1536]{1,0:T(8,128)(2,1)} %constant_dynamic-update-slice_fusion.18.normed_ref, ...), custom_call_target="tpu_custom_call" | custom-call | flops 28991029248 | bytes 41680896 | tf_op jit(solution)/shard_map/pallas_call | solution.py:222
  253.8 21.4 %shard_map.274 = bf16[1536,2304]{1,0:T(8,128)(2,1)} custom-call(bf16[2048,1536]{1,0:T(8,128)(2,1)} %constant_dynamic-update-slice_fusion.18.normed_ref, bf16[2048,1536]{1,0:T(8,128)(2,1)} %constant_dynamic-update-slice_fusion.29.gradient_ref, bf16[2048,2304]{1,0:T(8,128)(2,1)} %get-tuple-element.100.acts_ref), custom_call_target="tpu_custom_call" | custom-call | flops 14495514624 | bytes 29097984 | tf_op jit(solution)/shard_map/pallas_call | solution.py:255
  275.3 28.2 %shard_map.275 = (bf16[2048,1152]{1,0:T(8,128)(2,1)}, bf16[1024,1536]{1,0:T(8,128)(2,1)}, bf16[1024,1536]{1,0:T(8,128)(2,1)}, bf16[1024,1536]{1,0:T(8,128)(2,1)}, bf16[1024,1536]{1,0:T(8,128)(2,1)}) custom-call(bf16[2048,1536]{1,0:T(8,128)(2,1)} %constant_dynamic-update-slice_fusion.18.normed_ref, ...), custom_call_target="tpu_custom_call" | custom-call | flops 14495514624 | bytes 33423360 | tf_op jit(solution)/shard_map/pallas_call | solution.py:222
  304.0 13.4 %shard_map.276 = bf16[1536,1152]{1,0:T(8,128)(2,1)} custom-call(bf16[2048,1536]{1,0:T(8,128)(2,1)} %constant_dynamic-update-slice_fusion.18.normed_ref, bf16[2048,1536]{1,0:T(8,128)(2,1)} %constant_dynamic-update-slice_fusion.29.gradient_ref, bf16[2048,1152]{1,0:T(8,128)(2,1)} %get-tuple-element.111.acts_ref), custom_call_target="tpu_custom_call" | custom-call | flops 7247757312 | bytes 20840448 | tf_op jit(solution)/shard_map/pallas_call | solution.py:255
  324.2 16.9 %collective-permute-done.30 = bf16[256,1536]{1,0:T(8,128)(2,1)S(1)} collective-permute-done((bf16[256,1536]{1,0:T(8,128)(2,1)S(1)}, bf16[256,1536]{1,0:T(8,128)(2,1)S(1)}, u32[]{:S(2)}, u32[]{:S(2)}) %collective-permute-start.30) | collective-permute-done | bytes 786464 | tf_op jit(solution)/shard_map/ppermute | solution.py:73
  341.2 17.0 %collective-permute-done.32 = bf16[256,1536]{1,0:T(8,128)(2,1)S(1)} collective-permute-done((bf16[256,1536]{1,0:T(8,128)(2,1)S(1)}, bf16[256,1536]{1,0:T(8,128)(2,1)S(1)}, u32[]{:S(2)}, u32[]{:S(2)}) %collective-permute-start.32) | collective-permute-done | bytes 786464 | tf_op jit(solution)/shard_map/ppermute | solution.py:73
  370.2 27.1 %shard_map.277 = (bf16[3,512,256]{2,1,0:T(8,128)(2,1)}, f32[2048,256]{1,0:T(8,128)}) custom-call(bf16[4,512,256]{2,1,0:T(8,128)(2,1)} %copy-done.33, bf16[512,768]{1,0:T(8,128)(2,1)} %convolution_convert_fusion.2.grad_ref, f32[512,128]{1,0:T(8,128)} %get-tuple-element.305.cosine_ref, f32[512,128]{1,0:T(8,128)} %get-tuple-element.306.sine_ref, ...), custom_call_target="tpu_custom_call" | custom-call | flops 16106127360 | bytes 2359296 | tf_op jit(solution)/shard_map/pallas_call | solution.py:401
  403.7 12.5 %collective-permute-done.42 = bf16[4,96,768]{2,1,0:T(8,128)(2,1)S(1)} collective-permute-done((bf16[4,96,768]{2,1,0:T(8,128)(2,1)S(1)}, bf16[4,96,768]{2,1,0:T(8,128)(2,1)S(1)}, u32[]{:S(2)}, u32[]{:S(2)}) %collective-permute-start.42) | collective-permute-done | bytes 589856 | tf_op jit(solution)/shard_map/ppermute | solution.py:73
  416.9 11.1 %collective-permute-done.44 = bf16[4,96,768]{2,1,0:T(8,128)(2,1)S(1)} collective-permute-done((bf16[4,96,768]{2,1,0:T(8,128)(2,1)S(1)}, bf16[4,96,768]{2,1,0:T(8,128)(2,1)S(1)}, u32[]{:S(2)}, u32[]{:S(2)}) %collective-permute-start.44) | collective-permute-done | bytes 589856 | tf_op jit(solution)/shard_map/ppermute | solution.py:73
  429.4 4.9 collective-permute-done.43
  448.2 13.0 %collective-permute-done.45 = bf16[1536,256]{1,0:T(8,128)(2,1)S(1)} collective-permute-done((bf16[1536,256]{1,0:T(8,128)(2,1)}, bf16[1536,256]{1,0:T(8,128)(2,1)S(1)}, u32[]{:S(2)}, u32[]{:S(2)}) %collective-permute-start.45) | collective-permute-done | bytes 786464 | tf_op jit(solution)/shard_map/ppermute | solution.py:73
  467.0 3.9 fusion.46
  481.0 24.8 %collective-permute-done.39 = bf16[512,256]{1,0:T(8,128)(2,1)} collective-permute-done((bf16[512,256]{1,0:T(8,128)(2,1)}, bf16[512,256]{1,0:T(8,128)(2,1)}, u32[]{:S(2)}, u32[]{:S(2)}) %collective-permute-start.39) | collective-permute-done | bytes 262176 | tf_op jit(solution)/shard_map/ppermute | solution.py:73
  519.3 4.7 convolution_convert_fusion.1
  528.6 16.5 %collective-permute-done.60 = bf16[256,1536]{1,0:T(8,128)(2,1)} collective-permute-done((bf16[256,1536]{1,0:T(8,128)(2,1)}, bf16[256,1536]{1,0:T(8,128)(2,1)}, u32[]{:S(2)}, u32[]{:S(2)}) %collective-permute-start.60) | collective-permute-done | bytes 786464 | tf_op jit(solution)/shard_map/ppermute | solution.py:73
  551.9 6.6 %collective-permute-done.50 = bf16[704,256]{1,0:T(8,128)(2,1)S(1)} collective-permute-done((bf16[704,256]{1,0:T(8,128)(2,1)S(1)}, bf16[704,256]{1,0:T(8,128)(2,1)S(1)}, u32[]{:S(2)}, u32[]{:S(2)}) %collective-permute-start.50) | collective-permute-done | bytes 360480 | tf_op jit(solution)/shard_map/ppermute | solution.py:721
  558.5 4.6 collective-permute-done.54
  563.1 4.6 collective-permute-done.53
  567.7 14.3 %collective-permute-done.56.refs_6_ = bf16[384,1152]{1,0:T(8,128)(2,1)S(1)} collective-permute-done((bf16[384,1152]{1,0:T(8,128)(2,1)S(1)}, bf16[384,1152]{1,0:T(8,128)(2,1)S(1)}, u32[]{:S(2)}, u32[]{:S(2)}) %collective-permute-start.56) | collective-permute-done | bytes 884768 | tf_op jit(solution)/shard_map/ppermute | solution.py:73
  595.4 4.1 collective-permute-done.66
  618.1 9.9 %shard_map.279 = (f32[384,4480]{1,0:T(8,128)}, f32[384,4480]{1,0:T(8,128)}, f32[384,4480]{1,0:T(8,128)}) custom-call(s32[1]{0:T(128)} %bitcast.64.context_ref, bf16[384,2304]{1,0:T(8,128)(2,1)} %bitcast.42.refs_0_, bf16[384,2304]{1,0:T(8,128)(2,1)S(1)} %collective-permute-done.40.refs_1_, bf16[384,2304]{1,0:T(8,128)(2,1)S(1)} %collective-permute-done.41.refs_2_, ...), custom_call_target="tpu_custom_call" | custom-call | tf_op jit(solution)/shard_map/pallas_call | solution.py:125
  (478 shorter events, 237.1 us)
Async XLA Ops:
  7.2 205.5 %all-gather.3.cloned.1.call-start = ((), (), s32[]{:S(2)}) async-start(), calls=%async_computation.2 | async-start | bytes 8847360 | tf_op jit(solution)/shard_map/all_gather | solution.py:596
  20.5 41.3 %collective-permute-start.6 = (bf16[384,512]{1,0:T(8,128)(2,1)}, bf16[384,512]{1,0:T(8,128)(2,1)}, u32[]{:S(2)}, u32[]{:S(2)}) collective-permute-start(bf16[384,512]{1,0:T(8,128)(2,1)} %pad_maximum_fusion.12), channel_id=1, source_target_pairs={{0,16},{8,24},{16,0},{24,8},{1,17},{9,25},{17,1},{25,9},{2,18},{10... | collective-permute-start | bytes 1179656 | tf_op jit(solution)/shard_map/ppermute | solution.py:429
  23.1 37.6 %collective-permute-start.5 = (bf16[384,512]{1,0:T(8,128)(2,1)}, bf16[384,512]{1,0:T(8,128)(2,1)}, u32[]{:S(2)}, u32[]{:S(2)}) collective-permute-start(bf16[384,512]{1,0:T(8,128)(2,1)} %pad_maximum_fusion.12), channel_id=1, source_target_pairs={{0,8},{8,16},{16,24},{24,0},{1,9},{9,17},{17,25},{25,1},{2,10},{10... | collective-permute-start | bytes 1179656 | tf_op jit(solution)/shard_map/ppermute | solution.py:429
  24.7 38.2 %collective-permute-start.7 = (bf16[384,512]{1,0:T(8,128)(2,1)}, bf16[384,512]{1,0:T(8,128)(2,1)}, u32[]{:S(2)}, u32[]{:S(2)}) collective-permute-start(bf16[384,512]{1,0:T(8,128)(2,1)} %pad_maximum_fusion.12), channel_id=1, source_target_pairs={{0,24},{8,0},{16,8},{24,16},{1,25},{9,1},{17,9},{25,17},{2,26},{10... | collective-permute-start | bytes 1179656 | tf_op jit(solution)/shard_map/ppermute | solution.py:429
  52.7 222.5 %all-gather.5.cloned.1.call-start = ((), (), s32[]{:S(2)}) async-start(), calls=%async_computation.3 | async-start | bytes 4423680 | tf_op jit(solution)/shard_map/all_gather | solution.py:596
  70.2 36.6 %collective-permute-start.12 = (bf16[96,768]{1,0:T(8,128)(2,1)}, bf16[96,768]{1,0:T(8,128)(2,1)}, u32[]{:S(2)}, u32[]{:S(2)}) collective-permute-start(bf16[96,768]{1,0:T(8,128)(2,1)} %get-tuple-element.189), channel_id=1, source_target_pairs={{0,16},{8,24},{16,0},{24,8},{1,17},{9,25},{17,1},{25,9},{2,18},{10... | collective-permute-start | bytes 442376 | tf_op jit(solution)/shard_map/ppermute | solution.py:429
  72.9 31.4 %collective-permute-start.11 = (bf16[96,768]{1,0:T(8,128)(2,1)}, bf16[96,768]{1,0:T(8,128)(2,1)}, u32[]{:S(2)}, u32[]{:S(2)}) collective-permute-start(bf16[96,768]{1,0:T(8,128)(2,1)} %get-tuple-element.189), channel_id=1, source_target_pairs={{0,8},{8,16},{16,24},{24,0},{1,9},{9,17},{17,25},{25,1},{2,10},{10... | collective-permute-start | bytes 442376 | tf_op jit(solution)/shard_map/ppermute | solution.py:429
  74.5 33.3 %collective-permute-start.13 = (bf16[96,768]{1,0:T(8,128)(2,1)}, bf16[96,768]{1,0:T(8,128)(2,1)}, u32[]{:S(2)}, u32[]{:S(2)}) collective-permute-start(bf16[96,768]{1,0:T(8,128)(2,1)} %get-tuple-element.189), channel_id=1, source_target_pairs={{0,24},{8,0},{16,8},{24,16},{1,25},{9,1},{17,9},{25,17},{2,26},{10... | collective-permute-start | bytes 442376 | tf_op jit(solution)/shard_map/ppermute | solution.py:429
  108.7 28.8 %collective-permute-start.15 = (bf16[4,96,768]{2,1,0:T(8,128)(2,1)S(1)}, bf16[4,96,768]{2,1,0:T(8,128)(2,1)S(1)}, u32[]{:S(2)}, u32[]{:S(2)}) collective-permute-start(bf16[4,96,768]{2,1,0:T(8,128)(2,1)S(1)} %bitcast_dynamic-update-slice_fusion.10), channel_id=1, source_target_pairs={{0,4},{2,6},{4,0},{6,2},{1,5},{3,7},{5,1},{7,3},{8,12},{10,14},{12... | collective-permute-start | bytes 1769480 | tf_op jit(solution)/shard_map/ppermute | solution.py:73
  110.3 27.9 %collective-permute-start.14 = (bf16[4,96,768]{2,1,0:T(8,128)(2,1)S(1)}, bf16[4,96,768]{2,1,0:T(8,128)(2,1)S(1)}, u32[]{:S(2)}, u32[]{:S(2)}) collective-permute-start(bf16[4,96,768]{2,1,0:T(8,128)(2,1)S(1)} %bitcast_dynamic-update-slice_fusion.10), channel_id=1, source_target_pairs={{0,2},{2,0},{4,6},{6,4},{1,3},{3,1},{5,7},{7,5},{8,10},{10,8},{12,... | collective-permute-start | bytes 1769480 | tf_op jit(solution)/shard_map/ppermute | solution.py:73
  119.0 34.7 %collective-permute-start.25 = (bf16[256,1536]{1,0:T(8,128)(2,1)S(1)}, bf16[256,1536]{1,0:T(8,128)(2,1)S(1)}, u32[]{:S(2)}, u32[]{:S(2)}) collective-permute-start(bf16[256,1536]{1,0:T(8,128)(2,1)S(1)} %get-tuple-element.183), channel_id=1, source_target_pairs={{0,4},{2,6},{4,0},{6,2},{1,5},{3,7},{5,1},{7,3},{8,12},{10,14},{12... | collective-permute-start | bytes 2359304 | tf_op jit(solution)/shard_map/ppermute | solution.py:73
  120.0 35.2 %collective-permute-start.24 = (bf16[256,1536]{1,0:T(8,128)(2,1)S(1)}, bf16[256,1536]{1,0:T(8,128)(2,1)S(1)}, u32[]{:S(2)}, u32[]{:S(2)}) collective-permute-start(bf16[256,1536]{1,0:T(8,128)(2,1)S(1)} %get-tuple-element.183), channel_id=1, source_target_pairs={{0,2},{2,0},{4,6},{6,4},{1,3},{3,1},{5,7},{7,5},{8,10},{10,8},{12,... | collective-permute-start | bytes 2359304 | tf_op jit(solution)/shard_map/ppermute | solution.py:73
  168.9 36.1 %collective-permute-start.28 = (bf16[1024,1536]{1,0:T(8,128)(2,1)}, bf16[1024,1536]{1,0:T(8,128)(2,1)}, u32[]{:S(2)}, u32[]{:S(2)}) collective-permute-start(bf16[1024,1536]{1,0:T(8,128)(2,1)} %get-tuple-element.257), channel_id=1, source_target_pairs={{0,1},{1,0},{2,3},{3,2},{4,5},{5,4},{6,7},{7,6},{8,9},{9,8},{10,11... | collective-permute-start | bytes 9437192 | tf_op jit(solution)/shard_map/ppermute | solution.py:73
  202.9 194.5 %reduce-scatter.3.cloned.1.call-start = ((), (), s32[]{:S(2)}) async-start(), calls=%async_computation.4 | async-start | bytes 8847360 | tf_op jit(solution)/shard_map/reduce_scatter | solution.py:621
  275.3 236.7 %reduce-scatter.5.cloned.1.call-start = ((), (), s32[]{:S(2)}) async-start(), calls=%async_computation.5 | async-start | bytes 4423680 | tf_op jit(solution)/shard_map/reduce_scatter | solution.py:621
  322.2 35.9 %collective-permute-start.32 = (bf16[256,1536]{1,0:T(8,128)(2,1)S(1)}, bf16[256,1536]{1,0:T(8,128)(2,1)S(1)}, u32[]{:S(2)}, u32[]{:S(2)}) collective-permute-start(bf16[256,1536]{1,0:T(8,128)(2,1)S(1)} %get-tuple-element.202), channel_id=1, source_target_pairs={{0,6},{2,4},{4,2},{6,0},{1,7},{3,5},{5,3},{7,1},{8,14},{10,12},{12... | collective-permute-start | bytes 2359304 | tf_op jit(solution)/shard_map/ppermute | solution.py:73
  323.7 35.8 %collective-permute-start.31 = (bf16[256,1536]{1,0:T(8,128)(2,1)S(1)}, bf16[256,1536]{1,0:T(8,128)(2,1)S(1)}, u32[]{:S(2)}, u32[]{:S(2)}) collective-permute-start(bf16[256,1536]{1,0:T(8,128)(2,1)S(1)} %get-tuple-element.203), channel_id=1, source_target_pairs={{0,4},{2,6},{4,0},{6,2},{1,5},{3,7},{5,1},{7,3},{8,12},{10,14},{12... | collective-permute-start | bytes 2359304 | tf_op jit(solution)/shard_map/ppermute | solution.py:73
  363.7 81.2 %collective-permute-start.47 = (bf16[1536,256]{1,0:T(8,128)(2,1)}, bf16[1536,256]{1,0:T(8,128)(2,1)}, u32[]{:S(2)}, u32[]{:S(2)}) collective-permute-start(bf16[1536,256]{1,0:T(8,128)(2,1)} %slice.436), channel_id=1, source_target_pairs={{0,6},{2,4},{4,2},{6,0},{1,7},{3,5},{5,3},{7,1},{8,14},{10,12},{12... | collective-permute-start | bytes 2359304 | tf_op jit(solution)/shard_map/ppermute | solution.py:73
  365.2 99.4 %collective-permute-start.46 = (bf16[1536,256]{1,0:T(8,128)(2,1)}, bf16[1536,256]{1,0:T(8,128)(2,1)}, u32[]{:S(2)}, u32[]{:S(2)}) collective-permute-start(bf16[1536,256]{1,0:T(8,128)(2,1)} %slice.436), channel_id=1, source_target_pairs={{0,4},{2,6},{4,0},{6,2},{1,5},{3,7},{5,1},{7,3},{8,12},{10,14},{12... | collective-permute-start | bytes 2359304 | tf_op jit(solution)/shard_map/ppermute | solution.py:73
  400.7 27.3 %collective-permute-start.44 = (bf16[4,96,768]{2,1,0:T(8,128)(2,1)S(1)}, bf16[4,96,768]{2,1,0:T(8,128)(2,1)S(1)}, u32[]{:S(2)}, u32[]{:S(2)}) collective-permute-start(bf16[4,96,768]{2,1,0:T(8,128)(2,1)S(1)} %get-tuple-element.205), channel_id=1, source_target_pairs={{0,6},{2,4},{4,2},{6,0},{1,7},{3,5},{5,3},{7,1},{8,14},{10,12},{12... | collective-permute-start | bytes 1769480 | tf_op jit(solution)/shard_map/ppermute | solution.py:73
  402.1 32.2 %collective-permute-start.43 = (bf16[4,96,768]{2,1,0:T(8,128)(2,1)S(1)}, bf16[4,96,768]{2,1,0:T(8,128)(2,1)S(1)}, u32[]{:S(2)}, u32[]{:S(2)}) collective-permute-start(bf16[4,96,768]{2,1,0:T(8,128)(2,1)S(1)} %get-tuple-element.206), channel_id=1, source_target_pairs={{0,4},{2,6},{4,0},{6,2},{1,5},{3,7},{5,1},{7,3},{8,12},{10,14},{12... | collective-permute-start | bytes 1769480 | tf_op jit(solution)/shard_map/ppermute | solution.py:73
  441.8 70.1 %collective-permute-start.41 = (bf16[384,2304]{1,0:T(8,128)(2,1)}, bf16[384,2304]{1,0:T(8,128)(2,1)S(1)}, u32[]{:S(2)}, u32[]{:S(2)}) collective-permute-start(bf16[384,2304]{1,0:T(8,128)(2,1)} %bitcast.42.refs_0_), channel_id=1, source_target_pairs={{0,4},{2,6},{4,0},{6,2},{1,5},{3,7},{5,1},{7,3},{8,12},{10,14},{12... | collective-permute-start | bytes 5308424 | tf_op jit(solution)/shard_map/ppermute | solution.py:73
  445.0 66.9 %collective-permute-start.40 = (bf16[384,2304]{1,0:T(8,128)(2,1)}, bf16[384,2304]{1,0:T(8,128)(2,1)S(1)}, u32[]{:S(2)}, u32[]{:S(2)}) collective-permute-start(bf16[384,2304]{1,0:T(8,128)(2,1)} %bitcast.42.refs_0_), channel_id=1, source_target_pairs={{0,2},{2,0},{4,6},{6,4},{1,3},{3,1},{5,7},{7,5},{8,10},{10,8},{12,... | collective-permute-start | bytes 5308424 | tf_op jit(solution)/shard_map/ppermute | solution.py:73
  474.1 31.6 %collective-permute-start.39 = (bf16[512,256]{1,0:T(8,128)(2,1)}, bf16[512,256]{1,0:T(8,128)(2,1)}, u32[]{:S(2)}, u32[]{:S(2)}) collective-permute-start(bf16[512,256]{1,0:T(8,128)(2,1)} %get-tuple-element.229), channel_id=1, source_target_pairs={{0,6},{2,4},{4,2},{6,0},{1,7},{3,5},{5,3},{7,1},{8,14},{10,12},{12... | collective-permute-start | bytes 786440 | tf_op jit(solution)/shard_map/ppermute | solution.py:73
  475.6 30.8 %collective-permute-start.38 = (bf16[512,256]{1,0:T(8,128)(2,1)}, bf16[512,256]{1,0:T(8,128)(2,1)}, u32[]{:S(2)}, u32[]{:S(2)}) collective-permute-start(bf16[512,256]{1,0:T(8,128)(2,1)} %get-tuple-element.230), channel_id=1, source_target_pairs={{0,4},{2,6},{4,0},{6,2},{1,5},{3,7},{5,1},{7,3},{8,12},{10,14},{12... | collective-permute-start | bytes 786440 | tf_op jit(solution)/shard_map/ppermute | solution.py:73
  476.8 33.7 %collective-permute-start.37 = (bf16[512,256]{1,0:T(8,128)(2,1)}, bf16[512,256]{1,0:T(8,128)(2,1)}, u32[]{:S(2)}, u32[]{:S(2)}) collective-permute-start(bf16[512,256]{1,0:T(8,128)(2,1)} %get-tuple-element.231), channel_id=1, source_target_pairs={{0,2},{2,0},{4,6},{6,4},{1,3},{3,1},{5,7},{7,5},{8,10},{10,8},{12,... | collective-permute-start | bytes 786440 | tf_op jit(solution)/shard_map/ppermute | solution.py:73
  506.4 38.7 %collective-permute-start.60 = (bf16[256,1536]{1,0:T(8,128)(2,1)}, bf16[256,1536]{1,0:T(8,128)(2,1)}, u32[]{:S(2)}, u32[]{:S(2)}) collective-permute-start(bf16[256,1536]{1,0:T(8,128)(2,1)} %get-tuple-element.199), channel_id=1, source_target_pairs={{0,6},{2,4},{4,2},{6,0},{1,7},{3,5},{5,3},{7,1},{8,14},{10,12},{12... | collective-permute-start | bytes 2359304 | tf_op jit(solution)/shard_map/ppermute | solution.py:73
  510.5 35.2 %collective-permute-start.59 = (bf16[256,1536]{1,0:T(8,128)(2,1)}, bf16[256,1536]{1,0:T(8,128)(2,1)}, u32[]{:S(2)}, u32[]{:S(2)}) collective-permute-start(bf16[256,1536]{1,0:T(8,128)(2,1)} %get-tuple-element.200), channel_id=1, source_target_pairs={{0,4},{2,6},{4,0},{6,2},{1,5},{3,7},{5,1},{7,3},{8,12},{10,14},{12... | collective-permute-start | bytes 2359304 | tf_op jit(solution)/shard_map/ppermute | solution.py:73
  527.4 35.8 %collective-permute-start.54 = (bf16[192,2304]{1,0:T(8,128)(2,1)S(1)}, bf16[192,2304]{1,0:T(8,128)(2,1)S(1)}, u32[]{:S(2)}, u32[]{:S(2)}) collective-permute-start(bf16[192,2304]{1,0:T(8,128)(2,1)S(1)} %slice.360), channel_id=1, source_target_pairs={{0,2},{2,0},{4,6},{6,4},{1,3},{3,1},{5,7},{7,5},{8,10},{10,8},{12,... | collective-permute-start | bytes 2654216 | tf_op jit(solution)/shard_map/ppermute | solution.py:73
  545.7 36.3 %collective-permute-start.56 = (bf16[384,1152]{1,0:T(8,128)(2,1)S(1)}, bf16[384,1152]{1,0:T(8,128)(2,1)S(1)}, u32[]{:S(2)}, u32[]{:S(2)}) collective-permute-start(bf16[384,1152]{1,0:T(8,128)(2,1)S(1)} %bitcast.154), channel_id=1, source_target_pairs={{0,4},{2,6},{4,0},{6,2},{1,5},{3,7},{5,1},{7,3},{8,12},{10,14},{12... | collective-permute-start | bytes 2654216 | tf_op jit(solution)/shard_map/ppermute | solution.py:73
  547.2 34.8 %collective-permute-start.55 = (bf16[384,1152]{1,0:T(8,128)(2,1)S(1)}, bf16[384,1152]{1,0:T(8,128)(2,1)S(1)}, u32[]{:S(2)}, u32[]{:S(2)}) collective-permute-start(bf16[384,1152]{1,0:T(8,128)(2,1)S(1)} %bitcast.155), channel_id=1, source_target_pairs={{0,2},{2,0},{4,6},{6,4},{1,3},{3,1},{5,7},{7,5},{8,10},{10,8},{12,... | collective-permute-start | bytes 2654216 | tf_op jit(solution)/shard_map/ppermute | solution.py:73
  588.3 26.8 %collective-permute-start.62 = (bf16[192,1152]{1,0:T(8,128)(2,1)}, bf16[192,1152]{1,0:T(8,128)(2,1)}, u32[]{:S(2)}, u32[]{:S(2)}) collective-permute-start(bf16[192,1152]{1,0:T(8,128)(2,1)} %slice.366), channel_id=1, source_target_pairs={{0,2},{2,0},{4,6},{6,4},{1,3},{3,1},{5,7},{7,5},{8,10},{10,8},{12,... | collective-permute-start | bytes 1327112 | tf_op jit(solution)/shard_map/ppermute | solution.py:73
  (112 other events, 1786.4 us)
Sparse Core Ops, SparseCore 0:
  52.9 141.1 all-gather.2
  203.0 68.3 all-gather.4
  275.4 121.8 reduce-scatter.2
  399.5 66.8 reduce-scatter.4

commit v3 on v2

--- a/solution.py
+++ b/solution.py
@@ -15,17 +15,6 @@
 NEG = -1e30
 
 
-def ancestor_codes(parents):
-    count = parents.shape[0]
-    ids = jnp.arange(count, dtype=jnp.int32)
-    chain = ids
-    codes = jnp.left_shift(jnp.ones((count,), jnp.int32), ids)
-    for step in range(count - 1):
-        chain = jnp.sum(jnp.where(chain[:, None] == ids[None, :], parents[None, :], 0), axis=1)
-        codes = jnp.bitwise_or(codes, jnp.left_shift(jnp.ones((count,), jnp.int32), chain))
-    return codes
-
-
 def rope_tables(pos):
     inverse = THETA ** (-jnp.arange(0, HD, 2, dtype=jnp.float32) / HD)
     angle = pos.astype(jnp.float32)[:, None] * inverse[None, :]
@@ -101,48 +90,74 @@
     return sum(block.astype(jnp.float32) for block in (blocks[0], *received[1:]))
 
 
-def spread_kernel(plan, width, total, context_ref, *refs):
+def spread_kernel(plan, spans, width, total, context_ref, *refs):
     count = len(plan)
     outs = refs[count:]
     context = context_ref[0]
-    for ref, (distance, offset, columns, matrices) in zip(refs[:count], plan):
-        start = jnp.bitwise_xor(context, distance) * width + offset
-        for slot, matrix in enumerate(matrices):
-            out = outs[matrix]
-            for piece in range(0, columns, 128):
-                place = start + piece
-
-                @pl.when(place < total)
-                def _():
-                    out[:, pl.ds(pl.multiple_of(place, 128), 128)] = ref[
-                        :, pl.ds(slot * columns + piece, 128)
-                    ].astype(jnp.float32)
-
-
-def spread(blocks, plan, width, total, context):
-    rows = blocks[0].shape[0]
-    tile = 48 if rows % 48 == 0 else rows
+    late = pl.program_id(0) >= pl.num_programs(0) // 2
+    for ref, (distance, half) in zip(refs[:count], plan):
+        start = jnp.bitwise_xor(context, distance) * width
+
+        def write():
+            base = 0
+            for offset, columns in spans:
+                for out in outs:
+                    for piece in range(0, columns, 128):
+                        place = start + offset + piece
+
+                        @pl.when(place < total)
+                        def _():
+                            out[:, pl.ds(pl.multiple_of(place, 128), 128)] = ref[
+                                :, pl.ds(base + piece, 128)
+                            ].astype(jnp.float32)
+
+                    base += columns
+
+        if half is None:
+            write()
+        else:
+            pl.when(late == (half == 1))(write)
+
+
+def spread(blocks, spans, width, total, context):
+    rows = blocks[0][0].shape[0]
+    tile = 48 if rows % 96 == 0 else rows // 2
+    steps = rows // tile // 2
+    maps = {
+        None: lambda i: (i, 0),
+        0: lambda i: (jnp.minimum(i, steps - 1), 0),
+        1: lambda i: (jnp.maximum(i - steps, 0), 0),
+    }
+    arrays = []
+    plan = []
+    for distance, pieces in enumerate(blocks):
+        for half, piece in enumerate(pieces):
+            arrays.append(piece)
+            plan.append((distance, None if len(pieces) == 1 else half))
     return pl.pallas_call(
-        functools.partial(spread_kernel, plan, width, total),
+        functools.partial(spread_kernel, tuple(plan), spans, width, total),
         grid=(rows // tile,),
         in_specs=[pl.BlockSpec(memory_space=pltpu.SMEM)]
-        + [pl.BlockSpec((tile, block.shape[1]), lambda i: (i, 0)) for block in blocks],
+        + [
+            pl.BlockSpec((tile, array.shape[1]), maps[half])
+            for array, (_, half) in zip(arrays, plan)
+        ],
         out_specs=[pl.BlockSpec((tile, total), lambda i: (i, 0))] * 3,
         out_shape=[jax.ShapeDtypeStruct((rows, total), jnp.float32)] * 3,
         compiler_params=pltpu.CompilerParams(vmem_limit_bytes=40 * 1024 * 1024),
-    )(context.reshape(1), *blocks)
-
-
-def place_kernel(count, context_ref, *refs):
-    query_ref, key_ref, value_ref, out_ref = refs[2 * count :]
+    )(context.reshape(1), *arrays)
+
+
+def place_kernel(count, part, context_ref, *refs):
+    query_ref, key_ref, value_ref, out_ref = refs[count:]
     context = context_ref[0]
+    depth = query_ref.shape[0]
     quarter = refs[0].shape[1]
-    part = refs[count].shape[0]
     whole = query_ref.shape[1] // quarter
     keys = key_ref.shape[1]
     for k in range(count):
         place = jnp.bitwise_xor(context, k)
-        block = refs[k][...].astype(jnp.float32)
+        block = refs[k][:depth].astype(jnp.float32)
 
         @pl.when(place < whole)
         def _():
@@ -154,21 +169,24 @@
             value_ref[...] = block[:, keys:]
 
         row = pl.multiple_of(place * part, 8)
-        out_ref[pl.ds(row, part), :] = refs[count + k][...].astype(jnp.float32)
-
-
-def place_attention(columns, rows, query_width, key_width, context):
-    count = len(columns)
-    depth = columns[0].shape[0]
+        for g in range(whole):
+            start = depth + g * part
+            out_ref[pl.ds(row, part), g * quarter : (g + 1) * quarter] = refs[k][
+                start : start + part
+            ].astype(jnp.float32)
+
+
+def place_attention(blocks, depth, part, query_width, key_width, context):
+    count = len(blocks)
     widths = (query_width, key_width, key_width, query_width)
     vmem = pl.BlockSpec(memory_space=pltpu.VMEM)
     return pl.pallas_call(
-        functools.partial(place_kernel, count),
-        in_specs=[pl.BlockSpec(memory_space=pltpu.SMEM)] + [vmem] * (2 * count),
+        functools.partial(place_kernel, count, part),
+        in_specs=[pl.BlockSpec(memory_space=pltpu.SMEM)] + [vmem] * count,
         out_specs=[vmem] * 4,
         out_shape=[jax.ShapeDtypeStruct((depth, width), jnp.float32) for width in widths],
         compiler_params=pltpu.CompilerParams(vmem_limit_bytes=VMEM_LIMIT),
-    )(context.reshape(1), *columns, *rows)
+    )(context.reshape(1), *blocks)
 
 
 NT = (((1,), (1,)), ((), ()))
@@ -179,6 +197,78 @@
 
 def multiply(left, right, dims):
     return lax.dot_general(left, right, dims, preferred_element_type=jnp.float32)
+
+
+def terms_kernel(count, core_ref, normed_ref, *refs):
+    blocks, (wo_ref, small_ref, out_ref, rows_ref) = refs[:count], refs[count:]
+    core = core_ref[0]
+    half = blocks[0].shape[0] // 2
+    depth = normed_ref.shape[1]
+    part = wo_ref.shape[1]
+    quarter = out_ref.shape[2]
+
+    @pl.when(pl.program_id(0) == 0)
+    def _():
+        for side in range(2):
+            start = pl.multiple_of((core if side == 0 else 1 - core) * half, half)
+            for k, block in enumerate(blocks):
+                place = (side * count + k) * half
+                rows_ref[place : place + half] = block[pl.ds(start, half), :]
+
+    out_ref[0, :depth] = multiply(normed_ref[...], rows_ref[...], TN).astype(jnp.bfloat16)
+    place = depth
+    for column in range(0, wo_ref.shape[2], quarter):
+        out_ref[0, place : place + part] = wo_ref[0, :, column : column + quarter]
+        place += part
+    size = small_ref.shape[0]
+    high = small_ref[...].astype(jnp.bfloat16)
+    out_ref[0, place : place + size] = high
+    out_ref[0, place + size :] = (small_ref[...] - high.astype(jnp.float32)).astype(jnp.bfloat16)
+
+
+def attention_terms(normed, blocks, grad_wo, small, core):
+    rows, model = normed.shape
+    shards, part, width = grad_wo.shape
+    depth = model // shards
+    quarter = blocks[0].shape[1]
+    count = depth + part * (width // quarter) + 2 * small.shape[0]
+    if depth % 128:
+        half = blocks[0].shape[0] // 2
+        ordered = [
+            lax.dynamic_slice_in_dim(block, side * half, half)
+            for side in (core, 1 - core)
+            for block in blocks
+        ]
+        columns = contract_first(normed, jnp.concatenate(ordered, axis=0)).astype(jnp.bfloat16)
+        high = small.astype(jnp.bfloat16)
+        low = (small - high.astype(jnp.float32)).astype(jnp.bfloat16)
+        return jnp.concatenate(
+            [columns.reshape(shards, depth, quarter)]
+            + [grad_wo[:, :, i : i + quarter] for i in range(0, width, quarter)]
+            + [jnp.broadcast_to(value, (shards,) + value.shape) for value in (high, low)],
+            axis=1,
+        )
+    whole = lambda value: pl.BlockSpec(value.shape, lambda i: (0, 0))
+    return pl.pallas_call(
+        functools.partial(terms_kernel, len(blocks)),
+        grid=(shards,),
+        in_specs=[
+            pl.BlockSpec(memory_space=pltpu.SMEM),
+            pl.BlockSpec((rows, depth), lambda i: (0, i)),
+            *(whole(block) for block in blocks),
+            pl.BlockSpec((1, part, width), lambda i: (i, 0, 0)),
+            whole(small),
+        ],
+        out_specs=pl.BlockSpec((1, count, quarter), lambda i: (i, 0, 0)),
+        out_shape=jax.ShapeDtypeStruct((shards, count, quarter), jnp.bfloat16),
+        scratch_shapes=[pltpu.VMEM((rows, quarter), jnp.bfloat16)],
+        compiler_params=pltpu.CompilerParams(vmem_limit_bytes=VMEM_LIMIT),
+        cost_estimate=pl.CostEstimate(
+            flops=2 * rows * model * quarter,
+            bytes_accessed=2 * (rows * model + rows * quarter + shards * count * quarter),
+            transcendentals=0,
+        ),
+    )(core.reshape(1), normed, *blocks, grad_wo, small)
 
 
 def ff_kernel(size, first, normed_ref, gradient_ref, weight_ref, *refs):
@@ -610,6 +700,7 @@
     quarter_blocks = context_send([quarter_late] * contexts)
 
     acts, *sums = feed_forward(tree_normed, tree_gradient, ff_weights[0])
+    acts, quarter_blocks = bar((acts, quarter_blocks))
     (grads,) = ff_grads(tree_normed, tree_gradient, acts, False)
     grads, late_weights = bar((grads, ff_weights[1]))
     late_acts, *sums = feed_forward(
@@ -647,11 +738,9 @@
     grad_query, grad_pairs = attend_back(
         queries, grad_mixed, cosine, sine, pairs, *mask_lines, logsum, head_loc
     )
-    grad_query, grad_pairs, ff_sums[0], late_grads = bar(
-        (grad_query, grad_pairs, ff_sums[0], late_grads)
-    )
+    grad_query, grad_pairs, ff_sums[0] = bar((grad_query, grad_pairs, ff_sums[0]))
     ff_sums.append(over_shard(late_grads))
-    early_near = context_gather_start(ff_sums[0])
+    grad_pairs, grad_wo, mlp = bar((grad_pairs, grad_wo, mlp))
     grad_pairs = context_sum([tree_block(grad_pairs, k) for k in range(contexts)])
     grad_keys = rope_back(grad_pairs[:, :kwp].reshape(rows, -1, HD), cosine, sine)
     grad_pairs = jnp.concatenate(
@@ -662,11 +751,9 @@
         lax.dynamic_index_in_dim(grad_quarters, d, axis=0, keepdims=False) for d in distances
     ]
     exchanged = context_send(relative_grads)
-    exchanged, early_near, grad_wo, ff_sums[1] = bar(
-        (exchanged, early_near, grad_wo, ff_sums[1])
-    )
-    early_blocks = context_gather_end(ff_sums[0], *early_near)
-    late_near = context_gather_start(ff_sums[1])
+    exchanged, *ff_sums = bar((exchanged, *ff_sums))
+    ff_grads_own = jnp.concatenate(ff_sums, axis=1)
+    ff_near = context_gather_start(ff_grads_own)
     normed_gradient = sum(
         contract_last(grads, block) for grads, block in zip(relative_grads, quarter_blocks)
     )
@@ -685,16 +772,6 @@
     small = small + swap(small, "tp", 1)
     small = jnp.concatenate([small, jnp.sum(grad_quarters.astype(jnp.float32), axis=1).reshape(-1)])
 
-    exchanged = jnp.concatenate(
-        [
-            lax.dynamic_slice_in_dim(block, side * half, half)
-            for side in (core, 1 - core)
-            for block in exchanged
-        ],
-        axis=0,
-    )
-    grad_columns = contract_first(first_normed, exchanged).astype(narrow_dtype)
-
     def packed(value):
         value = value.reshape(-1, quarter)
         high = value.astype(narrow_dtype)
@@ -706,12 +783,7 @@
         return value[..., :count, :] + value[..., count:, :]
 
     me = lax.axis_index("shard")
-    terms = jnp.concatenate(
-        [grad_columns.reshape(shards, depth, quarter)]
-        + [grad_wo[:, :, g * quarter : (g + 1) * quarter] for g in range(groups)]
-        + [jnp.broadcast_to(half_value, (shards,) + half_value.shape) for half_value in packed(small)],
-        axis=1,
-    )
+    terms = attention_terms(first_normed, exchanged, grad_wo, small.reshape(-1, quarter), core)
     if shards > 4:
         received = [lax.all_to_all(terms, "shard", 0, 0)[k] for k in range(shards)]
     else:
@@ -724,34 +796,20 @@
                     [(i, (i + k) % shards) for i in range(shards)],
                 )
             )
-    received, early_blocks, late_near, mlp = bar((received, early_blocks, late_near, mlp))
+    received, ff_near = bar((received, ff_near))
+    ff_blocks = context_gather_end(ff_grads_own, *ff_near)
     output = core_join((residual + mlp).astype(narrow_dtype))
-    late_blocks = context_gather_end(ff_sums[1], *late_near)
     count = depth + groups * part
     weight_sums = sum(value[:count].astype(jnp.float32) for value in received).astype(narrow_dtype)
     small = sum(unpacked(value[count:]) for value in received)
     blocks = context_send([jnp.concatenate([weight_sums, *packed(small)], axis=0)] * contexts)
     small = sum(unpacked(block[count:]) for block in blocks).reshape(-1)
-    column_blocks = [block[:depth] for block in blocks]
-    row_blocks = [
-        jnp.concatenate(
-            [block[depth + g * part : depth + (g + 1) * part] for g in range(groups)], axis=1
-        )
-        for block in blocks
-    ]
-    grad_wq, grad_wk, grad_wv, grad_wo = place_attention(
-        column_blocks, row_blocks, qwp, kwp, context
-    )
-
-    early_blocks, late_blocks, output, source_gradient, small, grad_wq = bar(
-        (early_blocks, late_blocks, output, source_gradient, small, grad_wq)
-    )
-    plan = [
-        (k, offset, size, (0, 1, 2)) for offset, size in spans for k in range(contexts)
-    ]
-    grad_wg, grad_wu, grad_wd = spread(
-        [jnp.concatenate(block, axis=0) for block in early_blocks + late_blocks], tuple(plan), width, ffp, context
-    )
+    grad_wq, grad_wk, grad_wv, grad_wo = place_attention(blocks, depth, part, qwp, kwp, context)
+
+    ff_blocks, output, source_gradient, small, grad_wq = bar(
+        (ff_blocks, output, source_gradient, small, grad_wq)
+    )
+    grad_wg, grad_wu, grad_wd = spread(ff_blocks, tuple(spans), width, ffp, context)
 
     edges = [0, model, 2 * model, 2 * model + qwp, 2 * model + qwp + kwp, small.shape[0]]
     sums = [small[edges[i] : edges[i + 1]] for i in range(5)]

time: 640 us -> 612 us (0.956)
  waiting for transfers between devices: 216 us -> 193 us
  Pallas kernels: 160 us -> 168 us
    ppermute x59 -> x55, waiting for transfers between devices: 209 us -> 166 us  [swap(): return lax.ppermute(value, axis, [(i, i ^ distance) for i in range(size)])]
    ppermute x3, waiting for transfers between devices: 6.64 us -> 26.2 us  [body(): lax.ppermute(lax.dynamic_index_in_dim(terms, lax.rem(me + k, shards), kee...]
    pallas_call x2 -> x3, Pallas kernels: 13 us -> 20.2 us  [the longest x1 10.8 us: spread(): pl.pallas_call(functools.partial(spread_kernel, tuple(plan), spans, width...]
    ppermute x59 -> x55, starting transfers between devices: 58.7 us -> 54.2 us  [swap(): return lax.ppermute(value, axis, [(i, i ^ distance) for i in range(size)])]
    unnamed x185 -> x156, local copies, waits for them, and re-layouts: 33.7 us -> 30.9 us
  transfers between devices with their start and end apart: 72 -> 68, of which waited for: 27 -> 25; matrix products, arithmetic and copies ran while one was open for 23% -> 22% of each run, Pallas kernels for 24% -> 26%
where the time goes in v3:
time: 612 us; the launch traced here: 606 us
  waiting for transfers between devices  193 us (32%)
  Pallas kernels  168 us (27%)
  local copies, waits for them, and re-layouts  81.2 us (13%)
  starting transfers between devices  72.6 us (12%)
  other arithmetic  59.9 us (10%)
  matrix products  16.5 us (3%)
  between operations  15.5 us (3%)
    ppermute x55, waiting for transfers between devices, swap(): return lax.ppermute(value, axis, [(i, i ^ distance) for i in range(size)])  166 us
    pallas_call x2, Pallas kernels, feed_forward(): pl.pallas_call(functools.partial(ff_kernel, columns // 3, not previous),...  69.7 us
    ppermute x55, starting transfers between devices, swap(): return lax.ppermute(value, axis, [(i, i ^ distance) for i in range(size)])  54.2 us
    pallas_call x2, Pallas kernels, ff_grads(): pl.pallas_call(functools.partial(ff_grads_kernel, columns // 3), grid=(mo...  34.8 us
    unnamed x156, local copies, waits for them, and re-layouts  30.9 us
    pallas_call x1, Pallas kernels, attend_back(): pl.pallas_call(attend_back_kernel, grid=(rows // tile, heads), in_specs=[...  27.2 us
    ppermute x3, waiting for transfers between devices, body(): lax.ppermute(lax.dynamic_index_in_dim(terms, lax.rem(me + k, shards), kee...  26.2 us
    pallas_call x1, Pallas kernels, attend(): pl.pallas_call(attend_kernel, grid=(rows // tile, heads), in_specs=[query...  15.8 us
  transfers between devices with their start and end apart: 68, of which 25 were waited for; matrix products, arithmetic and copies ran while one was open for 22% of the time, Pallas kernels for 26%

profile of v3, /device:TPU:0, one launch (start us, length us, event | category | flops | bytes accessed | tf_op | source)
XLA Modules:
  0.0 606.4 jit_solution(15730104021331678995)
XLA Ops:
  43.6 3.4 collective-permute-done.2
  50.8 5.3 multiply_cosine_fusion
  61.7 4.5 constant_dynamic-update-slice_fusion.5.normed_ref
  75.7 5.5 fusion.56
  108.2 6.5 %collective-permute-done.9 = bf16[512,256]{1,0:T(8,128)(2,1)S(1)} collective-permute-done((bf16[512,256]{1,0:T(8,128)(2,1)S(1)}, bf16[512,256]{1,0:T(8,128)(2,1)S(1)}, u32[]{:S(2)}, u32[]{:S(2)}) %collective-permute-start.9) | collective-permute-done | bytes 262176 | tf_op jit(solution)/shard_map/ppermute | solution.py:62
  118.7 15.8 %shard_map.272 = (bf16[512,768]{1,0:T(8,128)(2,1)}, f32[8,512]{1,0:T(8,128)}) custom-call(bf16[4,512,256]{2,1,0:T(8,128)(2,1)} %copy-done.33, bf16[2048,256]{1,0:T(8,128)(2,1)} %pad_maximum_fusion.6.key_ref.value_ref, bf16[2048,256]{1,0:T(8,128)(2,1)} %pad_maximum_fusion.6.key_ref.value_ref, s32[1,512]{1,0:T(1,128)} %bitcast.191, ...), custom_call_target="tpu_custom_call" | custom-call | flops 6442450944 | bytes 2359296 | tf_op jit(solution)/shard_map/pallas_call | solution.py:419
  136.1 9.1 %collective-permute-done.17 = bf16[2,96,768]{2,1,0:T(8,128)(2,1)S(1)} collective-permute-done((bf16[2,96,768]{2,1,0:T(8,128)(2,1)S(1)}, bf16[2,96,768]{2,1,0:T(8,128)(2,1)S(1)}, u32[]{:S(2)}, u32[]{:S(2)}) %collective-permute-start.17) | collective-permute-done | bytes 294944 | tf_op jit(solution)/shard_map/ppermute | solution.py:62
  145.2 3.5 collective-permute-done.16
  158.6 5.6 collective-permute-done.26
  165.9 14.4 %collective-permute-done.20 = bf16[256,1536]{1,0:T(8,128)(2,1)S(1)} collective-permute-done((bf16[256,1536]{1,0:T(8,128)(2,1)S(1)}, bf16[256,1536]{1,0:T(8,128)(2,1)S(1)}, u32[]{:S(2)}, u32[]{:S(2)}) %collective-permute-start.20) | collective-permute-done | bytes 786464 | tf_op jit(solution)/shard_map/ppermute | solution.py:62
  184.6 6.7 %collective-permute-done.21 = bf16[128,1536]{1,0:T(8,128)(2,1)S(1)} collective-permute-done((bf16[128,1536]{1,0:T(8,128)(2,1)S(1)}, bf16[128,1536]{1,0:T(8,128)(2,1)S(1)}, u32[]{:S(2)}, u32[]{:S(2)}) %collective-permute-start.21) | collective-permute-done | bytes 393248 | tf_op jit(solution)/shard_map/ppermute | solution.py:62
  201.1 4.0 constant_dynamic-update-slice_fusion.29.gradient_ref
  205.1 4.0 constant_dynamic-update-slice_fusion.18.normed_ref
  212.7 41.1 %shard_map.273 = (bf16[2048,2304]{1,0:T(8,128)(2,1)}, bf16[1024,1536]{1,0:T(8,128)(2,1)}, bf16[1024,1536]{1,0:T(8,128)(2,1)}, bf16[1024,1536]{1,0:T(8,128)(2,1)}, bf16[1024,1536]{1,0:T(8,128)(2,1)}) custom-call(bf16[2048,1536]{1,0:T(8,128)(2,1)} %constant_dynamic-update-slice_fusion.18.normed_ref, ...), custom_call_target="tpu_custom_call" | custom-call | flops 28991029248 | bytes 41680896 | tf_op jit(solution)/shard_map/pallas_call | solution.py:312
  253.8 21.4 %shard_map.274 = bf16[1536,2304]{1,0:T(8,128)(2,1)} custom-call(bf16[2048,1536]{1,0:T(8,128)(2,1)} %constant_dynamic-update-slice_fusion.18.normed_ref, bf16[2048,1536]{1,0:T(8,128)(2,1)} %constant_dynamic-update-slice_fusion.29.gradient_ref, bf16[2048,2304]{1,0:T(8,128)(2,1)} %get-tuple-element.96.acts_ref), custom_call_target="tpu_custom_call" | custom-call | flops 14495514624 | bytes 29097984 | tf_op jit(solution)/shard_map/pallas_call | solution.py:345
  275.3 28.5 %shard_map.275 = (bf16[2048,1152]{1,0:T(8,128)(2,1)}, bf16[1024,1536]{1,0:T(8,128)(2,1)}, bf16[1024,1536]{1,0:T(8,128)(2,1)}, bf16[1024,1536]{1,0:T(8,128)(2,1)}, bf16[1024,1536]{1,0:T(8,128)(2,1)}) custom-call(bf16[2048,1536]{1,0:T(8,128)(2,1)} %constant_dynamic-update-slice_fusion.18.normed_ref, ...), custom_call_target="tpu_custom_call" | custom-call | flops 14495514624 | bytes 33423360 | tf_op jit(solution)/shard_map/pallas_call | solution.py:312
  303.9 13.4 %shard_map.276 = bf16[1536,1152]{1,0:T(8,128)(2,1)} custom-call(bf16[2048,1536]{1,0:T(8,128)(2,1)} %constant_dynamic-update-slice_fusion.18.normed_ref, bf16[2048,1536]{1,0:T(8,128)(2,1)} %constant_dynamic-update-slice_fusion.29.gradient_ref, bf16[2048,1152]{1,0:T(8,128)(2,1)} %get-tuple-element.107.acts_ref), custom_call_target="tpu_custom_call" | custom-call | flops 7247757312 | bytes 20840448 | tf_op jit(solution)/shard_map/pallas_call | solution.py:345
  317.3 3.1 fusion.46
  324.1 16.8 %collective-permute-done.33 = bf16[256,1536]{1,0:T(8,128)(2,1)S(1)} collective-permute-done((bf16[256,1536]{1,0:T(8,128)(2,1)S(1)}, bf16[256,1536]{1,0:T(8,128)(2,1)S(1)}, u32[]{:S(2)}, u32[]{:S(2)}) %collective-permute-start.33) | collective-permute-done | bytes 786464 | tf_op jit(solution)/shard_map/ppermute | solution.py:62
  341.0 17.5 %collective-permute-done.35 = bf16[256,1536]{1,0:T(8,128)(2,1)S(1)} collective-permute-done((bf16[256,1536]{1,0:T(8,128)(2,1)S(1)}, bf16[256,1536]{1,0:T(8,128)(2,1)S(1)}, u32[]{:S(2)}, u32[]{:S(2)}) %collective-permute-start.35) | collective-permute-done | bytes 786464 | tf_op jit(solution)/shard_map/ppermute | solution.py:62
  382.1 3.9 collective-permute-done.37
  386.8 27.2 %shard_map.277 = (bf16[3,512,256]{2,1,0:T(8,128)(2,1)}, f32[2048,256]{1,0:T(8,128)}) custom-call(bf16[4,512,256]{2,1,0:T(8,128)(2,1)} %copy-done.33, bf16[512,768]{1,0:T(8,128)(2,1)} %convolution_convert_fusion.1.grad_ref, f32[512,128]{1,0:T(8,128)} %get-tuple-element.279.cosine_ref, f32[512,128]{1,0:T(8,128)} %get-tuple-element.280.sine_ref, ...), custom_call_target="tpu_custom_call" | custom-call | flops 16106127360 | bytes 2359296 | tf_op jit(solution)/shard_map/pallas_call | solution.py:491
  416.8 15.0 %collective-permute-done.43 = bf16[256,1536]{1,0:T(8,128)(2,1)} collective-permute-done((bf16[256,1536]{1,0:T(8,128)(2,1)}, bf16[256,1536]{1,0:T(8,128)(2,1)}, u32[]{:S(2)}, u32[]{:S(2)}) %collective-permute-start.43) | collective-permute-done | bytes 786464 | tf_op jit(solution)/shard_map/ppermute | solution.py:62
  433.3 3.1 fusion.16
  442.7 7.8 %collective-permute-done.45 = bf16[512,256]{1,0:T(8,128)(2,1)S(1)} collective-permute-done((bf16[512,256]{1,0:T(8,128)(2,1)S(1)}, bf16[512,256]{1,0:T(8,128)(2,1)S(1)}, u32[]{:S(2)}, u32[]{:S(2)}) %collective-permute-start.45) | collective-permute-done | bytes 262176 | tf_op jit(solution)/shard_map/ppermute | solution.py:62
  475.9 3.8 fusion.13
  482.2 6.3 %shard_map.278 = bf16[4,704,256]{2,1,0:T(8,128)(2,1)} custom-call(s32[1]{0:T(128)} %bitcast.59.core_ref, bf16[2048,1536]{1,0:T(8,128)(2,1)} %constant_dynamic-update-slice_fusion.5.normed_ref, bf16[512,256]{1,0:T(8,128)(2,1)} %copy-done.29, bf16[512,256]{1,0:T(8,128)(2,1)} %copy-done.44, bf16[512,256]{1,0:T(8,128)(2,1)} %copy-done.43, ...), custom_call_target="tpu_custom_call" | custom-call | flops 1610612736 | bytes 8781824 | tf_op jit(solution)/shard_map/pallas_call | solution.py:252
  501.6 23.4 %collective-permute-done.53 = bf16[704,256]{1,0:T(8,128)(2,1)S(1)} collective-permute-done((bf16[704,256]{1,0:T(8,128)(2,1)S(1)}, bf16[704,256]{1,0:T(8,128)(2,1)S(1)}, u32[]{:S(2)}, u32[]{:S(2)}) %collective-permute-start.53) | collective-permute-done | bytes 360480 | tf_op jit(solution)/shard_map/ppermute | solution.py:793
  524.9 5.4 collective-permute-done.56.refs_2_
  543.6 33.2 %collective-permute-done.63.refs_3_ = bf16[704,256]{1,0:T(8,128)(2,1)S(1)} collective-permute-done((bf16[704,256]{1,0:T(8,128)(2,1)S(1)}, bf16[704,256]{1,0:T(8,128)(2,1)S(1)}, u32[]{:S(2)}, u32[]{:S(2)}) %collective-permute-start.63) | collective-permute-done | bytes 360480 | tf_op jit(solution)/shard_map/ppermute | solution.py:62
  576.8 6.3 %collective-permute-done.62.refs_2_ = bf16[704,256]{1,0:T(8,128)(2,1)S(1)} collective-permute-done((bf16[704,256]{1,0:T(8,128)(2,1)S(1)}, bf16[704,256]{1,0:T(8,128)(2,1)S(1)}, u32[]{:S(2)}, u32[]{:S(2)}) %collective-permute-start.62) | collective-permute-done | bytes 360480 | tf_op jit(solution)/shard_map/ppermute | solution.py:62
  588.8 10.8 %shard_map.280 = (f32[384,4480]{1,0:T(8,128)}, f32[384,4480]{1,0:T(8,128)}, f32[384,4480]{1,0:T(8,128)}) custom-call(s32[1]{0:T(128)} %bitcast.64.context_ref, bf16[384,3456]{1,0:T(8,128)(2,1)S(1)} %constant_dynamic-update-slice_fusion.35.refs_0_, bf16[384,3456]{1,0:T(8,128)(2,1)} %collective-permute-done.55.refs_1_, ...), custom_call_target="tpu_custom_call" | custom-call | tf_op jit(solution)/shard_map/pallas_call | solution.py:137
  (423 shorter events, 214.0 us)
Async XLA Ops:
  7.2 205.5 %all-gather.3.cloned.1.call-start = ((), (), s32[]{:S(2)}) async-start(), calls=%async_computation.2 | async-start | bytes 8847360 | tf_op jit(solution)/shard_map/all_gather | solution.py:686
  20.5 38.9 %collective-permute-start.6 = (bf16[384,512]{1,0:T(8,128)(2,1)}, bf16[384,512]{1,0:T(8,128)(2,1)}, u32[]{:S(2)}, u32[]{:S(2)}) collective-permute-start(bf16[384,512]{1,0:T(8,128)(2,1)} %pad_maximum_fusion.10), channel_id=1, source_target_pairs={{0,16},{8,24},{16,0},{24,8},{1,17},{9,25},{17,1},{25,9},{2,18},{10... | collective-permute-start | bytes 1179656 | tf_op jit(solution)/shard_map/ppermute | solution.py:519
  23.1 35.2 %collective-permute-start.5 = (bf16[384,512]{1,0:T(8,128)(2,1)}, bf16[384,512]{1,0:T(8,128)(2,1)}, u32[]{:S(2)}, u32[]{:S(2)}) collective-permute-start(bf16[384,512]{1,0:T(8,128)(2,1)} %pad_maximum_fusion.10), channel_id=1, source_target_pairs={{0,8},{8,16},{16,24},{24,0},{1,9},{9,17},{17,25},{25,1},{2,10},{10... | collective-permute-start | bytes 1179656 | tf_op jit(solution)/shard_map/ppermute | solution.py:519
  24.7 35.8 %collective-permute-start.7 = (bf16[384,512]{1,0:T(8,128)(2,1)}, bf16[384,512]{1,0:T(8,128)(2,1)}, u32[]{:S(2)}, u32[]{:S(2)}) collective-permute-start(bf16[384,512]{1,0:T(8,128)(2,1)} %pad_maximum_fusion.10), channel_id=1, source_target_pairs={{0,24},{8,0},{16,8},{24,16},{1,25},{9,1},{17,9},{25,17},{2,26},{10... | collective-permute-start | bytes 1179656 | tf_op jit(solution)/shard_map/ppermute | solution.py:519
  50.4 224.9 %all-gather.5.cloned.1.call-start = ((), (), s32[]{:S(2)}) async-start(), calls=%async_computation.3 | async-start | bytes 4423680 | tf_op jit(solution)/shard_map/all_gather | solution.py:686
  67.8 36.1 %collective-permute-start.12 = (bf16[96,768]{1,0:T(8,128)(2,1)}, bf16[96,768]{1,0:T(8,128)(2,1)}, u32[]{:S(2)}, u32[]{:S(2)}) collective-permute-start(bf16[96,768]{1,0:T(8,128)(2,1)} %get-tuple-element.175), channel_id=1, source_target_pairs={{0,16},{8,24},{16,0},{24,8},{1,17},{9,25},{17,1},{25,9},{2,18},{10... | collective-permute-start | bytes 442376 | tf_op jit(solution)/shard_map/ppermute | solution.py:519
  70.5 30.9 %collective-permute-start.11 = (bf16[96,768]{1,0:T(8,128)(2,1)}, bf16[96,768]{1,0:T(8,128)(2,1)}, u32[]{:S(2)}, u32[]{:S(2)}) collective-permute-start(bf16[96,768]{1,0:T(8,128)(2,1)} %get-tuple-element.175), channel_id=1, source_target_pairs={{0,8},{8,16},{16,24},{24,0},{1,9},{9,17},{17,25},{25,1},{2,10},{10... | collective-permute-start | bytes 442376 | tf_op jit(solution)/shard_map/ppermute | solution.py:519
  72.1 32.8 %collective-permute-start.13 = (bf16[96,768]{1,0:T(8,128)(2,1)}, bf16[96,768]{1,0:T(8,128)(2,1)}, u32[]{:S(2)}, u32[]{:S(2)}) collective-permute-start(bf16[96,768]{1,0:T(8,128)(2,1)} %get-tuple-element.175), channel_id=1, source_target_pairs={{0,24},{8,0},{16,8},{24,16},{1,25},{9,1},{17,9},{25,17},{2,26},{10... | collective-permute-start | bytes 442376 | tf_op jit(solution)/shard_map/ppermute | solution.py:519
  115.9 34.6 %collective-permute-start.25 = (bf16[256,1536]{1,0:T(8,128)(2,1)S(1)}, bf16[256,1536]{1,0:T(8,128)(2,1)S(1)}, u32[]{:S(2)}, u32[]{:S(2)}) collective-permute-start(bf16[256,1536]{1,0:T(8,128)(2,1)S(1)} %get-tuple-element.169), channel_id=1, source_target_pairs={{0,4},{2,6},{4,0},{6,2},{1,5},{3,7},{5,1},{7,3},{8,12},{10,14},{12... | collective-permute-start | bytes 2359304 | tf_op jit(solution)/shard_map/ppermute | solution.py:62
  117.3 34.9 %collective-permute-start.24 = (bf16[256,1536]{1,0:T(8,128)(2,1)S(1)}, bf16[256,1536]{1,0:T(8,128)(2,1)S(1)}, u32[]{:S(2)}, u32[]{:S(2)}) collective-permute-start(bf16[256,1536]{1,0:T(8,128)(2,1)S(1)} %get-tuple-element.169), channel_id=1, source_target_pairs={{0,2},{2,0},{4,6},{6,4},{1,3},{3,1},{5,7},{7,5},{8,10},{10,8},{12,... | collective-permute-start | bytes 2359304 | tf_op jit(solution)/shard_map/ppermute | solution.py:62
  165.9 35.2 %collective-permute-start.28 = (bf16[1024,1536]{1,0:T(8,128)(2,1)}, bf16[1024,1536]{1,0:T(8,128)(2,1)}, u32[]{:S(2)}, u32[]{:S(2)}) collective-permute-start(bf16[1024,1536]{1,0:T(8,128)(2,1)} %get-tuple-element.243), channel_id=1, source_target_pairs={{0,1},{1,0},{2,3},{3,2},{4,5},{5,4},{6,7},{7,6},{8,9},{9,8},{10,11... | collective-permute-start | bytes 9437192 | tf_op jit(solution)/shard_map/ppermute | solution.py:62
  199.8 236.6 %reduce-scatter.3.cloned.1.call-start = ((), (), s32[]{:S(2)}) async-start(), calls=%async_computation.4 | async-start | bytes 8847360 | tf_op jit(solution)/shard_map/reduce_scatter | solution.py:712
  209.2 44.6 %collective-permute-start.31 = (bf16[1536,256]{1,0:T(8,128)(2,1)S(1)}, bf16[1536,256]{1,0:T(8,128)(2,1)}, u32[]{:S(2)}, u32[]{:S(2)}) collective-permute-start(bf16[1536,256]{1,0:T(8,128)(2,1)S(1)} %slice.352), channel_id=1, source_target_pairs={{0,6},{2,4},{4,2},{6,0},{1,7},{3,5},{5,3},{7,1},{8,14},{10,12},{12... | collective-permute-start | bytes 2359304 | tf_op jit(solution)/shard_map/ppermute | solution.py:62
  211.6 42.2 %collective-permute-start.30 = (bf16[1536,256]{1,0:T(8,128)(2,1)S(1)}, bf16[1536,256]{1,0:T(8,128)(2,1)}, u32[]{:S(2)}, u32[]{:S(2)}) collective-permute-start(bf16[1536,256]{1,0:T(8,128)(2,1)S(1)} %slice.352), channel_id=1, source_target_pairs={{0,4},{2,6},{4,0},{6,2},{1,5},{3,7},{5,1},{7,3},{8,12},{10,14},{12... | collective-permute-start | bytes 2359304 | tf_op jit(solution)/shard_map/ppermute | solution.py:62
  212.1 41.7 %collective-permute-start.29 = (bf16[1536,256]{1,0:T(8,128)(2,1)S(1)}, bf16[1536,256]{1,0:T(8,128)(2,1)}, u32[]{:S(2)}, u32[]{:S(2)}) collective-permute-start(bf16[1536,256]{1,0:T(8,128)(2,1)S(1)} %slice.352), channel_id=1, source_target_pairs={{0,2},{2,0},{4,6},{6,4},{1,3},{3,1},{5,7},{7,5},{8,10},{10,8},{12,... | collective-permute-start | bytes 2359304 | tf_op jit(solution)/shard_map/ppermute | solution.py:62
  275.3 190.9 %reduce-scatter.5.cloned.1.call-start = ((), (), s32[]{:S(2)}) async-start(), calls=%async_computation.5 | async-start | bytes 4423680 | tf_op jit(solution)/shard_map/reduce_scatter | solution.py:712
  322.1 36.4 %collective-permute-start.35 = (bf16[256,1536]{1,0:T(8,128)(2,1)S(1)}, bf16[256,1536]{1,0:T(8,128)(2,1)S(1)}, u32[]{:S(2)}, u32[]{:S(2)}) collective-permute-start(bf16[256,1536]{1,0:T(8,128)(2,1)S(1)} %get-tuple-element.188), channel_id=1, source_target_pairs={{0,6},{2,4},{4,2},{6,0},{1,7},{3,5},{5,3},{7,1},{8,14},{10,12},{12... | collective-permute-start | bytes 2359304 | tf_op jit(solution)/shard_map/ppermute | solution.py:62
  323.6 36.3 %collective-permute-start.34 = (bf16[256,1536]{1,0:T(8,128)(2,1)S(1)}, bf16[256,1536]{1,0:T(8,128)(2,1)S(1)}, u32[]{:S(2)}, u32[]{:S(2)}) collective-permute-start(bf16[256,1536]{1,0:T(8,128)(2,1)S(1)} %get-tuple-element.189), channel_id=1, source_target_pairs={{0,4},{2,6},{4,0},{6,2},{1,5},{3,7},{5,1},{7,3},{8,12},{10,14},{12... | collective-permute-start | bytes 2359304 | tf_op jit(solution)/shard_map/ppermute | solution.py:62
  371.3 42.8 %collective-permute-start.39 = (bf16[4,96,768]{2,1,0:T(8,128)(2,1)}, bf16[4,96,768]{2,1,0:T(8,128)(2,1)}, u32[]{:S(2)}, u32[]{:S(2)}) collective-permute-start(bf16[4,96,768]{2,1,0:T(8,128)(2,1)} %get-tuple-element.191), channel_id=1, source_target_pairs={{0,6},{2,4},{4,2},{6,0},{1,7},{3,5},{5,3},{7,1},{8,14},{10,12},{12... | collective-permute-start | bytes 1769480 | tf_op jit(solution)/shard_map/ppermute | solution.py:62
  371.8 42.2 %collective-permute-start.38 = (bf16[4,96,768]{2,1,0:T(8,128)(2,1)}, bf16[4,96,768]{2,1,0:T(8,128)(2,1)}, u32[]{:S(2)}, u32[]{:S(2)}) collective-permute-start(bf16[4,96,768]{2,1,0:T(8,128)(2,1)} %get-tuple-element.192), channel_id=1, source_target_pairs={{0,4},{2,6},{4,0},{6,2},{1,5},{3,7},{5,1},{7,3},{8,12},{10,14},{12... | collective-permute-start | bytes 1769480 | tf_op jit(solution)/shard_map/ppermute | solution.py:62
  380.0 36.8 %collective-permute-start.41 = (bf16[256,1536]{1,0:T(8,128)(2,1)}, bf16[256,1536]{1,0:T(8,128)(2,1)}, u32[]{:S(2)}, u32[]{:S(2)}) collective-permute-start(bf16[256,1536]{1,0:T(8,128)(2,1)} %get-tuple-element.184), channel_id=1, source_target_pairs={{0,2},{2,0},{4,6},{6,4},{1,3},{3,1},{5,7},{7,5},{8,10},{10,8},{12,... | collective-permute-start | bytes 2359304 | tf_op jit(solution)/shard_map/ppermute | solution.py:62
  381.5 50.3 %collective-permute-start.43 = (bf16[256,1536]{1,0:T(8,128)(2,1)}, bf16[256,1536]{1,0:T(8,128)(2,1)}, u32[]{:S(2)}, u32[]{:S(2)}) collective-permute-start(bf16[256,1536]{1,0:T(8,128)(2,1)} %get-tuple-element.185), channel_id=1, source_target_pairs={{0,6},{2,4},{4,2},{6,0},{1,7},{3,5},{5,3},{7,1},{8,14},{10,12},{12... | collective-permute-start | bytes 2359304 | tf_op jit(solution)/shard_map/ppermute | solution.py:62
  386.0 47.3 %collective-permute-start.42 = (bf16[256,1536]{1,0:T(8,128)(2,1)S(1)}, bf16[256,1536]{1,0:T(8,128)(2,1)}, u32[]{:S(2)}, u32[]{:S(2)}) collective-permute-start(bf16[256,1536]{1,0:T(8,128)(2,1)S(1)} %get-tuple-element.186), channel_id=1, source_target_pairs={{0,4},{2,6},{4,0},{6,2},{1,5},{3,7},{5,1},{7,3},{8,12},{10,14},{12... | collective-permute-start | bytes 2359304 | tf_op jit(solution)/shard_map/ppermute | solution.py:62
  471.0 59.4 %collective-permute-start.56 = (bf16[384,3456]{1,0:T(8,128)(2,1)S(1)}, bf16[384,3456]{1,0:T(8,128)(2,1)}, u32[]{:S(2)}, u32[]{:S(2)}) collective-permute-start(bf16[384,3456]{1,0:T(8,128)(2,1)S(1)} %constant_dynamic-update-slice_fusion.35.refs_0_), channel_id=1, source_target_pairs={{0,4},{2,6},{4,0},{6,2},{1,5},{3,7},{5,1},{7,3},{8,12},{10,14},{12... | collective-permute-start | bytes 7962632 | tf_op jit(solution)/shard_map/ppermute | solution.py:62
  472.6 59.0 %collective-permute-start.55 = (bf16[384,3456]{1,0:T(8,128)(2,1)S(1)}, bf16[384,3456]{1,0:T(8,128)(2,1)}, u32[]{:S(2)}, u32[]{:S(2)}) collective-permute-start(bf16[384,3456]{1,0:T(8,128)(2,1)S(1)} %constant_dynamic-update-slice_fusion.35.refs_0_), channel_id=1, source_target_pairs={{0,2},{2,0},{4,6},{6,4},{1,3},{3,1},{5,7},{7,5},{8,10},{10,8},{12,... | collective-permute-start | bytes 7962632 | tf_op jit(solution)/shard_map/ppermute | solution.py:62
  492.7 32.2 %collective-permute-start.53 = (bf16[704,256]{1,0:T(8,128)(2,1)S(1)}, bf16[704,256]{1,0:T(8,128)(2,1)S(1)}, u32[]{:S(2)}, u32[]{:S(2)}) collective-permute-start(bf16[704,256]{1,0:T(8,128)(2,1)S(1)} %get-tuple-element.212), channel_id=1, source_target_pairs={{0,16},{8,24},{16,0},{24,8},{1,17},{9,25},{17,1},{25,9},{2,18},{10... | collective-permute-start | bytes 1081352 | tf_op jit(solution)/shard_map/ppermute | solution.py:793
  494.2 30.8 %collective-permute-start.52 = (bf16[704,256]{1,0:T(8,128)(2,1)S(1)}, bf16[704,256]{1,0:T(8,128)(2,1)S(1)}, u32[]{:S(2)}, u32[]{:S(2)}) collective-permute-start(bf16[704,256]{1,0:T(8,128)(2,1)S(1)} %get-tuple-element.213), channel_id=1, source_target_pairs={{0,8},{8,16},{16,24},{24,0},{1,9},{9,17},{17,25},{25,1},{2,10},{10... | collective-permute-start | bytes 1081352 | tf_op jit(solution)/shard_map/ppermute | solution.py:793
  536.7 50.3 %collective-permute-start.58 = (bf16[192,3456]{1,0:T(8,128)(2,1)}, bf16[192,3456]{1,0:T(8,128)(2,1)S(1)}, u32[]{:S(2)}, u32[]{:S(2)}) collective-permute-start(bf16[192,3456]{1,0:T(8,128)(2,1)} %slice.298), channel_id=1, source_target_pairs={{0,2},{2,0},{4,6},{6,4},{1,3},{3,1},{5,7},{7,5},{8,10},{10,8},{12,... | collective-permute-start | bytes 3981320 | tf_op jit(solution)/shard_map/ppermute | solution.py:62
  538.2 48.9 %collective-permute-start.57 = (bf16[192,3456]{1,0:T(8,128)(2,1)}, bf16[192,3456]{1,0:T(8,128)(2,1)S(1)}, u32[]{:S(2)}, u32[]{:S(2)}) collective-permute-start(bf16[192,3456]{1,0:T(8,128)(2,1)} %slice.297), channel_id=1, source_target_pairs={{0,4},{2,6},{4,0},{6,2},{1,5},{3,7},{5,1},{7,3},{8,12},{10,14},{12... | collective-permute-start | bytes 3981320 | tf_op jit(solution)/shard_map/ppermute | solution.py:62
  538.8 38.0 %collective-permute-start.63 = (bf16[704,256]{1,0:T(8,128)(2,1)S(1)}, bf16[704,256]{1,0:T(8,128)(2,1)S(1)}, u32[]{:S(2)}, u32[]{:S(2)}) collective-permute-start(bf16[704,256]{1,0:T(8,128)(2,1)S(1)} %pad_maximum_fusion.11.refs_0_), channel_id=1, source_target_pairs={{0,6},{2,4},{4,2},{6,0},{1,7},{3,5},{5,3},{7,1},{8,14},{10,12},{12... | collective-permute-start | bytes 1081352 | tf_op jit(solution)/shard_map/ppermute | solution.py:62
  540.4 42.7 %collective-permute-start.62 = (bf16[704,256]{1,0:T(8,128)(2,1)S(1)}, bf16[704,256]{1,0:T(8,128)(2,1)S(1)}, u32[]{:S(2)}, u32[]{:S(2)}) collective-permute-start(bf16[704,256]{1,0:T(8,128)(2,1)S(1)} %pad_maximum_fusion.11.refs_0_), channel_id=1, source_target_pairs={{0,4},{2,6},{4,0},{6,2},{1,5},{3,7},{5,1},{7,3},{8,12},{10,14},{12... | collective-permute-start | bytes 1081352 | tf_op jit(solution)/shard_map/ppermute | solution.py:62
  542.2 41.0 %collective-permute-start.61 = (bf16[704,256]{1,0:T(8,128)(2,1)S(1)}, bf16[704,256]{1,0:T(8,128)(2,1)S(1)}, u32[]{:S(2)}, u32[]{:S(2)}) collective-permute-start(bf16[704,256]{1,0:T(8,128)(2,1)S(1)} %pad_maximum_fusion.11.refs_0_), channel_id=1, source_target_pairs={{0,2},{2,0},{4,6},{6,4},{1,3},{3,1},{5,7},{7,5},{8,10},{10,8},{12,... | collective-permute-start | bytes 1081352 | tf_op jit(solution)/shard_map/ppermute | solution.py:62
  (99 other events, 1078.3 us)
Sparse Core Ops, SparseCore 0:
  50.5 141.1 all-gather.2
  199.9 68.3 all-gather.4
  275.4 121.6 reduce-scatter.2
  399.3 66.8 reduce-scatter.4

commit v4 on v3

--- a/solution.py
+++ b/solution.py
@@ -85,67 +85,97 @@
     return [blocks[0]] + [swap(blocks[k], "ctx", k) for k in range(1, len(blocks))]
 
 
+def context_sum_large(blocks):
+    half = blocks[0].shape[0] // 2
+    narrow = [block.astype(jnp.bfloat16) for block in blocks]
+    far_low = swap(narrow[3][:half], "ctx", 1)
+    far_high = swap(narrow[3][half:], "ctx", 2)
+    low = (blocks[2][:half].astype(jnp.float32) + far_low.astype(jnp.float32)).astype(jnp.bfloat16)
+    high = (blocks[1][half:].astype(jnp.float32) + far_high.astype(jnp.float32)).astype(jnp.bfloat16)
+    first = swap(jnp.concatenate([narrow[1][:half], high], axis=0), "ctx", 1)
+    second = swap(jnp.concatenate([low, narrow[2][half:]], axis=0), "ctx", 2)
+    return blocks[0].astype(jnp.float32) + first.astype(jnp.float32) + second.astype(jnp.float32)
+
+
 def context_sum(blocks):
     received = context_send([block.astype(jnp.bfloat16) for block in blocks])
     return sum(block.astype(jnp.float32) for block in (blocks[0], *received[1:]))
 
 
-def spread_kernel(plan, spans, width, total, context_ref, *refs):
-    count = len(plan)
-    outs = refs[count:]
+def spread_kernel(spans, width, total, context_ref, *refs):
+    *blocks, gate_ref, up_ref, down_ref = refs
     context = context_ref[0]
+    for distance, ref in enumerate(blocks):
+        start = jnp.bitwise_xor(context, distance) * width
+        base = 0
+        for offset, columns in spans:
+            for out in (gate_ref, up_ref, down_ref):
+                for piece in range(0, columns, 128):
+                    place = start + offset + piece
+
+                    @pl.when(place < total)
+                    def _():
+                        out[:, pl.ds(pl.multiple_of(place, 128), 128)] = ref[
+                            :, pl.ds(base + piece, 128)
+                        ].astype(jnp.float32)
+
+                base += columns
+
+
+def spread(blocks, spans, width, total, context):
+    rows = blocks[0].shape[0]
+    tile = 48 if rows % 48 == 0 else rows
+    return pl.pallas_call(
+        functools.partial(spread_kernel, spans, width, total),
+        grid=(rows // tile,),
+        in_specs=[pl.BlockSpec(memory_space=pltpu.SMEM)]
+        + [pl.BlockSpec((tile, block.shape[1]), lambda i: (i, 0)) for block in blocks],
+        out_specs=[pl.BlockSpec((tile, total), lambda i: (i, 0))] * 3,
+        out_shape=[jax.ShapeDtypeStruct((rows, total), jnp.float32)] * 3,
+        compiler_params=pltpu.CompilerParams(vmem_limit_bytes=40 * 1024 * 1024),
+    )(context.reshape(1), *blocks)
+
+
+def spread_far_kernel(spans, place_ref, low_ref, high_ref, *refs):
+    outs = refs[3:]
     late = pl.program_id(0) >= pl.num_programs(0) // 2
-    for ref, (distance, half) in zip(refs[:count], plan):
-        start = jnp.bitwise_xor(context, distance) * width
-
-        def write():
+    for side, ref in enumerate((low_ref, high_ref)):
+
+        @pl.when(late == (side == 1))
+        def _():
             base = 0
             for offset, columns in spans:
                 for out in outs:
-                    for piece in range(0, columns, 128):
-                        place = start + offset + piece
-
-                        @pl.when(place < total)
-                        def _():
-                            out[:, pl.ds(pl.multiple_of(place, 128), 128)] = ref[
-                                :, pl.ds(base + piece, 128)
-                            ].astype(jnp.float32)
-
+                    out[:, offset : offset + columns] = ref[:, base : base + columns].astype(
+                        jnp.float32
+                    )
                     base += columns
 
-        if half is None:
-            write()
-        else:
-            pl.when(late == (half == 1))(write)
-
-
-def spread(blocks, spans, width, total, context):
-    rows = blocks[0][0].shape[0]
-    tile = 48 if rows % 96 == 0 else rows // 2
-    steps = rows // tile // 2
-    maps = {
-        None: lambda i: (i, 0),
-        0: lambda i: (jnp.minimum(i, steps - 1), 0),
-        1: lambda i: (jnp.maximum(i - steps, 0), 0),
-    }
-    arrays = []
-    plan = []
-    for distance, pieces in enumerate(blocks):
-        for half, piece in enumerate(pieces):
-            arrays.append(piece)
-            plan.append((distance, None if len(pieces) == 1 else half))
+
+def spread_far(low, high, wholes, spans, width, place):
+    rows, total = wholes[0].shape
+    steps = 1
+    tile = rows // 2
+    while tile % 2 == 0 and tile > 96:
+        tile //= 2
+        steps *= 2
+    grid_spec = pltpu.PrefetchScalarGridSpec(
+        num_scalar_prefetch=1,
+        grid=(2 * steps,),
+        in_specs=[
+            pl.BlockSpec((tile, low.shape[1]), lambda i, p: (jnp.minimum(i, steps - 1), 0)),
+            pl.BlockSpec((tile, low.shape[1]), lambda i, p: (jnp.maximum(i - steps, 0), 0)),
+        ]
+        + [pl.BlockSpec(memory_space=pl.ANY)] * 3,
+        out_specs=[pl.BlockSpec((tile, width), lambda i, p: (i, p[0]))] * 3,
+    )
     return pl.pallas_call(
-        functools.partial(spread_kernel, tuple(plan), spans, width, total),
-        grid=(rows // tile,),
-        in_specs=[pl.BlockSpec(memory_space=pltpu.SMEM)]
-        + [
-            pl.BlockSpec((tile, array.shape[1]), maps[half])
-            for array, (_, half) in zip(arrays, plan)
-        ],
-        out_specs=[pl.BlockSpec((tile, total), lambda i: (i, 0))] * 3,
+        functools.partial(spread_far_kernel, spans),
+        grid_spec=grid_spec,
         out_shape=[jax.ShapeDtypeStruct((rows, total), jnp.float32)] * 3,
+        input_output_aliases={3: 0, 4: 1, 5: 2},
         compiler_params=pltpu.CompilerParams(vmem_limit_bytes=40 * 1024 * 1024),
-    )(context.reshape(1), *arrays)
+    )(place.reshape(1), low, high, *wholes)
 
 
 def place_kernel(count, part, context_ref, *refs):
@@ -717,7 +747,7 @@
 
     mlp_mine, mlp_other, back_mine, back_other = sums
     back_mine, back_other, late_grads = bar((back_mine, swap(back_other, "tp", 1), late_grads))
-    second_normed_gradient = context_sum(tree_terms(back_mine, back_other))
+    second_normed_gradient = context_sum_large(tree_terms(back_mine, back_other))
     second_normed_gradient, mlp_mine, mlp_other = bar(
         (second_normed_gradient, mlp_mine, mlp_other)
     )
@@ -740,7 +770,7 @@
     )
     grad_query, grad_pairs, ff_sums[0] = bar((grad_query, grad_pairs, ff_sums[0]))
     ff_sums.append(over_shard(late_grads))
-    grad_pairs, grad_wo, mlp = bar((grad_pairs, grad_wo, mlp))
+    grad_pairs, mlp = bar((grad_pairs, mlp))
     grad_pairs = context_sum([tree_block(grad_pairs, k) for k in range(contexts)])
     grad_keys = rope_back(grad_pairs[:, :kwp].reshape(rows, -1, HD), cosine, sine)
     grad_pairs = jnp.concatenate(
@@ -751,7 +781,7 @@
         lax.dynamic_index_in_dim(grad_quarters, d, axis=0, keepdims=False) for d in distances
     ]
     exchanged = context_send(relative_grads)
-    exchanged, *ff_sums = bar((exchanged, *ff_sums))
+    exchanged, grad_wo, *ff_sums = bar((exchanged, grad_wo, *ff_sums))
     ff_grads_own = jnp.concatenate(ff_sums, axis=1)
     ff_near = context_gather_start(ff_grads_own)
     normed_gradient = sum(
@@ -806,10 +836,11 @@
     small = sum(unpacked(block[count:]) for block in blocks).reshape(-1)
     grad_wq, grad_wk, grad_wv, grad_wo = place_attention(blocks, depth, part, qwp, kwp, context)
 
-    ff_blocks, output, source_gradient, small, grad_wq = bar(
-        (ff_blocks, output, source_gradient, small, grad_wq)
-    )
-    grad_wg, grad_wu, grad_wd = spread(ff_blocks, tuple(spans), width, ffp, context)
+    wholes = spread([block[0] for block in ff_blocks[:3]], tuple(spans), width, ffp, context)
+    far, wholes, output, source_gradient, small, grad_wq = bar(
+        (ff_blocks[3], wholes, output, source_gradient, small, grad_wq)
+    )
+    grad_wg, grad_wu, grad_wd = spread_far(*far, wholes, tuple(spans), width, distances[3])
 
     edges = [0, model, 2 * model, 2 * model + qwp, 2 * model + qwp + kwp, small.shape[0]]
     sums = [small[edges[i] : edges[i + 1]] for i in range(5)]

time: 612 us -> 602 us (0.984)
  waiting for transfers between devices: 193 us -> 177 us
    ppermute x55 -> x56, waiting for transfers between devices: 166 us -> 141 us  [swap(): return lax.ppermute(value, axis, [(i, i ^ distance) for i in range(size)])]
    reduce_scatter x2, waiting for transfers between devices: 0.8 us -> 9.91 us  [over_shard(): lax.psum_scatter(value.reshape(shards, depth, value.shape[1]), 'shard', s...]
    ppermute x55 -> x56, starting transfers between devices: 54.2 us -> 57.9 us  [swap(): return lax.ppermute(value, axis, [(i, i ^ distance) for i in range(size)])]
    pallas_call x1 -> x2, Pallas kernels: 10.8 us -> 13.1 us  [the longest x1 10.5 us: spread(): pl.pallas_call(functools.partial(spread_kernel, spans, width, total), gri...]
    unnamed x156 -> x152, local copies, waits for them, and re-layouts: 30.9 us -> 30.2 us
  transfers between devices with their start and end apart: 68 -> 69, of which waited for: 25 -> 27; matrix products, arithmetic and copies ran while one was open for 22% -> 22% of each run, Pallas kernels for 26% -> 28%
where the time goes in v4:
time: 602 us; the launch traced here: 597 us
  waiting for transfers between devices  177 us (29%)
  Pallas kernels  170 us (28%)
  local copies, waits for them, and re-layouts  80.4 us (13%)
  starting transfers between devices  76 us (13%)
  other arithmetic  58.6 us (10%)
  matrix products  19.8 us (3%)
  between operations  15.5 us (3%)
    ppermute x56, waiting for transfers between devices, swap(): return lax.ppermute(value, axis, [(i, i ^ distance) for i in range(size)])  141 us
    pallas_call x2, Pallas kernels, feed_forward(): pl.pallas_call(functools.partial(ff_kernel, columns // 3, not previous),...  69.4 us
    ppermute x56, starting transfers between devices, swap(): return lax.ppermute(value, axis, [(i, i ^ distance) for i in range(size)])  57.9 us
    pallas_call x2, Pallas kernels, ff_grads(): pl.pallas_call(functools.partial(ff_grads_kernel, columns // 3), grid=(mo...  34.9 us
    unnamed x152, local copies, waits for them, and re-layouts  30.2 us
    pallas_call x1, Pallas kernels, attend_back(): pl.pallas_call(attend_back_kernel, grid=(rows // tile, heads), in_specs=[...  27.1 us
    ppermute x3, waiting for transfers between devices, body(): lax.ppermute(lax.dynamic_index_in_dim(terms, lax.rem(me + k, shards), kee...  26.2 us
    pallas_call x1, Pallas kernels, attend(): pl.pallas_call(attend_kernel, grid=(rows // tile, heads), in_specs=[query...  16 us
  transfers between devices with their start and end apart: 69, of which 27 were waited for; matrix products, arithmetic and copies ran while one was open for 22% of the time, Pallas kernels for 28%

profile of v4, /device:TPU:0, one launch (start us, length us, event | category | flops | bytes accessed | tf_op | source)
XLA Modules:
  0.0 596.9 jit_solution(7026796948955698382)
XLA Ops:
  43.6 3.4 collective-permute-done.2
  50.7 5.3 multiply_cosine_fusion
  61.6 4.6 constant_dynamic-update-slice_fusion.5.normed_ref
  75.3 5.5 fusion.57
  107.8 6.5 %collective-permute-done.9 = bf16[512,256]{1,0:T(8,128)(2,1)S(1)} collective-permute-done((bf16[512,256]{1,0:T(8,128)(2,1)S(1)}, bf16[512,256]{1,0:T(8,128)(2,1)S(1)}, u32[]{:S(2)}, u32[]{:S(2)}) %collective-permute-start.9) | collective-permute-done | bytes 262176 | tf_op jit(solution)/shard_map/ppermute | solution.py:62
  118.2 16.0 %shard_map.272 = (bf16[512,768]{1,0:T(8,128)(2,1)}, f32[8,512]{1,0:T(8,128)}) custom-call(bf16[4,512,256]{2,1,0:T(8,128)(2,1)} %copy-done.33, bf16[2048,256]{1,0:T(8,128)(2,1)} %pad_maximum_fusion.6.key_ref.value_ref, bf16[2048,256]{1,0:T(8,128)(2,1)} %pad_maximum_fusion.6.key_ref.value_ref, s32[1,512]{1,0:T(1,128)} %bitcast.192, ...), custom_call_target="tpu_custom_call" | custom-call | flops 6442450944 | bytes 2359296 | tf_op jit(solution)/shard_map/pallas_call | solution.py:449
  135.9 9.0 %collective-permute-done.17 = bf16[2,96,768]{2,1,0:T(8,128)(2,1)S(1)} collective-permute-done((bf16[2,96,768]{2,1,0:T(8,128)(2,1)S(1)}, bf16[2,96,768]{2,1,0:T(8,128)(2,1)S(1)}, u32[]{:S(2)}, u32[]{:S(2)}) %collective-permute-start.17) | collective-permute-done | bytes 294944 | tf_op jit(solution)/shard_map/ppermute | solution.py:62
  144.8 3.5 collective-permute-done.16
  158.1 5.6 collective-permute-done.26
  165.5 14.4 %collective-permute-done.20 = bf16[256,1536]{1,0:T(8,128)(2,1)S(1)} collective-permute-done((bf16[256,1536]{1,0:T(8,128)(2,1)S(1)}, bf16[256,1536]{1,0:T(8,128)(2,1)S(1)}, u32[]{:S(2)}, u32[]{:S(2)}) %collective-permute-start.20) | collective-permute-done | bytes 786464 | tf_op jit(solution)/shard_map/ppermute | solution.py:62
  184.1 6.7 %collective-permute-done.21 = bf16[128,1536]{1,0:T(8,128)(2,1)S(1)} collective-permute-done((bf16[128,1536]{1,0:T(8,128)(2,1)S(1)}, bf16[128,1536]{1,0:T(8,128)(2,1)S(1)}, u32[]{:S(2)}, u32[]{:S(2)}) %collective-permute-start.21) | collective-permute-done | bytes 393248 | tf_op jit(solution)/shard_map/ppermute | solution.py:62
  200.7 4.0 constant_dynamic-update-slice_fusion.29.gradient_ref
  204.7 4.0 constant_dynamic-update-slice_fusion.18.normed_ref
  212.3 41.2 %shard_map.273 = (bf16[2048,2304]{1,0:T(8,128)(2,1)}, bf16[1024,1536]{1,0:T(8,128)(2,1)}, bf16[1024,1536]{1,0:T(8,128)(2,1)}, bf16[1024,1536]{1,0:T(8,128)(2,1)}, bf16[1024,1536]{1,0:T(8,128)(2,1)}) custom-call(bf16[2048,1536]{1,0:T(8,128)(2,1)} %constant_dynamic-update-slice_fusion.18.normed_ref, ...), custom_call_target="tpu_custom_call" | custom-call | flops 28991029248 | bytes 41680896 | tf_op jit(solution)/shard_map/pallas_call | solution.py:342
  253.4 21.5 %shard_map.274 = bf16[1536,2304]{1,0:T(8,128)(2,1)} custom-call(bf16[2048,1536]{1,0:T(8,128)(2,1)} %constant_dynamic-update-slice_fusion.18.normed_ref, bf16[2048,1536]{1,0:T(8,128)(2,1)} %constant_dynamic-update-slice_fusion.29.gradient_ref, bf16[2048,2304]{1,0:T(8,128)(2,1)} %get-tuple-element.99.acts_ref), custom_call_target="tpu_custom_call" | custom-call | flops 14495514624 | bytes 29097984 | tf_op jit(solution)/shard_map/pallas_call | solution.py:375
  275.0 28.2 %shard_map.275 = (bf16[2048,1152]{1,0:T(8,128)(2,1)}, bf16[1024,1536]{1,0:T(8,128)(2,1)}, bf16[1024,1536]{1,0:T(8,128)(2,1)}, bf16[1024,1536]{1,0:T(8,128)(2,1)}, bf16[1024,1536]{1,0:T(8,128)(2,1)}) custom-call(bf16[2048,1536]{1,0:T(8,128)(2,1)} %constant_dynamic-update-slice_fusion.18.normed_ref, ...), custom_call_target="tpu_custom_call" | custom-call | flops 14495514624 | bytes 33423360 | tf_op jit(solution)/shard_map/pallas_call | solution.py:342
  303.2 13.4 %shard_map.276 = bf16[1536,1152]{1,0:T(8,128)(2,1)} custom-call(bf16[2048,1536]{1,0:T(8,128)(2,1)} %constant_dynamic-update-slice_fusion.18.normed_ref, bf16[2048,1536]{1,0:T(8,128)(2,1)} %constant_dynamic-update-slice_fusion.29.gradient_ref, bf16[2048,1152]{1,0:T(8,128)(2,1)} %get-tuple-element.110.acts_ref), custom_call_target="tpu_custom_call" | custom-call | flops 7247757312 | bytes 20840448 | tf_op jit(solution)/shard_map/pallas_call | solution.py:375
  322.9 8.5 %collective-permute-done.35 = bf16[128,1536]{1,0:T(8,128)(2,1)S(1)} collective-permute-done((bf16[128,1536]{1,0:T(8,128)(2,1)S(1)}, bf16[128,1536]{1,0:T(8,128)(2,1)S(1)}, u32[]{:S(2)}, u32[]{:S(2)}) %collective-permute-start.35) | collective-permute-done | bytes 393248 | tf_op jit(solution)/shard_map/ppermute | solution.py:62
  335.1 16.8 %collective-permute-done.36 = bf16[256,1536]{1,0:T(8,128)(2,1)S(1)} collective-permute-done((bf16[256,1536]{1,0:T(8,128)(2,1)S(1)}, bf16[256,1536]{1,0:T(8,128)(2,1)S(1)}, u32[]{:S(2)}, u32[]{:S(2)}) %collective-permute-start.36) | collective-permute-done | bytes 786464 | tf_op jit(solution)/shard_map/ppermute | solution.py:62
  371.2 27.1 %shard_map.277 = (bf16[3,512,256]{2,1,0:T(8,128)(2,1)}, f32[2048,256]{1,0:T(8,128)}) custom-call(bf16[4,512,256]{2,1,0:T(8,128)(2,1)} %copy-done.33, bf16[512,768]{1,0:T(8,128)(2,1)} %convolution_convert_fusion.1.grad_ref, f32[512,128]{1,0:T(8,128)} %get-tuple-element.288.cosine_ref, f32[512,128]{1,0:T(8,128)} %get-tuple-element.289.sine_ref, ...), custom_call_target="tpu_custom_call" | custom-call | flops 16106127360 | bytes 2359296 | tf_op jit(solution)/shard_map/pallas_call | solution.py:521
  398.3 4.4 convolution_convert_fusion
  405.7 3.3 fusion.16
  418.7 3.7 collective-permute-done.43
  441.8 11.7 %collective-permute-done.50 = bf16[4,96,768]{2,1,0:T(8,128)(2,1)S(1)} collective-permute-done((bf16[4,96,768]{2,1,0:T(8,128)(2,1)S(1)}, bf16[4,96,768]{2,1,0:T(8,128)(2,1)S(1)}, u32[]{:S(2)}, u32[]{:S(2)}) %collective-permute-start.50) | collective-permute-done | bytes 589856 | tf_op jit(solution)/shard_map/ppermute | solution.py:62
  455.9 9.9 %reduce-scatter.5.cloned.1.call-done = bf16[1,384,1152]{2,1,0:T(8,128)(2,1)} async-done(((bf16[4,384,1152]{2,1,0:T(8,128)(2,1)}), bf16[1,384,1152]{2,1,0:T(8,128)(2,1)}) %reduce-scatter.5.cloned.1.call-update) | async-done | bytes 884752 | tf_op jit(solution)/shard_map/reduce_scatter | solution.py:742
  474.7 3.8 fusion.13
  481.1 6.1 %shard_map.278 = bf16[4,704,256]{2,1,0:T(8,128)(2,1)} custom-call(s32[1]{0:T(128)} %bitcast.core_ref, bf16[2048,1536]{1,0:T(8,128)(2,1)} %constant_dynamic-update-slice_fusion.5.normed_ref, bf16[512,256]{1,0:T(8,128)(2,1)} %copy-done.29, bf16[512,256]{1,0:T(8,128)(2,1)} %copy-done.43, bf16[512,256]{1,0:T(8,128)(2,1)} %collective-permute-done.46.refs_2_, ...), custom_call_target="tpu_custom_call" | custom-call | flops 1610612736 | bytes 8781824 | tf_op jit(solution)/shard_map/pallas_call | solution.py:282
  500.2 23.4 %collective-permute-done.54 = bf16[704,256]{1,0:T(8,128)(2,1)S(1)} collective-permute-done((bf16[704,256]{1,0:T(8,128)(2,1)S(1)}, bf16[704,256]{1,0:T(8,128)(2,1)S(1)}, u32[]{:S(2)}, u32[]{:S(2)}) %collective-permute-start.54) | collective-permute-done | bytes 360480 | tf_op jit(solution)/shard_map/ppermute | solution.py:823
  523.5 5.6 collective-permute-done.57.refs_2_
  542.5 10.5 %shard_map.279 = (f32[384,4480]{1,0:T(8,128)}, f32[384,4480]{1,0:T(8,128)}, f32[384,4480]{1,0:T(8,128)}) custom-call(s32[1]{0:T(128)} %bitcast.64.context_ref, bf16[384,3456]{1,0:T(8,128)(2,1)S(1)} %constant_dynamic-update-slice_fusion.35.refs_0_, bf16[384,3456]{1,0:T(8,128)(2,1)} %collective-permute-done.56.refs_1_, ...), custom_call_target="tpu_custom_call" | custom-call | tf_op jit(solution)/shard_map/pallas_call | solution.py:128
  553.0 22.7 %collective-permute-done.64.refs_3_ = bf16[704,256]{1,0:T(8,128)(2,1)S(1)} collective-permute-done((bf16[704,256]{1,0:T(8,128)(2,1)S(1)}, bf16[704,256]{1,0:T(8,128)(2,1)S(1)}, u32[]{:S(2)}, u32[]{:S(2)}) %collective-permute-start.64) | collective-permute-done | bytes 360480 | tf_op jit(solution)/shard_map/ppermute | solution.py:62
  575.7 6.3 %collective-permute-done.63.refs_2_ = bf16[704,256]{1,0:T(8,128)(2,1)S(1)} collective-permute-done((bf16[704,256]{1,0:T(8,128)(2,1)S(1)}, bf16[704,256]{1,0:T(8,128)(2,1)S(1)}, u32[]{:S(2)}, u32[]{:S(2)}) %collective-permute-start.63) | collective-permute-done | bytes 360480 | tf_op jit(solution)/shard_map/ppermute | solution.py:62
  (425 shorter events, 224.8 us)
Async XLA Ops:
  7.2 205.1 %all-gather.3.cloned.1.call-start = ((), (), s32[]{:S(2)}) async-start(), calls=%async_computation.2 | async-start | bytes 8847360 | tf_op jit(solution)/shard_map/all_gather | solution.py:716
  20.5 38.8 %collective-permute-start.6 = (bf16[384,512]{1,0:T(8,128)(2,1)}, bf16[384,512]{1,0:T(8,128)(2,1)}, u32[]{:S(2)}, u32[]{:S(2)}) collective-permute-start(bf16[384,512]{1,0:T(8,128)(2,1)} %pad_maximum_fusion.12), channel_id=1, source_target_pairs={{0,16},{8,24},{16,0},{24,8},{1,17},{9,25},{17,1},{25,9},{2,18},{10... | collective-permute-start | bytes 1179656 | tf_op jit(solution)/shard_map/ppermute | solution.py:549
  23.1 35.2 %collective-permute-start.5 = (bf16[384,512]{1,0:T(8,128)(2,1)}, bf16[384,512]{1,0:T(8,128)(2,1)}, u32[]{:S(2)}, u32[]{:S(2)}) collective-permute-start(bf16[384,512]{1,0:T(8,128)(2,1)} %pad_maximum_fusion.12), channel_id=1, source_target_pairs={{0,8},{8,16},{16,24},{24,0},{1,9},{9,17},{17,25},{25,1},{2,10},{10... | collective-permute-start | bytes 1179656 | tf_op jit(solution)/shard_map/ppermute | solution.py:549
  24.7 35.8 %collective-permute-start.7 = (bf16[384,512]{1,0:T(8,128)(2,1)}, bf16[384,512]{1,0:T(8,128)(2,1)}, u32[]{:S(2)}, u32[]{:S(2)}) collective-permute-start(bf16[384,512]{1,0:T(8,128)(2,1)} %pad_maximum_fusion.12), channel_id=1, source_target_pairs={{0,24},{8,0},{16,8},{24,16},{1,25},{9,1},{17,9},{25,17},{2,26},{10... | collective-permute-start | bytes 1179656 | tf_op jit(solution)/shard_map/ppermute | solution.py:549
  50.3 224.6 %all-gather.5.cloned.1.call-start = ((), (), s32[]{:S(2)}) async-start(), calls=%async_computation.3 | async-start | bytes 4423680 | tf_op jit(solution)/shard_map/all_gather | solution.py:716
  67.8 35.8 %collective-permute-start.12 = (bf16[96,768]{1,0:T(8,128)(2,1)}, bf16[96,768]{1,0:T(8,128)(2,1)}, u32[]{:S(2)}, u32[]{:S(2)}) collective-permute-start(bf16[96,768]{1,0:T(8,128)(2,1)} %get-tuple-element.181), channel_id=1, source_target_pairs={{0,16},{8,24},{16,0},{24,8},{1,17},{9,25},{17,1},{25,9},{2,18},{10... | collective-permute-start | bytes 442376 | tf_op jit(solution)/shard_map/ppermute | solution.py:549
  70.4 30.5 %collective-permute-start.11 = (bf16[96,768]{1,0:T(8,128)(2,1)}, bf16[96,768]{1,0:T(8,128)(2,1)}, u32[]{:S(2)}, u32[]{:S(2)}) collective-permute-start(bf16[96,768]{1,0:T(8,128)(2,1)} %get-tuple-element.181), channel_id=1, source_target_pairs={{0,8},{8,16},{16,24},{24,0},{1,9},{9,17},{17,25},{25,1},{2,10},{10... | collective-permute-start | bytes 442376 | tf_op jit(solution)/shard_map/ppermute | solution.py:549
  72.0 32.5 %collective-permute-start.13 = (bf16[96,768]{1,0:T(8,128)(2,1)}, bf16[96,768]{1,0:T(8,128)(2,1)}, u32[]{:S(2)}, u32[]{:S(2)}) collective-permute-start(bf16[96,768]{1,0:T(8,128)(2,1)} %get-tuple-element.181), channel_id=1, source_target_pairs={{0,24},{8,0},{16,8},{24,16},{1,25},{9,1},{17,9},{25,17},{2,26},{10... | collective-permute-start | bytes 442376 | tf_op jit(solution)/shard_map/ppermute | solution.py:549
  115.5 34.7 %collective-permute-start.25 = (bf16[256,1536]{1,0:T(8,128)(2,1)S(1)}, bf16[256,1536]{1,0:T(8,128)(2,1)S(1)}, u32[]{:S(2)}, u32[]{:S(2)}) collective-permute-start(bf16[256,1536]{1,0:T(8,128)(2,1)S(1)} %get-tuple-element.175), channel_id=1, source_target_pairs={{0,4},{2,6},{4,0},{6,2},{1,5},{3,7},{5,1},{7,3},{8,12},{10,14},{12... | collective-permute-start | bytes 2359304 | tf_op jit(solution)/shard_map/ppermute | solution.py:62
  116.8 34.9 %collective-permute-start.24 = (bf16[256,1536]{1,0:T(8,128)(2,1)S(1)}, bf16[256,1536]{1,0:T(8,128)(2,1)S(1)}, u32[]{:S(2)}, u32[]{:S(2)}) collective-permute-start(bf16[256,1536]{1,0:T(8,128)(2,1)S(1)} %get-tuple-element.175), channel_id=1, source_target_pairs={{0,2},{2,0},{4,6},{6,4},{1,3},{3,1},{5,7},{7,5},{8,10},{10,8},{12,... | collective-permute-start | bytes 2359304 | tf_op jit(solution)/shard_map/ppermute | solution.py:62
  165.4 35.2 %collective-permute-start.28 = (bf16[1024,1536]{1,0:T(8,128)(2,1)}, bf16[1024,1536]{1,0:T(8,128)(2,1)}, u32[]{:S(2)}, u32[]{:S(2)}) collective-permute-start(bf16[1024,1536]{1,0:T(8,128)(2,1)} %get-tuple-element.252), channel_id=1, source_target_pairs={{0,1},{1,0},{2,3},{3,2},{4,5},{5,4},{6,7},{7,6},{8,9},{9,8},{10,11... | collective-permute-start | bytes 9437192 | tf_op jit(solution)/shard_map/ppermute | solution.py:62
  199.4 209.5 %reduce-scatter.3.cloned.1.call-start = ((), (), s32[]{:S(2)}) async-start(), calls=%async_computation.4 | async-start | bytes 8847360 | tf_op jit(solution)/shard_map/reduce_scatter | solution.py:742
  208.8 44.7 %collective-permute-start.31 = (bf16[1536,256]{1,0:T(8,128)(2,1)S(1)}, bf16[1536,256]{1,0:T(8,128)(2,1)}, u32[]{:S(2)}, u32[]{:S(2)}) collective-permute-start(bf16[1536,256]{1,0:T(8,128)(2,1)S(1)} %slice.373), channel_id=1, source_target_pairs={{0,6},{2,4},{4,2},{6,0},{1,7},{3,5},{5,3},{7,1},{8,14},{10,12},{12... | collective-permute-start | bytes 2359304 | tf_op jit(solution)/shard_map/ppermute | solution.py:62
  211.2 42.2 %collective-permute-start.30 = (bf16[1536,256]{1,0:T(8,128)(2,1)S(1)}, bf16[1536,256]{1,0:T(8,128)(2,1)}, u32[]{:S(2)}, u32[]{:S(2)}) collective-permute-start(bf16[1536,256]{1,0:T(8,128)(2,1)S(1)} %slice.373), channel_id=1, source_target_pairs={{0,4},{2,6},{4,0},{6,2},{1,5},{3,7},{5,1},{7,3},{8,12},{10,14},{12... | collective-permute-start | bytes 2359304 | tf_op jit(solution)/shard_map/ppermute | solution.py:62
  211.7 41.7 %collective-permute-start.29 = (bf16[1536,256]{1,0:T(8,128)(2,1)S(1)}, bf16[1536,256]{1,0:T(8,128)(2,1)}, u32[]{:S(2)}, u32[]{:S(2)}) collective-permute-start(bf16[1536,256]{1,0:T(8,128)(2,1)S(1)} %slice.373), channel_id=1, source_target_pairs={{0,2},{2,0},{4,6},{6,4},{1,3},{3,1},{5,7},{7,5},{8,10},{10,8},{12,... | collective-permute-start | bytes 2359304 | tf_op jit(solution)/shard_map/ppermute | solution.py:62
  274.9 190.9 %reduce-scatter.5.cloned.1.call-start = ((), (), s32[]{:S(2)}) async-start(), calls=%async_computation.5 | async-start | bytes 4423680 | tf_op jit(solution)/shard_map/reduce_scatter | solution.py:742
  367.7 35.1 %collective-permute-start.39 = (bf16[256,1536]{1,0:T(8,128)(2,1)}, bf16[256,1536]{1,0:T(8,128)(2,1)}, u32[]{:S(2)}, u32[]{:S(2)}) collective-permute-start(bf16[256,1536]{1,0:T(8,128)(2,1)} %get-tuple-element.192), channel_id=1, source_target_pairs={{0,2},{2,0},{4,6},{6,4},{1,3},{3,1},{5,7},{7,5},{8,10},{10,8},{12,... | collective-permute-start | bytes 2359304 | tf_op jit(solution)/shard_map/ppermute | solution.py:62
  368.3 36.2 %collective-permute-start.41 = (bf16[256,1536]{1,0:T(8,128)(2,1)}, bf16[256,1536]{1,0:T(8,128)(2,1)}, u32[]{:S(2)}, u32[]{:S(2)}) collective-permute-start(bf16[256,1536]{1,0:T(8,128)(2,1)} %get-tuple-element.193), channel_id=1, source_target_pairs={{0,6},{2,4},{4,2},{6,0},{1,7},{3,5},{5,3},{7,1},{8,14},{10,12},{12... | collective-permute-start | bytes 2359304 | tf_op jit(solution)/shard_map/ppermute | solution.py:62
  369.7 36.0 %collective-permute-start.40 = (bf16[256,1536]{1,0:T(8,128)(2,1)S(1)}, bf16[256,1536]{1,0:T(8,128)(2,1)}, u32[]{:S(2)}, u32[]{:S(2)}) collective-permute-start(bf16[256,1536]{1,0:T(8,128)(2,1)S(1)} %get-tuple-element.194), channel_id=1, source_target_pairs={{0,4},{2,6},{4,0},{6,2},{1,5},{3,7},{5,1},{7,3},{8,12},{10,14},{12... | collective-permute-start | bytes 2359304 | tf_op jit(solution)/shard_map/ppermute | solution.py:62
  415.6 37.9 %collective-permute-start.50 = (bf16[4,96,768]{2,1,0:T(8,128)(2,1)S(1)}, bf16[4,96,768]{2,1,0:T(8,128)(2,1)S(1)}, u32[]{:S(2)}, u32[]{:S(2)}) collective-permute-start(bf16[4,96,768]{2,1,0:T(8,128)(2,1)S(1)} %get-tuple-element.200), channel_id=1, source_target_pairs={{0,6},{2,4},{4,2},{6,0},{1,7},{3,5},{5,3},{7,1},{8,14},{10,12},{12... | collective-permute-start | bytes 1769480 | tf_op jit(solution)/shard_map/ppermute | solution.py:62
  422.4 32.4 %collective-permute-start.49 = (bf16[4,96,768]{2,1,0:T(8,128)(2,1)S(1)}, bf16[4,96,768]{2,1,0:T(8,128)(2,1)S(1)}, u32[]{:S(2)}, u32[]{:S(2)}) collective-permute-start(bf16[4,96,768]{2,1,0:T(8,128)(2,1)S(1)} %get-tuple-element.201), channel_id=1, source_target_pairs={{0,4},{2,6},{4,0},{6,2},{1,5},{3,7},{5,1},{7,3},{8,12},{10,14},{12... | collective-permute-start | bytes 1769480 | tf_op jit(solution)/shard_map/ppermute | solution.py:62
  429.3 36.5 %collective-permute-start.47 = (bf16[512,256]{1,0:T(8,128)(2,1)}, bf16[512,256]{1,0:T(8,128)(2,1)}, u32[]{:S(2)}, u32[]{:S(2)}) collective-permute-start(bf16[512,256]{1,0:T(8,128)(2,1)} %get-tuple-element.224), channel_id=1, source_target_pairs={{0,6},{2,4},{4,2},{6,0},{1,7},{3,5},{5,3},{7,1},{8,14},{10,12},{12... | collective-permute-start | bytes 786440 | tf_op jit(solution)/shard_map/ppermute | solution.py:62
  431.3 34.6 %collective-permute-start.46 = (bf16[512,256]{1,0:T(8,128)(2,1)}, bf16[512,256]{1,0:T(8,128)(2,1)}, u32[]{:S(2)}, u32[]{:S(2)}) collective-permute-start(bf16[512,256]{1,0:T(8,128)(2,1)} %get-tuple-element.225), channel_id=1, source_target_pairs={{0,4},{2,6},{4,0},{6,2},{1,5},{3,7},{5,1},{7,3},{8,12},{10,14},{12... | collective-permute-start | bytes 786440 | tf_op jit(solution)/shard_map/ppermute | solution.py:62
  469.8 59.3 %collective-permute-start.57 = (bf16[384,3456]{1,0:T(8,128)(2,1)S(1)}, bf16[384,3456]{1,0:T(8,128)(2,1)}, u32[]{:S(2)}, u32[]{:S(2)}) collective-permute-start(bf16[384,3456]{1,0:T(8,128)(2,1)S(1)} %constant_dynamic-update-slice_fusion.35.refs_0_), channel_id=1, source_target_pairs={{0,4},{2,6},{4,0},{6,2},{1,5},{3,7},{5,1},{7,3},{8,12},{10,14},{12... | collective-permute-start | bytes 7962632 | tf_op jit(solution)/shard_map/ppermute | solution.py:62
  471.4 59.0 %collective-permute-start.56 = (bf16[384,3456]{1,0:T(8,128)(2,1)S(1)}, bf16[384,3456]{1,0:T(8,128)(2,1)}, u32[]{:S(2)}, u32[]{:S(2)}) collective-permute-start(bf16[384,3456]{1,0:T(8,128)(2,1)S(1)} %constant_dynamic-update-slice_fusion.35.refs_0_), channel_id=1, source_target_pairs={{0,2},{2,0},{4,6},{6,4},{1,3},{3,1},{5,7},{7,5},{8,10},{10,8},{12,... | collective-permute-start | bytes 7962632 | tf_op jit(solution)/shard_map/ppermute | solution.py:62
  491.3 32.2 %collective-permute-start.54 = (bf16[704,256]{1,0:T(8,128)(2,1)S(1)}, bf16[704,256]{1,0:T(8,128)(2,1)S(1)}, u32[]{:S(2)}, u32[]{:S(2)}) collective-permute-start(bf16[704,256]{1,0:T(8,128)(2,1)S(1)} %get-tuple-element.221), channel_id=1, source_target_pairs={{0,16},{8,24},{16,0},{24,8},{1,17},{9,25},{17,1},{25,9},{2,18},{10... | collective-permute-start | bytes 1081352 | tf_op jit(solution)/shard_map/ppermute | solution.py:823
  492.8 30.8 %collective-permute-start.53 = (bf16[704,256]{1,0:T(8,128)(2,1)S(1)}, bf16[704,256]{1,0:T(8,128)(2,1)S(1)}, u32[]{:S(2)}, u32[]{:S(2)}) collective-permute-start(bf16[704,256]{1,0:T(8,128)(2,1)S(1)} %get-tuple-element.222), channel_id=1, source_target_pairs={{0,8},{8,16},{16,24},{24,0},{1,9},{9,17},{17,25},{25,1},{2,10},{10... | collective-permute-start | bytes 1081352 | tf_op jit(solution)/shard_map/ppermute | solution.py:823
  535.6 50.2 %collective-permute-start.59 = (bf16[192,3456]{1,0:T(8,128)(2,1)}, bf16[192,3456]{1,0:T(8,128)(2,1)S(1)}, u32[]{:S(2)}, u32[]{:S(2)}) collective-permute-start(bf16[192,3456]{1,0:T(8,128)(2,1)} %slice.319), channel_id=1, source_target_pairs={{0,2},{2,0},{4,6},{6,4},{1,3},{3,1},{5,7},{7,5},{8,10},{10,8},{12,... | collective-permute-start | bytes 3981320 | tf_op jit(solution)/shard_map/ppermute | solution.py:62
  537.1 48.8 %collective-permute-start.58 = (bf16[192,3456]{1,0:T(8,128)(2,1)}, bf16[192,3456]{1,0:T(8,128)(2,1)S(1)}, u32[]{:S(2)}, u32[]{:S(2)}) collective-permute-start(bf16[192,3456]{1,0:T(8,128)(2,1)} %slice.318), channel_id=1, source_target_pairs={{0,4},{2,6},{4,0},{6,2},{1,5},{3,7},{5,1},{7,3},{8,12},{10,14},{12... | collective-permute-start | bytes 3981320 | tf_op jit(solution)/shard_map/ppermute | solution.py:62
  537.7 37.9 %collective-permute-start.64 = (bf16[704,256]{1,0:T(8,128)(2,1)S(1)}, bf16[704,256]{1,0:T(8,128)(2,1)S(1)}, u32[]{:S(2)}, u32[]{:S(2)}) collective-permute-start(bf16[704,256]{1,0:T(8,128)(2,1)S(1)} %pad_maximum_fusion.13.refs_0_), channel_id=1, source_target_pairs={{0,6},{2,4},{4,2},{6,0},{1,7},{3,5},{5,3},{7,1},{8,14},{10,12},{12... | collective-permute-start | bytes 1081352 | tf_op jit(solution)/shard_map/ppermute | solution.py:62
  539.2 42.7 %collective-permute-start.63 = (bf16[704,256]{1,0:T(8,128)(2,1)S(1)}, bf16[704,256]{1,0:T(8,128)(2,1)S(1)}, u32[]{:S(2)}, u32[]{:S(2)}) collective-permute-start(bf16[704,256]{1,0:T(8,128)(2,1)S(1)} %pad_maximum_fusion.13.refs_0_), channel_id=1, source_target_pairs={{0,4},{2,6},{4,0},{6,2},{1,5},{3,7},{5,1},{7,3},{8,12},{10,14},{12... | collective-permute-start | bytes 1081352 | tf_op jit(solution)/shard_map/ppermute | solution.py:62
  541.0 40.9 %collective-permute-start.62 = (bf16[704,256]{1,0:T(8,128)(2,1)S(1)}, bf16[704,256]{1,0:T(8,128)(2,1)S(1)}, u32[]{:S(2)}, u32[]{:S(2)}) collective-permute-start(bf16[704,256]{1,0:T(8,128)(2,1)S(1)} %pad_maximum_fusion.13.refs_0_), channel_id=1, source_target_pairs={{0,2},{2,0},{4,6},{6,4},{1,3},{3,1},{5,7},{7,5},{8,10},{10,8},{12,... | collective-permute-start | bytes 1081352 | tf_op jit(solution)/shard_map/ppermute | solution.py:62
  (98 other events, 1085.0 us)
Sparse Core Ops, SparseCore 0:
  50.4 141.1 all-gather.2
  199.5 68.3 all-gather.4
  275.0 121.6 reduce-scatter.2
  398.9 66.8 reduce-scatter.4

commit v5 on v4

--- a/solution.py
+++ b/solution.py
@@ -105,21 +105,18 @@
 def spread_kernel(spans, width, total, context_ref, *refs):
     *blocks, gate_ref, up_ref, down_ref = refs
     context = context_ref[0]
-    for distance, ref in enumerate(blocks):
-        start = jnp.bitwise_xor(context, distance) * width
-        base = 0
-        for offset, columns in spans:
-            for out in (gate_ref, up_ref, down_ref):
-                for piece in range(0, columns, 128):
-                    place = start + offset + piece
-
-                    @pl.when(place < total)
-                    def _():
-                        out[:, pl.ds(pl.multiple_of(place, 128), 128)] = ref[
-                            :, pl.ds(base + piece, 128)
-                        ].astype(jnp.float32)
-
-                base += columns
+    for index, ref in enumerate(blocks):
+        offset, columns = spans[index % len(spans)]
+        start = jnp.bitwise_xor(context, index // len(spans)) * width + offset
+        for matrix, out in enumerate((gate_ref, up_ref, down_ref)):
+            for piece in range(0, columns, 128):
+                place = start + piece
+
+                @pl.when(place < total)
+                def _():
+                    out[:, pl.ds(pl.multiple_of(place, 128), 128)] = ref[
+                        :, pl.ds(matrix * columns + piece, 128)
+                    ].astype(jnp.float32)
 
 
 def spread(blocks, spans, width, total, context):
@@ -136,46 +133,50 @@
     )(context.reshape(1), *blocks)
 
 
-def spread_far_kernel(spans, place_ref, low_ref, high_ref, *refs):
-    outs = refs[3:]
+def spread_far_kernel(spans, place_ref, *refs):
+    count = 2 * len(spans)
+    outs = refs[count + 3 :]
     late = pl.program_id(0) >= pl.num_programs(0) // 2
-    for side, ref in enumerate((low_ref, high_ref)):
-
-        @pl.when(late == (side == 1))
+    for index, ref in enumerate(refs[:count]):
+        offset, columns = spans[index // 2]
+
+        @pl.when(late == (index % 2 == 1))
         def _():
-            base = 0
-            for offset, columns in spans:
-                for out in outs:
-                    out[:, offset : offset + columns] = ref[:, base : base + columns].astype(
-                        jnp.float32
-                    )
-                    base += columns
-
-
-def spread_far(low, high, wholes, spans, width, place):
+            for matrix, out in enumerate(outs):
+                out[:, offset : offset + columns] = ref[
+                    :, matrix * columns : (matrix + 1) * columns
+                ].astype(jnp.float32)
+
+
+def spread_far(pieces, wholes, spans, width, place):
     rows, total = wholes[0].shape
     steps = 1
     tile = rows // 2
     while tile % 2 == 0 and tile > 96:
         tile //= 2
         steps *= 2
+    maps = (
+        lambda i, p: (jnp.minimum(i, steps - 1), 0),
+        lambda i, p: (jnp.maximum(i - steps, 0), 0),
+    )
     grid_spec = pltpu.PrefetchScalarGridSpec(
         num_scalar_prefetch=1,
         grid=(2 * steps,),
         in_specs=[
-            pl.BlockSpec((tile, low.shape[1]), lambda i, p: (jnp.minimum(i, steps - 1), 0)),
-            pl.BlockSpec((tile, low.shape[1]), lambda i, p: (jnp.maximum(i - steps, 0), 0)),
+            pl.BlockSpec((tile, piece.shape[1]), maps[index % 2])
+            for index, piece in enumerate(pieces)
         ]
         + [pl.BlockSpec(memory_space=pl.ANY)] * 3,
         out_specs=[pl.BlockSpec((tile, width), lambda i, p: (i, p[0]))] * 3,
     )
+    count = len(pieces) + 1
     return pl.pallas_call(
         functools.partial(spread_far_kernel, spans),
         grid_spec=grid_spec,
         out_shape=[jax.ShapeDtypeStruct((rows, total), jnp.float32)] * 3,
-        input_output_aliases={3: 0, 4: 1, 5: 2},
+        input_output_aliases={count: 0, count + 1: 1, count + 2: 2},
         compiler_params=pltpu.CompilerParams(vmem_limit_bytes=40 * 1024 * 1024),
-    )(place.reshape(1), low, high, *wholes)
+    )(place.reshape(1), *pieces, *wholes)
 
 
 def place_kernel(count, part, context_ref, *refs):
@@ -781,9 +782,8 @@
         lax.dynamic_index_in_dim(grad_quarters, d, axis=0, keepdims=False) for d in distances
     ]
     exchanged = context_send(relative_grads)
-    exchanged, grad_wo, *ff_sums = bar((exchanged, grad_wo, *ff_sums))
-    ff_grads_own = jnp.concatenate(ff_sums, axis=1)
-    ff_near = context_gather_start(ff_grads_own)
+    exchanged, grad_wo, ff_sums[0] = bar((exchanged, grad_wo, ff_sums[0]))
+    early_near = context_gather_start(ff_sums[0])
     normed_gradient = sum(
         contract_last(grads, block) for grads, block in zip(relative_grads, quarter_blocks)
     )
@@ -813,6 +813,8 @@
         return value[..., :count, :] + value[..., count:, :]
 
     me = lax.axis_index("shard")
+    small, early_near, ff_sums[1] = bar((small, early_near, ff_sums[1]))
+    late_near = context_gather_start(ff_sums[1])
     terms = attention_terms(first_normed, exchanged, grad_wo, small.reshape(-1, quarter), core)
     if shards > 4:
         received = [lax.all_to_all(terms, "shard", 0, 0)[k] for k in range(shards)]
@@ -826,8 +828,9 @@
                     [(i, (i + k) % shards) for i in range(shards)],
                 )
             )
-    received, ff_near = bar((received, ff_near))
-    ff_blocks = context_gather_end(ff_grads_own, *ff_near)
+    received, late_near = bar((received, late_near))
+    early_blocks = context_gather_end(ff_sums[0], *early_near)
+    late_blocks = context_gather_end(ff_sums[1], *late_near)
     output = core_join((residual + mlp).astype(narrow_dtype))
     count = depth + groups * part
     weight_sums = sum(value[:count].astype(jnp.float32) for value in received).astype(narrow_dtype)
@@ -836,11 +839,13 @@
     small = sum(unpacked(block[count:]) for block in blocks).reshape(-1)
     grad_wq, grad_wk, grad_wv, grad_wo = place_attention(blocks, depth, part, qwp, kwp, context)
 
-    wholes = spread([block[0] for block in ff_blocks[:3]], tuple(spans), width, ffp, context)
+    near = [blocks[k][0] for k in range(3) for blocks in (early_blocks, late_blocks)]
+    wholes = spread(near, tuple(spans), width, ffp, context)
+    far = early_blocks[3] + late_blocks[3]
     far, wholes, output, source_gradient, small, grad_wq = bar(
-        (ff_blocks[3], wholes, output, source_gradient, small, grad_wq)
-    )
-    grad_wg, grad_wu, grad_wd = spread_far(*far, wholes, tuple(spans), width, distances[3])
+        (far, wholes, output, source_gradient, small, grad_wq)
+    )
+    grad_wg, grad_wu, grad_wd = spread_far(far, wholes, tuple(spans), width, distances[3])
 
     edges = [0, model, 2 * model, 2 * model + qwp, 2 * model + qwp + kwp, small.shape[0]]
     sums = [small[edges[i] : edges[i + 1]] for i in range(5)]

time: 602 us -> 608 us (level)
  waiting for transfers between devices: 177 us -> 185 us
  local copies, waits for them, and re-layouts: 80.4 us -> 73.7 us
    ppermute x56 -> x60, waiting for transfers between devices: 141 us -> 159 us  [swap(): return lax.ppermute(value, axis, [(i, i ^ distance) for i in range(size)])]
    reduce_scatter x2, waiting for transfers between devices: 9.91 us -> 0.01 us  [over_shard(): lax.psum_scatter(value.reshape(shards, depth, value.shape[1]), 'shard', s...]
    unnamed x152 -> x169, local copies, waits for them, and re-layouts: 30.2 us -> 26.1 us
    ppermute x56 -> x60, starting transfers between devices: 57.9 us -> 61.6 us  [swap(): return lax.ppermute(value, axis, [(i, i ^ distance) for i in range(size)])]
  transfers between devices with their start and end apart: 69 -> 73, of which waited for: 27 -> 29; matrix products, arithmetic and copies ran while one was open for 22% -> 23% of each run, Pallas kernels for 28% -> 28%
where the time goes in v5:
time: 608 us; the launch traced here: 601 us
  waiting for transfers between devices  185 us (30%)
  Pallas kernels  170 us (28%)
  starting transfers between devices  76.9 us (13%)
  local copies, waits for them, and re-layouts  73.7 us (12%)
  other arithmetic  60.4 us (10%)
  matrix products  19.9 us (3%)
  between operations  15.7 us (3%)
    ppermute x60, waiting for transfers between devices, swap(): return lax.ppermute(value, axis, [(i, i ^ distance) for i in range(size)])  159 us
    pallas_call x2, Pallas kernels, feed_forward(): pl.pallas_call(functools.partial(ff_kernel, columns // 3, not previous),...  69.4 us
    ppermute x60, starting transfers between devices, swap(): return lax.ppermute(value, axis, [(i, i ^ distance) for i in range(size)])  61.6 us
    pallas_call x2, Pallas kernels, ff_grads(): pl.pallas_call(functools.partial(ff_grads_kernel, columns // 3), grid=(mo...  34.9 us
    pallas_call x1, Pallas kernels, attend_back(): pl.pallas_call(attend_back_kernel, grid=(rows // tile, heads), in_specs=[...  27.1 us
    ppermute x3, waiting for transfers between devices, body(): lax.ppermute(lax.dynamic_index_in_dim(terms, lax.rem(me + k, shards), kee...  26.1 us
    unnamed x169, local copies, waits for them, and re-layouts  26.1 us
    pallas_call x1, Pallas kernels, attend(): pl.pallas_call(attend_kernel, grid=(rows // tile, heads), in_specs=[query...  16.1 us
  transfers between devices with their start and end apart: 73, of which 29 were waited for; matrix products, arithmetic and copies ran while one was open for 23% of the time, Pallas kernels for 28%

profile of v5, /device:TPU:0, one launch (start us, length us, event | category | flops | bytes accessed | tf_op | source)
XLA Modules:
  0.0 601.3 jit_solution(6154973897924485263)
XLA Ops:
  43.6 3.4 collective-permute-done.2
  50.7 5.3 multiply_cosine_fusion
  61.6 4.6 constant_dynamic-update-slice_fusion.5.normed_ref
  75.3 5.5 fusion.57
  109.1 6.7 %collective-permute-done.9 = bf16[512,256]{1,0:T(8,128)(2,1)S(1)} collective-permute-done((bf16[512,256]{1,0:T(8,128)(2,1)}, bf16[512,256]{1,0:T(8,128)(2,1)S(1)}, u32[]{:S(2)}, u32[]{:S(2)}) %collective-permute-start.9) | collective-permute-done | bytes 262176 | tf_op jit(solution)/shard_map/ppermute | solution.py:62
  119.6 16.1 %shard_map.272 = (bf16[512,768]{1,0:T(8,128)(2,1)}, f32[8,512]{1,0:T(8,128)}) custom-call(bf16[4,512,256]{2,1,0:T(8,128)(2,1)} %copy-done.35, bf16[2048,256]{1,0:T(8,128)(2,1)} %pad_maximum_fusion.6.key_ref.value_ref, bf16[2048,256]{1,0:T(8,128)(2,1)} %pad_maximum_fusion.6.key_ref.value_ref, s32[1,512]{1,0:T(1,128)} %bitcast.193, ...), custom_call_target="tpu_custom_call" | custom-call | flops 6442450944 | bytes 2359296 | tf_op jit(solution)/shard_map/pallas_call | solution.py:450
  137.4 8.2 %collective-permute-done.17 = bf16[2,96,768]{2,1,0:T(8,128)(2,1)S(1)} collective-permute-done((bf16[2,96,768]{2,1,0:T(8,128)(2,1)S(1)}, bf16[2,96,768]{2,1,0:T(8,128)(2,1)S(1)}, u32[]{:S(2)}, u32[]{:S(2)}) %collective-permute-start.17) | collective-permute-done | bytes 294944 | tf_op jit(solution)/shard_map/ppermute | solution.py:62
  145.7 4.2 collective-permute-done.16
  159.7 5.7 collective-permute-done.26
  167.1 14.4 %collective-permute-done.20 = bf16[256,1536]{1,0:T(8,128)(2,1)S(1)} collective-permute-done((bf16[256,1536]{1,0:T(8,128)(2,1)S(1)}, bf16[256,1536]{1,0:T(8,128)(2,1)S(1)}, u32[]{:S(2)}, u32[]{:S(2)}) %collective-permute-start.20) | collective-permute-done | bytes 786464 | tf_op jit(solution)/shard_map/ppermute | solution.py:62
  185.8 6.6 %collective-permute-done.21 = bf16[128,1536]{1,0:T(8,128)(2,1)S(1)} collective-permute-done((bf16[128,1536]{1,0:T(8,128)(2,1)S(1)}, bf16[128,1536]{1,0:T(8,128)(2,1)S(1)}, u32[]{:S(2)}, u32[]{:S(2)}) %collective-permute-start.21) | collective-permute-done | bytes 393248 | tf_op jit(solution)/shard_map/ppermute | solution.py:62
  202.1 4.0 constant_dynamic-update-slice_fusion.29.gradient_ref
  206.2 4.0 constant_dynamic-update-slice_fusion.18.normed_ref
  213.7 41.2 %shard_map.273 = (bf16[2048,2304]{1,0:T(8,128)(2,1)}, bf16[1024,1536]{1,0:T(8,128)(2,1)}, bf16[1024,1536]{1,0:T(8,128)(2,1)}, bf16[1024,1536]{1,0:T(8,128)(2,1)}, bf16[1024,1536]{1,0:T(8,128)(2,1)}) custom-call(bf16[2048,1536]{1,0:T(8,128)(2,1)} %constant_dynamic-update-slice_fusion.18.normed_ref, ...), custom_call_target="tpu_custom_call" | custom-call | flops 28991029248 | bytes 41680896 | tf_op jit(solution)/shard_map/pallas_call | solution.py:343
  254.9 21.4 %shard_map.274 = bf16[1536,2304]{1,0:T(8,128)(2,1)} custom-call(bf16[2048,1536]{1,0:T(8,128)(2,1)} %constant_dynamic-update-slice_fusion.18.normed_ref, bf16[2048,1536]{1,0:T(8,128)(2,1)} %constant_dynamic-update-slice_fusion.29.gradient_ref, bf16[2048,2304]{1,0:T(8,128)(2,1)} %get-tuple-element.104.acts_ref), custom_call_target="tpu_custom_call" | custom-call | flops 14495514624 | bytes 29097984 | tf_op jit(solution)/shard_map/pallas_call | solution.py:376
  276.4 28.2 %shard_map.275 = (bf16[2048,1152]{1,0:T(8,128)(2,1)}, bf16[1024,1536]{1,0:T(8,128)(2,1)}, bf16[1024,1536]{1,0:T(8,128)(2,1)}, bf16[1024,1536]{1,0:T(8,128)(2,1)}, bf16[1024,1536]{1,0:T(8,128)(2,1)}) custom-call(bf16[2048,1536]{1,0:T(8,128)(2,1)} %constant_dynamic-update-slice_fusion.18.normed_ref, ...), custom_call_target="tpu_custom_call" | custom-call | flops 14495514624 | bytes 33423360 | tf_op jit(solution)/shard_map/pallas_call | solution.py:343
  304.6 13.4 %shard_map.276 = bf16[1536,1152]{1,0:T(8,128)(2,1)} custom-call(bf16[2048,1536]{1,0:T(8,128)(2,1)} %constant_dynamic-update-slice_fusion.18.normed_ref, bf16[2048,1536]{1,0:T(8,128)(2,1)} %constant_dynamic-update-slice_fusion.29.gradient_ref, bf16[2048,1152]{1,0:T(8,128)(2,1)} %get-tuple-element.115.acts_ref), custom_call_target="tpu_custom_call" | custom-call | flops 7247757312 | bytes 20840448 | tf_op jit(solution)/shard_map/pallas_call | solution.py:376
  324.3 8.5 %collective-permute-done.35 = bf16[128,1536]{1,0:T(8,128)(2,1)S(1)} collective-permute-done((bf16[128,1536]{1,0:T(8,128)(2,1)S(1)}, bf16[128,1536]{1,0:T(8,128)(2,1)S(1)}, u32[]{:S(2)}, u32[]{:S(2)}) %collective-permute-start.35) | collective-permute-done | bytes 393248 | tf_op jit(solution)/shard_map/ppermute | solution.py:62
  336.6 16.8 %collective-permute-done.36 = bf16[256,1536]{1,0:T(8,128)(2,1)S(1)} collective-permute-done((bf16[256,1536]{1,0:T(8,128)(2,1)S(1)}, bf16[256,1536]{1,0:T(8,128)(2,1)S(1)}, u32[]{:S(2)}, u32[]{:S(2)}) %collective-permute-start.36) | collective-permute-done | bytes 786464 | tf_op jit(solution)/shard_map/ppermute | solution.py:62
  358.7 3.1 collective-permute-done.37
  372.6 27.1 %shard_map.277 = (bf16[3,512,256]{2,1,0:T(8,128)(2,1)}, f32[2048,256]{1,0:T(8,128)}) custom-call(bf16[4,512,256]{2,1,0:T(8,128)(2,1)} %copy-done.35, bf16[512,768]{1,0:T(8,128)(2,1)} %convolution_convert_fusion.1.grad_ref, f32[512,128]{1,0:T(8,128)} %get-tuple-element.298.cosine_ref, f32[512,128]{1,0:T(8,128)} %get-tuple-element.299.sine_ref, ...), custom_call_target="tpu_custom_call" | custom-call | flops 16106127360 | bytes 2359296 | tf_op jit(solution)/shard_map/pallas_call | solution.py:522
  399.7 4.4 convolution_convert_fusion
  407.1 3.3 fusion.16
  420.1 3.8 collective-permute-done.43
  425.3 3.2 collective-permute-done.42
  442.7 12.1 %collective-permute-done.52 = bf16[4,96,768]{2,1,0:T(8,128)(2,1)S(1)} collective-permute-done((bf16[4,96,768]{2,1,0:T(8,128)(2,1)S(1)}, bf16[4,96,768]{2,1,0:T(8,128)(2,1)S(1)}, u32[]{:S(2)}, u32[]{:S(2)}) %collective-permute-start.52) | collective-permute-done | bytes 589856 | tf_op jit(solution)/shard_map/ppermute | solution.py:62
  472.8 30.3 %collective-permute-done.54.refs_4_ = bf16[384,2304]{1,0:T(8,128)(2,1)S(1)} collective-permute-done((bf16[384,2304]{1,0:T(8,128)(2,1)}, bf16[384,2304]{1,0:T(8,128)(2,1)S(1)}, u32[]{:S(2)}, u32[]{:S(2)}) %collective-permute-start.54) | collective-permute-done | bytes 1769504 | tf_op jit(solution)/shard_map/ppermute | solution.py:62
  506.5 6.1 %shard_map.278 = bf16[4,704,256]{2,1,0:T(8,128)(2,1)} custom-call(s32[1]{0:T(128)} %bitcast.59.core_ref, bf16[2048,1536]{1,0:T(8,128)(2,1)} %constant_dynamic-update-slice_fusion.5.normed_ref, bf16[512,256]{1,0:T(8,128)(2,1)} %copy-done.31, bf16[512,256]{1,0:T(8,128)(2,1)} %copy-done.47, bf16[512,256]{1,0:T(8,128)(2,1)} %copy-done.46, ...), custom_call_target="tpu_custom_call" | custom-call | flops 1610612736 | bytes 8781824 | tf_op jit(solution)/shard_map/pallas_call | solution.py:283
  519.0 5.3 collective-permute-done.59
  524.2 20.8 %collective-permute-done.58 = bf16[704,256]{1,0:T(8,128)(2,1)S(1)} collective-permute-done((bf16[704,256]{1,0:T(8,128)(2,1)S(1)}, bf16[704,256]{1,0:T(8,128)(2,1)S(1)}, u32[]{:S(2)}, u32[]{:S(2)}) %collective-permute-start.58) | collective-permute-done | bytes 360480 | tf_op jit(solution)/shard_map/ppermute | solution.py:825
  557.6 10.5 %shard_map.279 = (f32[384,4480]{1,0:T(8,128)}, f32[384,4480]{1,0:T(8,128)}, f32[384,4480]{1,0:T(8,128)}) custom-call(s32[1]{0:T(128)} %bitcast.64.context_ref, bf16[384,2304]{1,0:T(8,128)(2,1)} %bitcast.42.refs_0_, bf16[384,1152]{1,0:T(8,128)(2,1)S(1)} %bitcast.155, bf16[384,2304]{1,0:T(8,128)(2,1)S(1)} %collective-permute-done.53.refs_2_, ...), custom_call_target="tpu_custom_call" | custom-call | tf_op jit(solution)/shard_map/pallas_call | solution.py:125
  570.5 12.5 %collective-permute-done.66.refs_1_ = bf16[704,256]{1,0:T(8,128)(2,1)S(1)} collective-permute-done((bf16[704,256]{1,0:T(8,128)(2,1)S(1)}, bf16[704,256]{1,0:T(8,128)(2,1)S(1)}, u32[]{:S(2)}, u32[]{:S(2)}) %collective-permute-start.66) | collective-permute-done | bytes 360480 | tf_op jit(solution)/shard_map/ppermute | solution.py:62
  (451 shorter events, 224.7 us)
Async XLA Ops:
  7.2 206.5 %all-gather.3.cloned.1.call-start = ((), (), s32[]{:S(2)}) async-start(), calls=%async_computation.2 | async-start | bytes 8847360 | tf_op jit(solution)/shard_map/all_gather | solution.py:717
  20.5 38.8 %collective-permute-start.6 = (bf16[384,512]{1,0:T(8,128)(2,1)}, bf16[384,512]{1,0:T(8,128)(2,1)}, u32[]{:S(2)}, u32[]{:S(2)}) collective-permute-start(bf16[384,512]{1,0:T(8,128)(2,1)} %pad_maximum_fusion.12), channel_id=1, source_target_pairs={{0,16},{8,24},{16,0},{24,8},{1,17},{9,25},{17,1},{25,9},{2,18},{10... | collective-permute-start | bytes 1179656 | tf_op jit(solution)/shard_map/ppermute | solution.py:550
  23.1 35.1 %collective-permute-start.5 = (bf16[384,512]{1,0:T(8,128)(2,1)}, bf16[384,512]{1,0:T(8,128)(2,1)}, u32[]{:S(2)}, u32[]{:S(2)}) collective-permute-start(bf16[384,512]{1,0:T(8,128)(2,1)} %pad_maximum_fusion.12), channel_id=1, source_target_pairs={{0,8},{8,16},{16,24},{24,0},{1,9},{9,17},{17,25},{25,1},{2,10},{10... | collective-permute-start | bytes 1179656 | tf_op jit(solution)/shard_map/ppermute | solution.py:550
  24.7 35.8 %collective-permute-start.7 = (bf16[384,512]{1,0:T(8,128)(2,1)}, bf16[384,512]{1,0:T(8,128)(2,1)}, u32[]{:S(2)}, u32[]{:S(2)}) collective-permute-start(bf16[384,512]{1,0:T(8,128)(2,1)} %pad_maximum_fusion.12), channel_id=1, source_target_pairs={{0,24},{8,0},{16,8},{24,16},{1,25},{9,1},{17,9},{25,17},{2,26},{10... | collective-permute-start | bytes 1179656 | tf_op jit(solution)/shard_map/ppermute | solution.py:550
  50.3 226.1 %all-gather.5.cloned.1.call-start = ((), (), s32[]{:S(2)}) async-start(), calls=%async_computation.3 | async-start | bytes 4423680 | tf_op jit(solution)/shard_map/all_gather | solution.py:717
  67.8 37.1 %collective-permute-start.12 = (bf16[96,768]{1,0:T(8,128)(2,1)}, bf16[96,768]{1,0:T(8,128)(2,1)}, u32[]{:S(2)}, u32[]{:S(2)}) collective-permute-start(bf16[96,768]{1,0:T(8,128)(2,1)} %get-tuple-element.191), channel_id=1, source_target_pairs={{0,16},{8,24},{16,0},{24,8},{1,17},{9,25},{17,1},{25,9},{2,18},{10... | collective-permute-start | bytes 442376 | tf_op jit(solution)/shard_map/ppermute | solution.py:550
  70.4 31.9 %collective-permute-start.11 = (bf16[96,768]{1,0:T(8,128)(2,1)}, bf16[96,768]{1,0:T(8,128)(2,1)}, u32[]{:S(2)}, u32[]{:S(2)}) collective-permute-start(bf16[96,768]{1,0:T(8,128)(2,1)} %get-tuple-element.191), channel_id=1, source_target_pairs={{0,8},{8,16},{16,24},{24,0},{1,9},{9,17},{17,25},{25,1},{2,10},{10... | collective-permute-start | bytes 442376 | tf_op jit(solution)/shard_map/ppermute | solution.py:550
  72.0 33.8 %collective-permute-start.13 = (bf16[96,768]{1,0:T(8,128)(2,1)}, bf16[96,768]{1,0:T(8,128)(2,1)}, u32[]{:S(2)}, u32[]{:S(2)}) collective-permute-start(bf16[96,768]{1,0:T(8,128)(2,1)} %get-tuple-element.191), channel_id=1, source_target_pairs={{0,24},{8,0},{16,8},{24,16},{1,25},{9,1},{17,9},{25,17},{2,26},{10... | collective-permute-start | bytes 442376 | tf_op jit(solution)/shard_map/ppermute | solution.py:550
  106.8 28.9 %collective-permute-start.15 = (bf16[4,96,768]{2,1,0:T(8,128)(2,1)S(1)}, bf16[4,96,768]{2,1,0:T(8,128)(2,1)S(1)}, u32[]{:S(2)}, u32[]{:S(2)}) collective-permute-start(bf16[4,96,768]{2,1,0:T(8,128)(2,1)S(1)} %bitcast_dynamic-update-slice_fusion.10), channel_id=1, source_target_pairs={{0,4},{2,6},{4,0},{6,2},{1,5},{3,7},{5,1},{7,3},{8,12},{10,14},{12... | collective-permute-start | bytes 1769480 | tf_op jit(solution)/shard_map/ppermute | solution.py:62
  117.0 34.7 %collective-permute-start.25 = (bf16[256,1536]{1,0:T(8,128)(2,1)S(1)}, bf16[256,1536]{1,0:T(8,128)(2,1)S(1)}, u32[]{:S(2)}, u32[]{:S(2)}) collective-permute-start(bf16[256,1536]{1,0:T(8,128)(2,1)S(1)} %get-tuple-element.185), channel_id=1, source_target_pairs={{0,4},{2,6},{4,0},{6,2},{1,5},{3,7},{5,1},{7,3},{8,12},{10,14},{12... | collective-permute-start | bytes 2359304 | tf_op jit(solution)/shard_map/ppermute | solution.py:62
  118.3 35.1 %collective-permute-start.24 = (bf16[256,1536]{1,0:T(8,128)(2,1)S(1)}, bf16[256,1536]{1,0:T(8,128)(2,1)S(1)}, u32[]{:S(2)}, u32[]{:S(2)}) collective-permute-start(bf16[256,1536]{1,0:T(8,128)(2,1)S(1)} %get-tuple-element.185), channel_id=1, source_target_pairs={{0,2},{2,0},{4,6},{6,4},{1,3},{3,1},{5,7},{7,5},{8,10},{10,8},{12,... | collective-permute-start | bytes 2359304 | tf_op jit(solution)/shard_map/ppermute | solution.py:62
  167.0 35.1 %collective-permute-start.28 = (bf16[1024,1536]{1,0:T(8,128)(2,1)}, bf16[1024,1536]{1,0:T(8,128)(2,1)}, u32[]{:S(2)}, u32[]{:S(2)}) collective-permute-start(bf16[1024,1536]{1,0:T(8,128)(2,1)} %get-tuple-element.262), channel_id=1, source_target_pairs={{0,1},{1,0},{2,3},{3,2},{4,5},{5,4},{6,7},{7,6},{8,9},{9,8},{10,11... | collective-permute-start | bytes 9437192 | tf_op jit(solution)/shard_map/ppermute | solution.py:62
  200.8 209.5 %reduce-scatter.3.cloned.1.call-start = ((), (), s32[]{:S(2)}) async-start(), calls=%async_computation.4 | async-start | bytes 8847360 | tf_op jit(solution)/shard_map/reduce_scatter | solution.py:743
  210.2 44.7 %collective-permute-start.31 = (bf16[1536,256]{1,0:T(8,128)(2,1)S(1)}, bf16[1536,256]{1,0:T(8,128)(2,1)}, u32[]{:S(2)}, u32[]{:S(2)}) collective-permute-start(bf16[1536,256]{1,0:T(8,128)(2,1)S(1)} %slice.381), channel_id=1, source_target_pairs={{0,6},{2,4},{4,2},{6,0},{1,7},{3,5},{5,3},{7,1},{8,14},{10,12},{12... | collective-permute-start | bytes 2359304 | tf_op jit(solution)/shard_map/ppermute | solution.py:62
  212.6 42.2 %collective-permute-start.30 = (bf16[1536,256]{1,0:T(8,128)(2,1)S(1)}, bf16[1536,256]{1,0:T(8,128)(2,1)}, u32[]{:S(2)}, u32[]{:S(2)}) collective-permute-start(bf16[1536,256]{1,0:T(8,128)(2,1)S(1)} %slice.381), channel_id=1, source_target_pairs={{0,4},{2,6},{4,0},{6,2},{1,5},{3,7},{5,1},{7,3},{8,12},{10,14},{12... | collective-permute-start | bytes 2359304 | tf_op jit(solution)/shard_map/ppermute | solution.py:62
  213.2 41.7 %collective-permute-start.29 = (bf16[1536,256]{1,0:T(8,128)(2,1)S(1)}, bf16[1536,256]{1,0:T(8,128)(2,1)}, u32[]{:S(2)}, u32[]{:S(2)}) collective-permute-start(bf16[1536,256]{1,0:T(8,128)(2,1)S(1)} %slice.381), channel_id=1, source_target_pairs={{0,2},{2,0},{4,6},{6,4},{1,3},{3,1},{5,7},{7,5},{8,10},{10,8},{12,... | collective-permute-start | bytes 2359304 | tf_op jit(solution)/shard_map/ppermute | solution.py:62
  276.4 196.4 %reduce-scatter.5.cloned.1.call-start = ((), (), s32[]{:S(2)}) async-start(), calls=%async_computation.5 | async-start | bytes 4423680 | tf_op jit(solution)/shard_map/reduce_scatter | solution.py:743
  369.1 35.0 %collective-permute-start.39 = (bf16[256,1536]{1,0:T(8,128)(2,1)}, bf16[256,1536]{1,0:T(8,128)(2,1)}, u32[]{:S(2)}, u32[]{:S(2)}) collective-permute-start(bf16[256,1536]{1,0:T(8,128)(2,1)} %get-tuple-element.202), channel_id=1, source_target_pairs={{0,2},{2,0},{4,6},{6,4},{1,3},{3,1},{5,7},{7,5},{8,10},{10,8},{12,... | collective-permute-start | bytes 2359304 | tf_op jit(solution)/shard_map/ppermute | solution.py:62
  369.7 36.3 %collective-permute-start.41 = (bf16[256,1536]{1,0:T(8,128)(2,1)}, bf16[256,1536]{1,0:T(8,128)(2,1)}, u32[]{:S(2)}, u32[]{:S(2)}) collective-permute-start(bf16[256,1536]{1,0:T(8,128)(2,1)} %get-tuple-element.203), channel_id=1, source_target_pairs={{0,6},{2,4},{4,2},{6,0},{1,7},{3,5},{5,3},{7,1},{8,14},{10,12},{12... | collective-permute-start | bytes 2359304 | tf_op jit(solution)/shard_map/ppermute | solution.py:62
  371.1 36.0 %collective-permute-start.40 = (bf16[256,1536]{1,0:T(8,128)(2,1)S(1)}, bf16[256,1536]{1,0:T(8,128)(2,1)}, u32[]{:S(2)}, u32[]{:S(2)}) collective-permute-start(bf16[256,1536]{1,0:T(8,128)(2,1)S(1)} %get-tuple-element.204), channel_id=1, source_target_pairs={{0,4},{2,6},{4,0},{6,2},{1,5},{3,7},{5,1},{7,3},{8,12},{10,14},{12... | collective-permute-start | bytes 2359304 | tf_op jit(solution)/shard_map/ppermute | solution.py:62
  417.0 37.9 %collective-permute-start.52 = (bf16[4,96,768]{2,1,0:T(8,128)(2,1)S(1)}, bf16[4,96,768]{2,1,0:T(8,128)(2,1)S(1)}, u32[]{:S(2)}, u32[]{:S(2)}) collective-permute-start(bf16[4,96,768]{2,1,0:T(8,128)(2,1)S(1)} %get-tuple-element.210), channel_id=1, source_target_pairs={{0,6},{2,4},{4,2},{6,0},{1,7},{3,5},{5,3},{7,1},{8,14},{10,12},{12... | collective-permute-start | bytes 1769480 | tf_op jit(solution)/shard_map/ppermute | solution.py:62
  423.9 31.8 %collective-permute-start.51 = (bf16[4,96,768]{2,1,0:T(8,128)(2,1)S(1)}, bf16[4,96,768]{2,1,0:T(8,128)(2,1)S(1)}, u32[]{:S(2)}, u32[]{:S(2)}) collective-permute-start(bf16[4,96,768]{2,1,0:T(8,128)(2,1)S(1)} %get-tuple-element.211), channel_id=1, source_target_pairs={{0,4},{2,6},{4,0},{6,2},{1,5},{3,7},{5,1},{7,3},{8,12},{10,14},{12... | collective-permute-start | bytes 1769480 | tf_op jit(solution)/shard_map/ppermute | solution.py:62
  462.4 40.7 %collective-permute-start.54 = (bf16[384,2304]{1,0:T(8,128)(2,1)}, bf16[384,2304]{1,0:T(8,128)(2,1)S(1)}, u32[]{:S(2)}, u32[]{:S(2)}) collective-permute-start(bf16[384,2304]{1,0:T(8,128)(2,1)} %bitcast.42.refs_0_), channel_id=1, source_target_pairs={{0,4},{2,6},{4,0},{6,2},{1,5},{3,7},{5,1},{7,3},{8,12},{10,14},{12... | collective-permute-start | bytes 5308424 | tf_op jit(solution)/shard_map/ppermute | solution.py:62
  463.2 40.5 %collective-permute-start.53 = (bf16[384,2304]{1,0:T(8,128)(2,1)}, bf16[384,2304]{1,0:T(8,128)(2,1)S(1)}, u32[]{:S(2)}, u32[]{:S(2)}) collective-permute-start(bf16[384,2304]{1,0:T(8,128)(2,1)} %bitcast.42.refs_0_), channel_id=1, source_target_pairs={{0,2},{2,0},{4,6},{6,4},{1,3},{3,1},{5,7},{7,5},{8,10},{10,8},{12,... | collective-permute-start | bytes 5308424 | tf_op jit(solution)/shard_map/ppermute | solution.py:62
  468.6 46.6 %collective-permute-start.64 = (bf16[256,1536]{1,0:T(8,128)(2,1)}, bf16[256,1536]{1,0:T(8,128)(2,1)}, u32[]{:S(2)}, u32[]{:S(2)}) collective-permute-start(bf16[256,1536]{1,0:T(8,128)(2,1)} %get-tuple-element.225), channel_id=1, source_target_pairs={{0,1},{1,0},{2,3},{3,2},{4,5},{5,4},{6,7},{7,6},{8,9},{9,8},{10,11... | collective-permute-start | bytes 2359304 | tf_op jit(solution)/shard_map/ppermute | solution.py:62
  503.7 41.4 %collective-permute-start.61 = (bf16[384,1152]{1,0:T(8,128)(2,1)}, bf16[384,1152]{1,0:T(8,128)(2,1)}, u32[]{:S(2)}, u32[]{:S(2)}) collective-permute-start(bf16[384,1152]{1,0:T(8,128)(2,1)} %bitcast.153), channel_id=1, source_target_pairs={{0,4},{2,6},{4,0},{6,2},{1,5},{3,7},{5,1},{7,3},{8,12},{10,14},{12... | collective-permute-start | bytes 2654216 | tf_op jit(solution)/shard_map/ppermute | solution.py:62
  504.9 40.2 %collective-permute-start.60 = (bf16[384,1152]{1,0:T(8,128)(2,1)}, bf16[384,1152]{1,0:T(8,128)(2,1)}, u32[]{:S(2)}, u32[]{:S(2)}) collective-permute-start(bf16[384,1152]{1,0:T(8,128)(2,1)} %bitcast.154), channel_id=1, source_target_pairs={{0,2},{2,0},{4,6},{6,4},{1,3},{3,1},{5,7},{7,5},{8,10},{10,8},{12,... | collective-permute-start | bytes 2654216 | tf_op jit(solution)/shard_map/ppermute | solution.py:62
  514.4 30.6 %collective-permute-start.58 = (bf16[704,256]{1,0:T(8,128)(2,1)S(1)}, bf16[704,256]{1,0:T(8,128)(2,1)S(1)}, u32[]{:S(2)}, u32[]{:S(2)}) collective-permute-start(bf16[704,256]{1,0:T(8,128)(2,1)S(1)} %get-tuple-element.231), channel_id=1, source_target_pairs={{0,16},{8,24},{16,0},{24,8},{1,17},{9,25},{17,1},{25,9},{2,18},{10... | collective-permute-start | bytes 1081352 | tf_op jit(solution)/shard_map/ppermute | solution.py:825
  515.3 29.8 %collective-permute-start.57 = (bf16[704,256]{1,0:T(8,128)(2,1)S(1)}, bf16[704,256]{1,0:T(8,128)(2,1)S(1)}, u32[]{:S(2)}, u32[]{:S(2)}) collective-permute-start(bf16[704,256]{1,0:T(8,128)(2,1)S(1)} %get-tuple-element.232), channel_id=1, source_target_pairs={{0,8},{8,16},{16,24},{24,0},{1,9},{9,17},{17,25},{25,1},{2,10},{10... | collective-permute-start | bytes 1081352 | tf_op jit(solution)/shard_map/ppermute | solution.py:825
  551.3 35.5 %collective-permute-start.56 = (bf16[192,2304]{1,0:T(8,128)(2,1)}, bf16[192,2304]{1,0:T(8,128)(2,1)S(1)}, u32[]{:S(2)}, u32[]{:S(2)}) collective-permute-start(bf16[192,2304]{1,0:T(8,128)(2,1)} %slice.325), channel_id=1, source_target_pairs={{0,2},{2,0},{4,6},{6,4},{1,3},{3,1},{5,7},{7,5},{8,10},{10,8},{12,... | collective-permute-start | bytes 2654216 | tf_op jit(solution)/shard_map/ppermute | solution.py:62
  552.1 34.7 %collective-permute-start.55 = (bf16[192,2304]{1,0:T(8,128)(2,1)}, bf16[192,2304]{1,0:T(8,128)(2,1)S(1)}, u32[]{:S(2)}, u32[]{:S(2)}) collective-permute-start(bf16[192,2304]{1,0:T(8,128)(2,1)} %slice.324), channel_id=1, source_target_pairs={{0,4},{2,6},{4,0},{6,2},{1,5},{3,7},{5,1},{7,3},{8,12},{10,14},{12... | collective-permute-start | bytes 2654216 | tf_op jit(solution)/shard_map/ppermute | solution.py:62
  553.0 30.0 %collective-permute-start.66 = (bf16[704,256]{1,0:T(8,128)(2,1)S(1)}, bf16[704,256]{1,0:T(8,128)(2,1)S(1)}, u32[]{:S(2)}, u32[]{:S(2)}) collective-permute-start(bf16[704,256]{1,0:T(8,128)(2,1)S(1)} %pad_maximum_fusion.13.refs_0_), channel_id=1, source_target_pairs={{0,2},{2,0},{4,6},{6,4},{1,3},{3,1},{5,7},{7,5},{8,10},{10,8},{12,... | collective-permute-start | bytes 1081352 | tf_op jit(solution)/shard_map/ppermute | solution.py:62
  (111 other events, 1829.1 us)
Sparse Core Ops, SparseCore 0:
  50.4 141.1 all-gather.2
  201.0 68.3 all-gather.4
  276.5 121.6 reduce-scatter.2
  400.4 66.8 reduce-scatter.4

commit v6 on v4

--- a/solution.py
+++ b/solution.py
@@ -826,7 +826,6 @@
                     [(i, (i + k) % shards) for i in range(shards)],
                 )
             )
-    received, ff_near = bar((received, ff_near))
     ff_blocks = context_gather_end(ff_grads_own, *ff_near)
     output = core_join((residual + mlp).astype(narrow_dtype))
     count = depth + groups * part

time: 602 us -> 610 us (1.013)
  waiting for transfers between devices: 177 us -> 188 us
  local copies, waits for them, and re-layouts: 80.4 us -> 71 us
    ppermute x56, waiting for transfers between devices: 141 us -> 152 us  [swap(): return lax.ppermute(value, axis, [(i, i ^ distance) for i in range(size)])]
    unnamed x152 -> x158, local copies, waits for them, and re-layouts: 30.2 us -> 25.4 us
  transfers between devices with their start and end apart: 69 -> 69, of which waited for: 27 -> 29; matrix products, arithmetic and copies ran while one was open for 22% -> 22% of each run, Pallas kernels for 28% -> 26%
where the time goes in v6:
time: 610 us; the launch traced here: 605 us
  waiting for transfers between devices  188 us (31%)
  Pallas kernels  169 us (28%)
  starting transfers between devices  78.3 us (13%)
  local copies, waits for them, and re-layouts  71 us (12%)
  other arithmetic  62.9 us (10%)
  matrix products  19.9 us (3%)
  between operations  15.6 us (3%)
    ppermute x56, waiting for transfers between devices, swap(): return lax.ppermute(value, axis, [(i, i ^ distance) for i in range(size)])  152 us
    pallas_call x2, Pallas kernels, feed_forward(): pl.pallas_call(functools.partial(ff_kernel, columns // 3, not previous),...  69.4 us
    ppermute x56, starting transfers between devices, swap(): return lax.ppermute(value, axis, [(i, i ^ distance) for i in range(size)])  60.3 us
    pallas_call x2, Pallas kernels, ff_grads(): pl.pallas_call(functools.partial(ff_grads_kernel, columns // 3), grid=(mo...  34.9 us
    pallas_call x1, Pallas kernels, attend_back(): pl.pallas_call(attend_back_kernel, grid=(rows // tile, heads), in_specs=[...  27.1 us
    ppermute x3, waiting for transfers between devices, body(): lax.ppermute(lax.dynamic_index_in_dim(terms, lax.rem(me + k, shards), kee...  26.9 us
    unnamed x158, local copies, waits for them, and re-layouts  25.4 us
    pallas_call x1, Pallas kernels, attend(): pl.pallas_call(attend_kernel, grid=(rows // tile, heads), in_specs=[query...  16.1 us
  transfers between devices with their start and end apart: 69, of which 29 were waited for; matrix products, arithmetic and copies ran while one was open for 22% of the time, Pallas kernels for 26%

profile of v6, /device:TPU:0, one launch (start us, length us, event | category | flops | bytes accessed | tf_op | source)
XLA Modules:
  0.0 604.8 jit_solution(3498808667897238973)
XLA Ops:
  43.6 3.4 collective-permute-done.2
  50.7 5.3 multiply_cosine_fusion
  61.6 4.5 constant_dynamic-update-slice_fusion.5.normed_ref
  75.4 5.5 fusion.61
  109.2 6.7 %collective-permute-done.9 = bf16[512,256]{1,0:T(8,128)(2,1)S(1)} collective-permute-done((bf16[512,256]{1,0:T(8,128)(2,1)}, bf16[512,256]{1,0:T(8,128)(2,1)S(1)}, u32[]{:S(2)}, u32[]{:S(2)}) %collective-permute-start.9) | collective-permute-done | bytes 262176 | tf_op jit(solution)/shard_map/ppermute | solution.py:62
  119.6 16.1 %shard_map.272 = (bf16[512,768]{1,0:T(8,128)(2,1)}, f32[8,512]{1,0:T(8,128)}) custom-call(bf16[4,512,256]{2,1,0:T(8,128)(2,1)} %copy-done.35, bf16[2048,256]{1,0:T(8,128)(2,1)} %pad_maximum_fusion.6.key_ref.value_ref, bf16[2048,256]{1,0:T(8,128)(2,1)} %pad_maximum_fusion.6.key_ref.value_ref, s32[1,512]{1,0:T(1,128)} %bitcast.199, ...), custom_call_target="tpu_custom_call" | custom-call | flops 6442450944 | bytes 2359296 | tf_op jit(solution)/shard_map/pallas_call | solution.py:449
  137.5 8.2 %collective-permute-done.17 = bf16[2,96,768]{2,1,0:T(8,128)(2,1)S(1)} collective-permute-done((bf16[2,96,768]{2,1,0:T(8,128)(2,1)S(1)}, bf16[2,96,768]{2,1,0:T(8,128)(2,1)S(1)}, u32[]{:S(2)}, u32[]{:S(2)}) %collective-permute-start.17) | collective-permute-done | bytes 294944 | tf_op jit(solution)/shard_map/ppermute | solution.py:62
  145.7 4.2 collective-permute-done.16
  159.8 5.6 collective-permute-done.26
  167.1 14.4 %collective-permute-done.20 = bf16[256,1536]{1,0:T(8,128)(2,1)S(1)} collective-permute-done((bf16[256,1536]{1,0:T(8,128)(2,1)S(1)}, bf16[256,1536]{1,0:T(8,128)(2,1)S(1)}, u32[]{:S(2)}, u32[]{:S(2)}) %collective-permute-start.20) | collective-permute-done | bytes 786464 | tf_op jit(solution)/shard_map/ppermute | solution.py:62
  185.8 6.7 %collective-permute-done.21 = bf16[128,1536]{1,0:T(8,128)(2,1)S(1)} collective-permute-done((bf16[128,1536]{1,0:T(8,128)(2,1)S(1)}, bf16[128,1536]{1,0:T(8,128)(2,1)S(1)}, u32[]{:S(2)}, u32[]{:S(2)}) %collective-permute-start.21) | collective-permute-done | bytes 393248 | tf_op jit(solution)/shard_map/ppermute | solution.py:62
  202.2 4.0 constant_dynamic-update-slice_fusion.29.gradient_ref
  206.2 4.0 constant_dynamic-update-slice_fusion.18.normed_ref
  213.8 41.2 %shard_map.273 = (bf16[2048,2304]{1,0:T(8,128)(2,1)}, bf16[1024,1536]{1,0:T(8,128)(2,1)}, bf16[1024,1536]{1,0:T(8,128)(2,1)}, bf16[1024,1536]{1,0:T(8,128)(2,1)}, bf16[1024,1536]{1,0:T(8,128)(2,1)}) custom-call(bf16[2048,1536]{1,0:T(8,128)(2,1)} %constant_dynamic-update-slice_fusion.18.normed_ref, ...), custom_call_target="tpu_custom_call" | custom-call | flops 28991029248 | bytes 41680896 | tf_op jit(solution)/shard_map/pallas_call | solution.py:342
  255.0 21.5 %shard_map.274 = bf16[1536,2304]{1,0:T(8,128)(2,1)} custom-call(bf16[2048,1536]{1,0:T(8,128)(2,1)} %constant_dynamic-update-slice_fusion.18.normed_ref, bf16[2048,1536]{1,0:T(8,128)(2,1)} %constant_dynamic-update-slice_fusion.29.gradient_ref, bf16[2048,2304]{1,0:T(8,128)(2,1)} %get-tuple-element.93.acts_ref), custom_call_target="tpu_custom_call" | custom-call | flops 14495514624 | bytes 29097984 | tf_op jit(solution)/shard_map/pallas_call | solution.py:375
  276.5 28.2 %shard_map.275 = (bf16[2048,1152]{1,0:T(8,128)(2,1)}, bf16[1024,1536]{1,0:T(8,128)(2,1)}, bf16[1024,1536]{1,0:T(8,128)(2,1)}, bf16[1024,1536]{1,0:T(8,128)(2,1)}, bf16[1024,1536]{1,0:T(8,128)(2,1)}) custom-call(bf16[2048,1536]{1,0:T(8,128)(2,1)} %constant_dynamic-update-slice_fusion.18.normed_ref, ...), custom_call_target="tpu_custom_call" | custom-call | flops 14495514624 | bytes 33423360 | tf_op jit(solution)/shard_map/pallas_call | solution.py:342
  304.7 13.4 %shard_map.276 = bf16[1536,1152]{1,0:T(8,128)(2,1)} custom-call(bf16[2048,1536]{1,0:T(8,128)(2,1)} %constant_dynamic-update-slice_fusion.18.normed_ref, bf16[2048,1536]{1,0:T(8,128)(2,1)} %constant_dynamic-update-slice_fusion.29.gradient_ref, bf16[2048,1152]{1,0:T(8,128)(2,1)} %get-tuple-element.104.acts_ref), custom_call_target="tpu_custom_call" | custom-call | flops 7247757312 | bytes 20840448 | tf_op jit(solution)/shard_map/pallas_call | solution.py:375
  324.4 8.5 %collective-permute-done.35 = bf16[128,1536]{1,0:T(8,128)(2,1)S(1)} collective-permute-done((bf16[128,1536]{1,0:T(8,128)(2,1)S(1)}, bf16[128,1536]{1,0:T(8,128)(2,1)S(1)}, u32[]{:S(2)}, u32[]{:S(2)}) %collective-permute-start.35) | collective-permute-done | bytes 393248 | tf_op jit(solution)/shard_map/ppermute | solution.py:62
  336.7 16.8 %collective-permute-done.36 = bf16[256,1536]{1,0:T(8,128)(2,1)S(1)} collective-permute-done((bf16[256,1536]{1,0:T(8,128)(2,1)S(1)}, bf16[256,1536]{1,0:T(8,128)(2,1)S(1)}, u32[]{:S(2)}, u32[]{:S(2)}) %collective-permute-start.36) | collective-permute-done | bytes 786464 | tf_op jit(solution)/shard_map/ppermute | solution.py:62
  372.7 27.1 %shard_map.277 = (bf16[3,512,256]{2,1,0:T(8,128)(2,1)}, f32[2048,256]{1,0:T(8,128)}) custom-call(bf16[4,512,256]{2,1,0:T(8,128)(2,1)} %copy-done.35, bf16[512,768]{1,0:T(8,128)(2,1)} %convolution_convert_fusion.1.grad_ref, f32[512,128]{1,0:T(8,128)} %get-tuple-element.275.cosine_ref, f32[512,128]{1,0:T(8,128)} %get-tuple-element.276.sine_ref, ...), custom_call_target="tpu_custom_call" | custom-call | flops 16106127360 | bytes 2359296 | tf_op jit(solution)/shard_map/pallas_call | solution.py:521
  399.8 4.4 convolution_convert_fusion
  407.2 3.3 fusion.16
  442.9 12.1 %collective-permute-done.50 = bf16[4,96,768]{2,1,0:T(8,128)(2,1)} collective-permute-done((bf16[4,96,768]{2,1,0:T(8,128)(2,1)}, bf16[4,96,768]{2,1,0:T(8,128)(2,1)}, u32[]{:S(2)}, u32[]{:S(2)}) %collective-permute-start.50) | collective-permute-done | bytes 589856 | tf_op jit(solution)/shard_map/ppermute | solution.py:62
  458.6 8.9 %reduce-scatter.5.cloned.1.call-done = bf16[1,384,1152]{2,1,0:T(8,128)(2,1)} async-done(((bf16[4,384,1152]{2,1,0:T(8,128)(2,1)}), bf16[1,384,1152]{2,1,0:T(8,128)(2,1)}) %reduce-scatter.5.cloned.1.call-update) | async-done | bytes 884752 | tf_op jit(solution)/shard_map/reduce_scatter | solution.py:742
  471.6 6.3 %shard_map.279 = bf16[4,704,256]{2,1,0:T(8,128)(2,1)} custom-call(s32[1]{0:T(128)} %bitcast.60.core_ref, bf16[2048,1536]{1,0:T(8,128)(2,1)} %constant_dynamic-update-slice_fusion.5.normed_ref, bf16[512,256]{1,0:T(8,128)(2,1)} %copy-done.27, bf16[512,256]{1,0:T(8,128)(2,1)} %collective-permute-done.45.refs_1_, ...), custom_call_target="tpu_custom_call" | custom-call | flops 1610612736 | bytes 8781824 | tf_op jit(solution)/shard_map/pallas_call | solution.py:282
  487.9 4.5 collective-permute-done.59
  492.4 6.9 %collective-permute-done.61 = bf16[704,256]{1,0:T(8,128)(2,1)S(1)} collective-permute-done((bf16[704,256]{1,0:T(8,128)(2,1)S(1)}, bf16[704,256]{1,0:T(8,128)(2,1)S(1)}, u32[]{:S(2)}, u32[]{:S(2)}) %collective-permute-start.61) | collective-permute-done | bytes 360480 | tf_op jit(solution)/shard_map/ppermute | solution.py:823
  499.3 15.4 %collective-permute-done.60 = bf16[704,256]{1,0:T(8,128)(2,1)S(1)} collective-permute-done((bf16[704,256]{1,0:T(8,128)(2,1)S(1)}, bf16[704,256]{1,0:T(8,128)(2,1)S(1)}, u32[]{:S(2)}, u32[]{:S(2)}) %collective-permute-start.60) | collective-permute-done | bytes 360480 | tf_op jit(solution)/shard_map/ppermute | solution.py:823
  522.2 27.0 %collective-permute-done.64.refs_3_ = bf16[704,256]{1,0:T(8,128)(2,1)S(1)} collective-permute-done((bf16[704,256]{1,0:T(8,128)(2,1)S(1)}, bf16[704,256]{1,0:T(8,128)(2,1)S(1)}, u32[]{:S(2)}, u32[]{:S(2)}) %collective-permute-start.64) | collective-permute-done | bytes 360480 | tf_op jit(solution)/shard_map/ppermute | solution.py:62
  550.6 5.0 collective-permute-done.63.refs_2_
  571.4 9.6 %shard_map.278 = (f32[384,4480]{1,0:T(8,128)}, f32[384,4480]{1,0:T(8,128)}, f32[384,4480]{1,0:T(8,128)}) custom-call(s32[1]{0:T(128)} %bitcast.59.context_ref, bf16[384,3456]{1,0:T(8,128)(2,1)S(1)} %constant_dynamic-update-slice_fusion.35.refs_0_, bf16[384,3456]{1,0:T(8,128)(2,1)} %collective-permute-done.51.refs_1_, ...), custom_call_target="tpu_custom_call" | custom-call | tf_op jit(solution)/shard_map/pallas_call | solution.py:128
  581.1 10.0 %collective-permute-done.54.high_ref = bf16[192,3456]{1,0:T(8,128)(2,1)S(1)} collective-permute-done((bf16[192,3456]{1,0:T(8,128)(2,1)S(1)}, bf16[192,3456]{1,0:T(8,128)(2,1)S(1)}, u32[]{:S(2)}, u32[]{:S(2)}) %collective-permute-start.54) | collective-permute-done | bytes 1327136 | tf_op jit(solution)/shard_map/ppermute | solution.py:62
  (431 shorter events, 230.5 us)
Async XLA Ops:
  7.2 206.6 %all-gather.3.cloned.1.call-start = ((), (), s32[]{:S(2)}) async-start(), calls=%async_computation.2 | async-start | bytes 8847360 | tf_op jit(solution)/shard_map/all_gather | solution.py:716
  20.5 38.9 %collective-permute-start.6 = (bf16[384,512]{1,0:T(8,128)(2,1)}, bf16[384,512]{1,0:T(8,128)(2,1)}, u32[]{:S(2)}, u32[]{:S(2)}) collective-permute-start(bf16[384,512]{1,0:T(8,128)(2,1)} %pad_maximum_fusion.12), channel_id=1, source_target_pairs={{0,16},{8,24},{16,0},{24,8},{1,17},{9,25},{17,1},{25,9},{2,18},{10... | collective-permute-start | bytes 1179656 | tf_op jit(solution)/shard_map/ppermute | solution.py:549
  23.1 35.2 %collective-permute-start.5 = (bf16[384,512]{1,0:T(8,128)(2,1)}, bf16[384,512]{1,0:T(8,128)(2,1)}, u32[]{:S(2)}, u32[]{:S(2)}) collective-permute-start(bf16[384,512]{1,0:T(8,128)(2,1)} %pad_maximum_fusion.12), channel_id=1, source_target_pairs={{0,8},{8,16},{16,24},{24,0},{1,9},{9,17},{17,25},{25,1},{2,10},{10... | collective-permute-start | bytes 1179656 | tf_op jit(solution)/shard_map/ppermute | solution.py:549
  24.7 35.8 %collective-permute-start.7 = (bf16[384,512]{1,0:T(8,128)(2,1)}, bf16[384,512]{1,0:T(8,128)(2,1)}, u32[]{:S(2)}, u32[]{:S(2)}) collective-permute-start(bf16[384,512]{1,0:T(8,128)(2,1)} %pad_maximum_fusion.12), channel_id=1, source_target_pairs={{0,24},{8,0},{16,8},{24,16},{1,25},{9,1},{17,9},{25,17},{2,26},{10... | collective-permute-start | bytes 1179656 | tf_op jit(solution)/shard_map/ppermute | solution.py:549
  50.3 226.1 %all-gather.5.cloned.1.call-start = ((), (), s32[]{:S(2)}) async-start(), calls=%async_computation.3 | async-start | bytes 4423680 | tf_op jit(solution)/shard_map/all_gather | solution.py:716
  67.8 37.1 %collective-permute-start.12 = (bf16[96,768]{1,0:T(8,128)(2,1)}, bf16[96,768]{1,0:T(8,128)(2,1)}, u32[]{:S(2)}, u32[]{:S(2)}) collective-permute-start(bf16[96,768]{1,0:T(8,128)(2,1)} %get-tuple-element.169), channel_id=1, source_target_pairs={{0,16},{8,24},{16,0},{24,8},{1,17},{9,25},{17,1},{25,9},{2,18},{10... | collective-permute-start | bytes 442376 | tf_op jit(solution)/shard_map/ppermute | solution.py:549
  70.5 31.9 %collective-permute-start.11 = (bf16[96,768]{1,0:T(8,128)(2,1)}, bf16[96,768]{1,0:T(8,128)(2,1)}, u32[]{:S(2)}, u32[]{:S(2)}) collective-permute-start(bf16[96,768]{1,0:T(8,128)(2,1)} %get-tuple-element.169), channel_id=1, source_target_pairs={{0,8},{8,16},{16,24},{24,0},{1,9},{9,17},{17,25},{25,1},{2,10},{10... | collective-permute-start | bytes 442376 | tf_op jit(solution)/shard_map/ppermute | solution.py:549
  72.1 33.8 %collective-permute-start.13 = (bf16[96,768]{1,0:T(8,128)(2,1)}, bf16[96,768]{1,0:T(8,128)(2,1)}, u32[]{:S(2)}, u32[]{:S(2)}) collective-permute-start(bf16[96,768]{1,0:T(8,128)(2,1)} %get-tuple-element.169), channel_id=1, source_target_pairs={{0,24},{8,0},{16,8},{24,16},{1,25},{9,1},{17,9},{25,17},{2,26},{10... | collective-permute-start | bytes 442376 | tf_op jit(solution)/shard_map/ppermute | solution.py:549
  106.8 28.9 %collective-permute-start.15 = (bf16[4,96,768]{2,1,0:T(8,128)(2,1)S(1)}, bf16[4,96,768]{2,1,0:T(8,128)(2,1)S(1)}, u32[]{:S(2)}, u32[]{:S(2)}) collective-permute-start(bf16[4,96,768]{2,1,0:T(8,128)(2,1)S(1)} %bitcast_dynamic-update-slice_fusion.10), channel_id=1, source_target_pairs={{0,4},{2,6},{4,0},{6,2},{1,5},{3,7},{5,1},{7,3},{8,12},{10,14},{12... | collective-permute-start | bytes 1769480 | tf_op jit(solution)/shard_map/ppermute | solution.py:62
  117.1 34.7 %collective-permute-start.25 = (bf16[256,1536]{1,0:T(8,128)(2,1)S(1)}, bf16[256,1536]{1,0:T(8,128)(2,1)S(1)}, u32[]{:S(2)}, u32[]{:S(2)}) collective-permute-start(bf16[256,1536]{1,0:T(8,128)(2,1)S(1)} %get-tuple-element.163), channel_id=1, source_target_pairs={{0,4},{2,6},{4,0},{6,2},{1,5},{3,7},{5,1},{7,3},{8,12},{10,14},{12... | collective-permute-start | bytes 2359304 | tf_op jit(solution)/shard_map/ppermute | solution.py:62
  118.3 35.0 %collective-permute-start.24 = (bf16[256,1536]{1,0:T(8,128)(2,1)S(1)}, bf16[256,1536]{1,0:T(8,128)(2,1)S(1)}, u32[]{:S(2)}, u32[]{:S(2)}) collective-permute-start(bf16[256,1536]{1,0:T(8,128)(2,1)S(1)} %get-tuple-element.163), channel_id=1, source_target_pairs={{0,2},{2,0},{4,6},{6,4},{1,3},{3,1},{5,7},{7,5},{8,10},{10,8},{12,... | collective-permute-start | bytes 2359304 | tf_op jit(solution)/shard_map/ppermute | solution.py:62
  167.0 35.1 %collective-permute-start.28 = (bf16[1024,1536]{1,0:T(8,128)(2,1)}, bf16[1024,1536]{1,0:T(8,128)(2,1)}, u32[]{:S(2)}, u32[]{:S(2)}) collective-permute-start(bf16[1024,1536]{1,0:T(8,128)(2,1)} %get-tuple-element.239), channel_id=1, source_target_pairs={{0,1},{1,0},{2,3},{3,2},{4,5},{5,4},{6,7},{7,6},{8,9},{9,8},{10,11... | collective-permute-start | bytes 9437192 | tf_op jit(solution)/shard_map/ppermute | solution.py:62
  200.9 209.5 %reduce-scatter.3.cloned.1.call-start = ((), (), s32[]{:S(2)}) async-start(), calls=%async_computation.4 | async-start | bytes 8847360 | tf_op jit(solution)/shard_map/reduce_scatter | solution.py:742
  210.3 44.7 %collective-permute-start.31 = (bf16[1536,256]{1,0:T(8,128)(2,1)S(1)}, bf16[1536,256]{1,0:T(8,128)(2,1)}, u32[]{:S(2)}, u32[]{:S(2)}) collective-permute-start(bf16[1536,256]{1,0:T(8,128)(2,1)S(1)} %slice.377), channel_id=1, source_target_pairs={{0,6},{2,4},{4,2},{6,0},{1,7},{3,5},{5,3},{7,1},{8,14},{10,12},{12... | collective-permute-start | bytes 2359304 | tf_op jit(solution)/shard_map/ppermute | solution.py:62
  212.7 42.3 %collective-permute-start.30 = (bf16[1536,256]{1,0:T(8,128)(2,1)S(1)}, bf16[1536,256]{1,0:T(8,128)(2,1)}, u32[]{:S(2)}, u32[]{:S(2)}) collective-permute-start(bf16[1536,256]{1,0:T(8,128)(2,1)S(1)} %slice.377), channel_id=1, source_target_pairs={{0,4},{2,6},{4,0},{6,2},{1,5},{3,7},{5,1},{7,3},{8,12},{10,14},{12... | collective-permute-start | bytes 2359304 | tf_op jit(solution)/shard_map/ppermute | solution.py:62
  213.3 41.7 %collective-permute-start.29 = (bf16[1536,256]{1,0:T(8,128)(2,1)S(1)}, bf16[1536,256]{1,0:T(8,128)(2,1)}, u32[]{:S(2)}, u32[]{:S(2)}) collective-permute-start(bf16[1536,256]{1,0:T(8,128)(2,1)S(1)} %slice.377), channel_id=1, source_target_pairs={{0,2},{2,0},{4,6},{6,4},{1,3},{3,1},{5,7},{7,5},{8,10},{10,8},{12,... | collective-permute-start | bytes 2359304 | tf_op jit(solution)/shard_map/ppermute | solution.py:62
  276.5 191.0 %reduce-scatter.5.cloned.1.call-start = ((), (), s32[]{:S(2)}) async-start(), calls=%async_computation.5 | async-start | bytes 4423680 | tf_op jit(solution)/shard_map/reduce_scatter | solution.py:742
  369.2 35.1 %collective-permute-start.39 = (bf16[256,1536]{1,0:T(8,128)(2,1)}, bf16[256,1536]{1,0:T(8,128)(2,1)}, u32[]{:S(2)}, u32[]{:S(2)}) collective-permute-start(bf16[256,1536]{1,0:T(8,128)(2,1)} %get-tuple-element.180), channel_id=1, source_target_pairs={{0,2},{2,0},{4,6},{6,4},{1,3},{3,1},{5,7},{7,5},{8,10},{10,8},{12,... | collective-permute-start | bytes 2359304 | tf_op jit(solution)/shard_map/ppermute | solution.py:62
  369.8 36.2 %collective-permute-start.41 = (bf16[256,1536]{1,0:T(8,128)(2,1)}, bf16[256,1536]{1,0:T(8,128)(2,1)}, u32[]{:S(2)}, u32[]{:S(2)}) collective-permute-start(bf16[256,1536]{1,0:T(8,128)(2,1)} %get-tuple-element.181), channel_id=1, source_target_pairs={{0,6},{2,4},{4,2},{6,0},{1,7},{3,5},{5,3},{7,1},{8,14},{10,12},{12... | collective-permute-start | bytes 2359304 | tf_op jit(solution)/shard_map/ppermute | solution.py:62
  371.2 36.0 %collective-permute-start.40 = (bf16[256,1536]{1,0:T(8,128)(2,1)S(1)}, bf16[256,1536]{1,0:T(8,128)(2,1)}, u32[]{:S(2)}, u32[]{:S(2)}) collective-permute-start(bf16[256,1536]{1,0:T(8,128)(2,1)S(1)} %get-tuple-element.182), channel_id=1, source_target_pairs={{0,4},{2,6},{4,0},{6,2},{1,5},{3,7},{5,1},{7,3},{8,12},{10,14},{12... | collective-permute-start | bytes 2359304 | tf_op jit(solution)/shard_map/ppermute | solution.py:62
  418.0 37.0 %collective-permute-start.50 = (bf16[4,96,768]{2,1,0:T(8,128)(2,1)}, bf16[4,96,768]{2,1,0:T(8,128)(2,1)}, u32[]{:S(2)}, u32[]{:S(2)}) collective-permute-start(bf16[4,96,768]{2,1,0:T(8,128)(2,1)} %get-tuple-element.188), channel_id=1, source_target_pairs={{0,6},{2,4},{4,2},{6,0},{1,7},{3,5},{5,3},{7,1},{8,14},{10,12},{12... | collective-permute-start | bytes 1769480 | tf_op jit(solution)/shard_map/ppermute | solution.py:62
  423.8 32.1 %collective-permute-start.49 = (bf16[4,96,768]{2,1,0:T(8,128)(2,1)}, bf16[4,96,768]{2,1,0:T(8,128)(2,1)}, u32[]{:S(2)}, u32[]{:S(2)}) collective-permute-start(bf16[4,96,768]{2,1,0:T(8,128)(2,1)} %get-tuple-element.189), channel_id=1, source_target_pairs={{0,4},{2,6},{4,0},{6,2},{1,5},{3,7},{5,1},{7,3},{8,12},{10,14},{12... | collective-permute-start | bytes 1769480 | tf_op jit(solution)/shard_map/ppermute | solution.py:62
  437.5 30.0 %collective-permute-start.56 = (bf16[256,1536]{1,0:T(8,128)(2,1)}, bf16[256,1536]{1,0:T(8,128)(2,1)}, u32[]{:S(2)}, u32[]{:S(2)}) collective-permute-start(bf16[256,1536]{1,0:T(8,128)(2,1)} %dynamic-slice_convert_fusion), channel_id=1, source_target_pairs={{0,1},{1,0},{2,3},{3,2},{4,5},{5,4},{6,7},{7,6},{8,9},{9,8},{10,11... | collective-permute-start | bytes 2359304 | tf_op jit(solution)/shard_map/ppermute | solution.py:62
  437.5 29.9 %collective-permute-start.47 = (bf16[512,256]{1,0:T(8,128)(2,1)}, bf16[512,256]{1,0:T(8,128)(2,1)S(1)}, u32[]{:S(2)}, u32[]{:S(2)}) collective-permute-start(bf16[512,256]{1,0:T(8,128)(2,1)} %copy-done.34), channel_id=1, source_target_pairs={{0,6},{2,4},{4,2},{6,0},{1,7},{3,5},{5,3},{7,1},{8,14},{10,12},{12... | collective-permute-start | bytes 786440 | tf_op jit(solution)/shard_map/ppermute | solution.py:62
  480.7 81.2 %collective-permute-start.53 = (bf16[384,3456]{1,0:T(8,128)(2,1)S(1)}, bf16[384,3456]{1,0:T(8,128)(2,1)S(1)}, u32[]{:S(2)}, u32[]{:S(2)}) collective-permute-start(bf16[384,3456]{1,0:T(8,128)(2,1)S(1)} %constant_dynamic-update-slice_fusion.35.refs_0_), channel_id=1, source_target_pairs={{0,4},{2,6},{4,0},{6,2},{1,5},{3,7},{5,1},{7,3},{8,12},{10,14},{12... | collective-permute-start | bytes 7962632 | tf_op jit(solution)/shard_map/ppermute | solution.py:62
  482.2 81.3 %collective-permute-start.51 = (bf16[384,3456]{1,0:T(8,128)(2,1)S(1)}, bf16[384,3456]{1,0:T(8,128)(2,1)}, u32[]{:S(2)}, u32[]{:S(2)}) collective-permute-start(bf16[384,3456]{1,0:T(8,128)(2,1)S(1)} %constant_dynamic-update-slice_fusion.35.refs_0_), channel_id=1, source_target_pairs={{0,2},{2,0},{4,6},{6,4},{1,3},{3,1},{5,7},{7,5},{8,10},{10,8},{12,... | collective-permute-start | bytes 7962632 | tf_op jit(solution)/shard_map/ppermute | solution.py:62
  486.3 28.5 %collective-permute-start.60 = (bf16[704,256]{1,0:T(8,128)(2,1)S(1)}, bf16[704,256]{1,0:T(8,128)(2,1)S(1)}, u32[]{:S(2)}, u32[]{:S(2)}) collective-permute-start(bf16[704,256]{1,0:T(8,128)(2,1)S(1)} %get-tuple-element.210), channel_id=1, source_target_pairs={{0,16},{8,24},{16,0},{24,8},{1,17},{9,25},{17,1},{25,9},{2,18},{10... | collective-permute-start | bytes 1081352 | tf_op jit(solution)/shard_map/ppermute | solution.py:823
  516.0 33.1 %collective-permute-start.64 = (bf16[704,256]{1,0:T(8,128)(2,1)S(1)}, bf16[704,256]{1,0:T(8,128)(2,1)S(1)}, u32[]{:S(2)}, u32[]{:S(2)}) collective-permute-start(bf16[704,256]{1,0:T(8,128)(2,1)S(1)} %pad_maximum_fusion.13.refs_0_), channel_id=1, source_target_pairs={{0,6},{2,4},{4,2},{6,0},{1,7},{3,5},{5,3},{7,1},{8,14},{10,12},{12... | collective-permute-start | bytes 1081352 | tf_op jit(solution)/shard_map/ppermute | solution.py:62
  518.5 37.1 %collective-permute-start.63 = (bf16[704,256]{1,0:T(8,128)(2,1)S(1)}, bf16[704,256]{1,0:T(8,128)(2,1)S(1)}, u32[]{:S(2)}, u32[]{:S(2)}) collective-permute-start(bf16[704,256]{1,0:T(8,128)(2,1)S(1)} %pad_maximum_fusion.13.refs_0_), channel_id=1, source_target_pairs={{0,4},{2,6},{4,0},{6,2},{1,5},{3,7},{5,1},{7,3},{8,12},{10,14},{12... | collective-permute-start | bytes 1081352 | tf_op jit(solution)/shard_map/ppermute | solution.py:62
  522.1 44.4 %collective-permute-start.57 = (bf16[256,1536]{1,0:T(8,128)(2,1)S(1)}, bf16[256,1536]{1,0:T(8,128)(2,1)}, u32[]{:S(2)}, u32[]{:S(2)}) collective-permute-start(bf16[256,1536]{1,0:T(8,128)(2,1)S(1)} %get-tuple-element.202), channel_id=1, source_target_pairs={{0,1},{1,0},{2,3},{3,2},{4,5},{5,4},{6,7},{7,6},{8,9},{9,8},{10,11... | collective-permute-start | bytes 2359304 | tf_op jit(solution)/shard_map/ppermute | solution.py:62
  562.0 29.1 %collective-permute-start.54 = (bf16[192,3456]{1,0:T(8,128)(2,1)S(1)}, bf16[192,3456]{1,0:T(8,128)(2,1)S(1)}, u32[]{:S(2)}, u32[]{:S(2)}) collective-permute-start(bf16[192,3456]{1,0:T(8,128)(2,1)S(1)} %slice.396), channel_id=1, source_target_pairs={{0,2},{2,0},{4,6},{6,4},{1,3},{3,1},{5,7},{7,5},{8,10},{10,8},{12,... | collective-permute-start | bytes 3981320 | tf_op jit(solution)/shard_map/ppermute | solution.py:62
  564.9 28.8 %collective-permute-start.52 = (bf16[192,3456]{1,0:T(8,128)(2,1)S(1)}, bf16[192,3456]{1,0:T(8,128)(2,1)S(1)}, u32[]{:S(2)}, u32[]{:S(2)}) collective-permute-start(bf16[192,3456]{1,0:T(8,128)(2,1)S(1)} %slice.395), channel_id=1, source_target_pairs={{0,4},{2,6},{4,0},{6,2},{1,5},{3,7},{5,1},{7,3},{8,12},{10,14},{12... | collective-permute-start | bytes 3981320 | tf_op jit(solution)/shard_map/ppermute | solution.py:62
  (101 other events, 1548.4 us)
Sparse Core Ops, SparseCore 0:
  50.5 141.1 all-gather.2
  201.0 68.3 all-gather.4
  276.6 121.6 reduce-scatter.2
  400.5 66.8 reduce-scatter.4
